TPU v7x, 32 devices: a whole 2x2x4 slice. The times are simulated.
32 devices in a mesh: seq: 8 (over z, x), head: 4 (over y, core).
Axes of the slice: x: 2, y: 2, z: 4, core: 2. Of those that a mesh axis runs over, the one named last changes fastest.
Arguments:
- hidden: bfloat16 [128, 8192], P(None, 'seq'), may hold values from -6 to 6
- query_weight: bfloat16 [8192, 8192], P('seq', 'head'), may hold values from -0.0625 to 0.0625
- key_weight: bfloat16 [8192, 1024], P('seq', 'head'), may hold values from -0.0625 to 0.0625
- value_weight: bfloat16 [8192, 1024], P('seq', 'head'), may hold values from -0.0625 to 0.0625
- output_weight: bfloat16 [8192, 8192], P('head', 'seq'), may hold values from -0.0625 to 0.0625
- cache_keys: bfloat16 [65536, 1024], P('seq', 'head')
- cache_values: bfloat16 [65536, 1024], P('seq', 'head'), may hold values from -6 to 6
- cache_lens: int32 [8], P('seq'), may hold values from 1 to 8192, 40960 in all
Outputs:
- mixed: bfloat16 [128, 8192], P('head', 'seq')
Inputs may be any that keep to these rules, and one draw needn't show every extreme that they name: `cache_lens`: the lengths sum to 5/8 of all 65536 slots; the largest is exactly 8192.
All inputs are finite; a program needn't handle non-finite values. No bound on the sum of `cache_lens` on one device may be relied on, other than what follows from the above.
Results may differ from a plain program's by a relative error of at most 0.006.
The roundings to bfloat16 on the way count: a program that leaves them out, or rounds other values in their place, can miss the bound.
Values may be sent and summed in bfloat16 or wider, within the bound.
No kernel may reach another device: no remote copies, remote signals or barrier semaphores. Data moves between devices by JAX's collectives and lax.ppermute only.
A program may use at most 128 MiB of HBM per device.

v0:
```python
import math

import jax
import jax.numpy as jnp
from jax import lax
from jax.sharding import PartitionSpec as P

QH = 64
KVH = 8
HD = 128


NEG_BIG = -1e30


def merged(part, axis, combine):
    gathered = jax.tree.map(lambda a: lax.all_gather(a, axis), part)

    def take(source):
        return jax.tree.map(lambda a: lax.dynamic_index_in_dim(a, source, 0, False), gathered)

    return lax.fori_loop(
        1, lax.axis_size(axis), lambda source, state: combine(state, take(source)), take(0)
    )


def attend(q_block, keys3, values3, visible):
    scores = jnp.einsum("tkgd,ckd->tkgc", q_block, keys3, preferred_element_type=jnp.float32)
    scores = scores * (1.0 / math.sqrt(q_block.shape[-1]))
    mask = visible[:, None, None, :]
    masked = jnp.where(mask, scores, NEG_BIG)
    peaks = jnp.max(masked, axis=-1)
    weights = jnp.where(mask, jnp.exp(masked - peaks[..., None]), 0.0).astype(jnp.bfloat16)
    totals = jnp.sum(weights.astype(jnp.float32), axis=-1)
    outputs = jnp.einsum("tkgc,ckd->tkgd", weights, values3, preferred_element_type=jnp.float32)
    return (peaks, totals, outputs)


def cache_partial(queries, keys3, values3, length):
    tokens = queries.shape[0]
    block_len = math.gcd(tokens, 64)
    slot_count = keys3.shape[0]
    slot_ids = jnp.arange(slot_count, dtype=jnp.int32)
    visible = jnp.broadcast_to((slot_ids < length)[None, :], (block_len, slot_count))

    def handle(q_block):
        return attend(q_block, keys3, values3, visible)

    q_blocks = queries.reshape((tokens // block_len, block_len) + queries.shape[1:])
    peaks, totals, outputs = lax.map(handle, q_blocks)
    return (
        peaks.reshape((tokens,) + peaks.shape[2:]),
        totals.reshape((tokens,) + totals.shape[2:]),
        outputs.reshape((tokens,) + outputs.shape[2:]),
    )


def finish(peaks, totals, outputs, new_peaks, new_totals, new_outputs):
    joint_peak = jnp.maximum(peaks, new_peaks)
    first_scale = jnp.exp(peaks - joint_peak)
    second_scale = jnp.exp(new_peaks - joint_peak)
    whole_total = totals * first_scale + new_totals * second_scale
    whole_out = outputs * first_scale[..., None] + new_outputs * second_scale[..., None]
    attended = whole_out / whole_total[..., None]
    return attended.reshape(attended.shape[0], -1).astype(jnp.bfloat16)


def combine_pair(first_part, second_part):
    joint_peak = jnp.maximum(first_part[0], second_part[0])
    first_scale = jnp.exp(first_part[0] - joint_peak)
    second_scale = jnp.exp(second_part[0] - joint_peak)
    return (
        joint_peak,
        first_part[1] * first_scale + second_part[1] * second_scale,
        first_part[2] * first_scale[..., None] + second_part[2] * second_scale[..., None],
    )


def shards(
    hidden,
    query_weight,
    key_weight,
    value_weight,
    output_weight,
    cache_keys,
    cache_values,
    cache_lens,
):
    tokens = hidden.shape[0]
    kv_local = cache_keys.shape[1] // HD
    group_size = QH // KVH
    query_part = jnp.dot(hidden, query_weight, preferred_element_type=jnp.float32)
    key_part = jnp.dot(hidden, key_weight, preferred_element_type=jnp.float32)
    value_part = jnp.dot(hidden, value_weight, preferred_element_type=jnp.float32)
    query_sum, key_sum, value_sum = lax.psum((query_part, key_part, value_part), "seq")
    query_flat = query_sum.astype(jnp.bfloat16)
    key_flat = key_sum.astype(jnp.bfloat16)
    value_flat = value_sum.astype(jnp.bfloat16)
    queries = query_flat.reshape(tokens, kv_local, group_size, HD)
    new_keys = key_flat.reshape(tokens, kv_local, HD)
    new_values = value_flat.reshape(tokens, kv_local, HD)
    keys3 = cache_keys.reshape(cache_keys.shape[0], kv_local, HD)
    values3 = cache_values.reshape(cache_values.shape[0], kv_local, HD)
    peaks, totals, outputs = cache_partial(queries, keys3, values3, cache_lens[0])
    token_ids = jnp.arange(tokens, dtype=jnp.int32)
    peak, cache_total, cache_out = merged((peaks, totals, outputs), "seq", combine_pair)
    visible_new = token_ids[None, :] <= token_ids[:, None]
    new_peak, new_total, new_out = attend(queries, new_keys, new_values, visible_new)
    attended = finish(peak, cache_total, cache_out, new_peak, new_total, new_out)
    mixed = lax.psum_scatter(
        jnp.dot(attended, output_weight, preferred_element_type=jnp.float32),
        "head",
        scatter_dimension=0,
        tiled=True,
    )
    return mixed.astype(jnp.bfloat16)


def solution(mesh):
    placed = (
        P(None, "seq"),
        P("seq", "head"),
        P("seq", "head"),
        P("seq", "head"),
        P("head", "seq"),
        P("seq", "head"),
        P("seq", "head"),
        P("seq"),
    )
    return jax.shard_map(
        shards, mesh=mesh, in_specs=placed, out_specs=P("head", "seq"), check_vma=False
    )
```

profile of v0, /device:TPU:0, one launch (start us, length us, event | category | flops | bytes accessed | tf_op | source)
XLA Modules:
  0.0 386.5 jit_solution(6891535292086407650)
XLA Ops:
  6.5 1.0 copy-done
  7.6 1.2 fusion.33
  8.8 3.0 fusion.31
  11.8 1.4 fusion.32
  13.1 75.3 %all-reduce.2 = (bf16[128,256]{1,0:T(8,128)(2,1)}, bf16[128,2048]{1,0:T(8,128)(2,1)S(1)}, bf16[128,256]{1,0:T(8,128)(2,1)}) all-reduce(f32[128,256]{1,0:T(8,128)S(1)} %fusion.33, f32[128,2048]{1,0:T(8,128)S(1)} %fusion.31, f32[128,256]{1,0:T(8,128)S(1)} %fusion.32), channel_id=1, replica_groups=mesh['seq'=8,'head'=4] {'seq'}, use_global_device_ids=true, to_apply=%region_9.10 | all-reduce | flops 327680 | bytes 1966080 | tf_op jit(solution)/shard_map/psum | solution.py:95
  88.6 6.4 %copy.36 = bf16[8192,256]{0,1:T(8,128)(2,1)} copy(bf16[8192,256]{1,0:T(8,128)(2,1)} %param.17) | data formatting | bytes 8388608 | tf_op args[5]
  95.0 6.4 %copy.39 = bf16[8192,2,128]{2,0,1:T(8,128)(2,1)} copy(bf16[8192,2,128]{0,2,1:T(8,128)(2,1)} %bitcast.127) | data formatting | bytes 8388608
  101.4 6.4 %copy.37 = bf16[8192,256]{0,1:T(8,128)(2,1)} copy(bf16[8192,256]{1,0:T(8,128)(2,1)} %param.18) | data formatting | bytes 8388608 | tf_op args[6]
  107.8 6.3 %copy.40 = bf16[8192,2,128]{2,0,1:T(8,128)(2,1)} copy(bf16[8192,2,128]{0,2,1:T(8,128)(2,1)} %bitcast.128) | data formatting | bytes 8388608
  114.8 93.2 %while.35 = (s32[]{:T(128)}, f32[2,64,2,8]{1,0,3,2:T(2,128)S(1)}, f32[2,64,2,8]{1,0,3,2:T(2,128)S(1)}, f32[2,64,2,8,128]{4,3,2,1,0:T(8,128)S(1)}, bf16[2,64,2,8,...) while((s32[]{:T(128)}, f32[2,64,2,8]{1,0,3,2:T(2,128)S(1)}, ...), condition=%wide.region_4.5_spmd.clone, body=%wide.region_1.4_spmd.clone.sunk | while | flops 4420794368 | bytes 110960760 | solution.py:50
  114.8 15.6 %bitcast_reduce_fusion.2 = (f32[64,2,8]{2,0,1:T(8,128)S(1)}, f32[2,64,8,8192]{3,2,1,0:T(8,128)}) fusion(pred[8192]{0:T(1024)(128)(4,1)S(1)} %get-tuple-element.451, bf16[8192,2,128]{2,0,1:T(8,128)(2,1)} %get-tuple-element.449, bf16[2,64,2,8,128]{4,3,2,1,0:T(8,128)(2,1)S(1)} %get-tuple-element.448, s32[]{:T(128)S(6)} %copy.102), kind=kOutput, calls=%fused_computation.10.clone.1 | convolution fusion | flops 2172648448 | bytes 38023172 | tf_op jit(solution)/shard_map/while/body/eval_jaxpr/tkgd,ckd->tkgc/dot_general | solution.py:28
  130.6 15.7 %convert_reduce_fusion.3 = f32[64,2,8]{2,0,1:T(8,128)S(1)} fusion(f32[64,2,8]{2,0,1:T(8,128)S(1)} %get-tuple-element.422, f32[2,64,8,8192]{3,2,1,0:T(8,128)} %get-tuple-element.423, pred[8192]{0:T(1024)(128)(4,1)S(1)} %get-tuple-element.451), kind=kLoop, calls=%fused_computation.14.clone.1 | loop fusion | flops 58719232 | bytes 33570816 | tf_op jit(solution)/shard_map/while/body/eval_jaxpr/reduce_sum | solution.py:34
  146.4 14.9 %fusion.53 = f32[1,64,2,8,128]{4,3,1,2,0:T(8,128)S(1)} fusion(bf16[8192,2,128]{2,0,1:T(8,128)(2,1)} %get-tuple-element.450, f32[2,64,8,8192]{3,2,1,0:T(8,128)} %get-tuple-element.423, f32[64,2,8]{2,0,1:T(8,128)S(1)} %get-tuple-element.422, pred[8192]{0:T(1024)(128)(4,1)S(1)} %get-tuple-element.451), kind=kOutput, calls=%fused_computation.20.clone.1 | convolution fusion | flops 2189426688 | bytes 38285312 | tf_op jit(solution)/shard_map/while/body/eval_jaxpr/tkgc,ckd->tkgd/dot_general | solution.py:35
  161.4 15.6 %bitcast_reduce_fusion.2 = (f32[64,2,8]{2,0,1:T(8,128)S(1)}, f32[2,64,8,8192]{3,2,1,0:T(8,128)}) fusion(pred[8192]{0:T(1024)(128)(4,1)S(1)} %get-tuple-element.451, bf16[8192,2,128]{2,0,1:T(8,128)(2,1)} %get-tuple-element.449, bf16[2,64,2,8,128]{4,3,2,1,0:T(8,128)(2,1)S(1)} %get-tuple-element.448, s32[]{:T(128)S(6)} %copy.102), kind=kOutput, calls=%fused_computation.10.clone.1 | convolution fusion | flops 2172648448 | bytes 38023172 | tf_op jit(solution)/shard_map/while/body/eval_jaxpr/tkgd,ckd->tkgc/dot_general | solution.py:28
  177.2 15.7 %convert_reduce_fusion.3 = f32[64,2,8]{2,0,1:T(8,128)S(1)} fusion(f32[64,2,8]{2,0,1:T(8,128)S(1)} %get-tuple-element.422, f32[2,64,8,8192]{3,2,1,0:T(8,128)} %get-tuple-element.423, pred[8192]{0:T(1024)(128)(4,1)S(1)} %get-tuple-element.451), kind=kLoop, calls=%fused_computation.14.clone.1 | loop fusion | flops 58719232 | bytes 33570816 | tf_op jit(solution)/shard_map/while/body/eval_jaxpr/reduce_sum | solution.py:34
  193.0 14.9 %fusion.53 = f32[1,64,2,8,128]{4,3,1,2,0:T(8,128)S(1)} fusion(bf16[8192,2,128]{2,0,1:T(8,128)(2,1)} %get-tuple-element.450, f32[2,64,8,8192]{3,2,1,0:T(8,128)} %get-tuple-element.423, f32[64,2,8]{2,0,1:T(8,128)S(1)} %get-tuple-element.422, pred[8192]{0:T(1024)(128)(4,1)S(1)} %get-tuple-element.451), kind=kOutput, calls=%fused_computation.20.clone.1 | convolution fusion | flops 2189426688 | bytes 38285312 | tf_op jit(solution)/shard_map/while/body/eval_jaxpr/tkgc,ckd->tkgd/dot_general | solution.py:35
  208.1 1.1 copy-done.2
  209.5 30.9 %all_gather.9 = f32[8,128,2,8]{1,3,2,0:T(8,128)S(1)} all-gather(f32[1,128,2,8]{1,3,2,0:T(8,128)S(1)} %all_gather_reshape.9), channel_id=1, replica_groups=mesh['seq'=8,'head'=4] {'seq'}, dimensions={0}, use_global_device_ids=true | all-gather | bytes 73728 | tf_op jit(solution)/shard_map/all_gather | solution.py:17
  240.4 31.1 %all_gather.10 = f32[8,128,2,8]{1,3,2,0:T(8,128)S(1)} all-gather(f32[1,128,2,8]{1,3,2,0:T(8,128)S(1)} %all_gather_reshape.10), channel_id=1, replica_groups=mesh['seq'=8,'head'=4] {'seq'}, dimensions={0}, use_global_device_ids=true | all-gather | bytes 73728 | tf_op jit(solution)/shard_map/all_gather | solution.py:17
  271.5 0.3 fusion.30
  271.8 0.2 convert_reduce_fusion.1
  272.1 62.1 %all-gather.2.cloned.1.call-done = f32[8,128,2,8,128]{4,3,2,1,0:T(8,128)} async-done(((f32[1,128,2,8,128]{4,3,2,1,0:T(8,128)}), f32[8,128,2,8,128]{4,3,2,1,0:T(8,128)}) %all-gather.2.cloned.1.call-update) | async-done | bytes 8388624 | tf_op jit(solution)/shard_map/all_gather | solution.py:17
  334.1 1.4 slice_bitcast_fusion
  335.5 15.7 %while.34 = (s32[]{:T(128)}, f32[128,2,8]{0,2,1:T(8,128)S(1)}, f32[128,2,8]{0,2,1:T(8,128)S(1)}, f32[128,2,8,128]{3,2,1,0:T(8,128)S(1)}, f32[8,128,2,8]{1,3,2,0:...) while((s32[]{:T(128)}, f32[128,2,8]{0,2,1:T(8,128)S(1)}, ...), condition=%wide.region_6.7_spmd, body=%wide.region_5.6_spmd.sunk | while | flops 798725 | bytes 3260567 | solution.py:22
  335.5 0.1 copy.86
  335.7 0.1 copy.87
  335.8 1.9 fusion.50
  337.8 0.1 copy.86
  337.9 0.1 copy.87
  338.1 1.9 fusion.50
  340.0 0.1 copy.86
  340.2 0.1 copy.87
  340.3 1.9 fusion.50
  342.3 0.1 copy.86
  342.4 0.1 copy.87
  342.6 1.9 fusion.50
  344.5 0.1 copy.86
  344.7 0.1 copy.87
  344.8 1.9 fusion.50
  346.9 0.1 copy.87
  347.1 1.9 fusion.50
  349.1 0.1 copy.87
  349.3 1.9 fusion.50
  351.2 1.4 copy.46
  352.6 1.6 fusion.21
  354.2 3.7 fusion.34
  358.0 20.1 %reduce-scatter.2.cloned.1.call-done = f32[32,1024]{1,0:T(8,128)} async-done(((f32[128,1024]{1,0:T(8,128)}), f32[32,1024]{1,0:T(8,128)}) %reduce-scatter.2.cloned.1.call-update) | async-done | bytes 131088 | tf_op jit(solution)/shard_map/reduce_scatter | solution.py:110
  378.1 1.5 convert_element_type.37
  (44 shorter events, 1.5 us)
Async XLA Ops:
  6.5 1.0 copy-start
  6.5 327.6 %all-gather.2.cloned.1.call-start = ((), (), s32[]{:S(2)}) async-start(), calls=%async_computation.1 | async-start | bytes 9437184 | tf_op jit(solution)/shard_map/all_gather | solution.py:17
  114.8 94.4 %copy-start.4 = (bf16[128,256]{1,0:T(8,128)(2,1)S(1)}, bf16[128,256]{1,0:T(8,128)(2,1)}, u32[]{:S(2)}) copy-start(bf16[128,256]{1,0:T(8,128)(2,1)} %get-tuple-element.306) | copy-start | bytes 196612
  114.8 94.7 %copy-start.3 = (bf16[128,256]{1,0:T(8,128)(2,1)S(1)}, bf16[128,256]{1,0:T(8,128)(2,1)}, u32[]{:S(2)}) copy-start(bf16[128,256]{1,0:T(8,128)(2,1)} %get-tuple-element.308) | copy-start | bytes 196612
  208.0 1.1 copy-start.2
  209.1 168.9 %reduce-scatter.2.cloned.1.call-start = ((), (), s32[]{:S(2)}) async-start(), calls=%async_computation.2 | async-start | bytes 655360 | tf_op jit(solution)/shard_map/reduce_scatter | solution.py:110
  334.1 45.5 %copy-start.1 = (bf16[1024,256]{1,0:T(8,128)(2,1)S(1)}, bf16[1024,256]{1,0:T(8,128)(2,1)}, u32[]{:S(2)}) copy-start(bf16[1024,256]{1,0:T(8,128)(2,1)} %param.15) | copy-start | bytes 1572868
Sparse Core Ops, SparseCore 0:
  209.3 124.8 all-gather.1
  358.1 19.9 reduce-scatter.1
where the time goes:
time: 388 us; the launch traced here: 386 us
  blocking collectives  137 us (35%)
  waiting for transfers between devices  82.2 us (21%)
  matrix products  72.3 us (19%)
  other arithmetic  46.6 us (12%)
  local copies, waits for them, and re-layouts  33.4 us (9%)
  between operations  14.2 us (4%)
    psum x1, blocking collectives, shards(): lax.psum((query_part, key_part, value_part), 'seq')  75.3 us
    all_gather x1, waiting for transfers between devices, merged(): gathered = jax.tree.map(lambda a: lax.all_gather(a, axis), part)  62.1 us
    all_gather x2, blocking collectives, merged(): gathered = jax.tree.map(lambda a: lax.all_gather(a, axis), part)  62 us
    reduce_sum x3, other arithmetic, attend(): totals = jnp.sum(weights.astype(jnp.float32), axis=-1)  31.6 us
    dot_general x3, matrix products, attend(): jnp.einsum('tkgd,ckd->tkgc', q_block, keys3, preferred_element_type=jnp.f...  31.6 us
    dot_general x3, matrix products, attend(): jnp.einsum('tkgc,ckd->tkgd', weights, values3, preferred_element_type=jnp...  31.5 us
    unnamed x15, local copies, waits for them, and re-layouts  27.8 us
    reduce_scatter x1, waiting for transfers between devices, shards(): lax.psum_scatter(jnp.dot(attended, output_weight, preferred_element_type=...  20.1 us
  transfers between devices with their start and end apart: 2, of which 2 were waited for; matrix products, arithmetic and copies ran while one was open for 0% of the time, Pallas kernels for 0%

commit v1 on v0

v1 whole, which is shorter than its diff:
```python
import functools
import math

import jax
import jax.numpy as jnp
from jax import lax
from jax.experimental import pallas as pl
from jax.experimental.pallas import tpu as pltpu
from jax.sharding import PartitionSpec as P

QH = 64
KVH = 8
HD = 128

NEG_BIG = -1e30
LANES = 128
STAT_ROWS = 8
NT = (((1,), (1,)), ((), ()))

OUTPUT_SCALE = 2.0**12
MIXED_SCALE = 2.0**-3


def vmem_spec():
    return pl.BlockSpec(memory_space=pltpu.VMEM)


def smem_spec():
    return pl.BlockSpec(memory_space=pltpu.SMEM)


def to_owners(array, axis):
    return lax.all_to_all(array, axis, 0, 0)


def project_kernel(hidden_ref, *refs, blocks):
    out = refs[-1]
    tokens = hidden_ref.shape[0]
    hidden = hidden_ref[...]
    first = 0
    for weight_refs, block in zip((refs[:1], refs[1:-1]), blocks):
        per = tokens // block
        piece = 0
        for weight_ref in weight_refs:
            product = jnp.dot(hidden, weight_ref[...], preferred_element_type=jnp.float32)
            for c in range(product.shape[1] // LANES):
                for e in range(per):
                    out[piece, first : first + block, :] = product[
                        e * block : (e + 1) * block, c * LANES : (c + 1) * LANES
                    ]
                    piece += 1
        first += block


def project(hidden, weight, chunk, columns, others, count):
    tokens, depth = hidden.shape
    wide = [columns] + [other.shape[1] for other in others]
    blocks = [columns // LANES * tokens // count]
    if others:
        blocks.append(sum(wide[1:]) // LANES * tokens // count)
    total = sum(wide)
    return pl.pallas_call(
        functools.partial(project_kernel, blocks=blocks),
        grid=(1,),
        out_shape=jax.ShapeDtypeStruct((count, sum(blocks), LANES), jnp.float32),
        in_specs=[
            pl.BlockSpec((tokens, depth), lambda i: (0, 0)),
            pl.BlockSpec((depth, columns), lambda i: (0, chunk)),
        ]
        + [pl.BlockSpec(other.shape, lambda i: (0, 0)) for other in others],
        out_specs=pl.BlockSpec((count, sum(blocks), LANES), lambda i: (0, 0, 0)),
        compiler_params=pltpu.CompilerParams(vmem_limit_bytes=24 << 20),
        cost_estimate=pl.CostEstimate(
            flops=2 * tokens * depth * total,
            bytes_accessed=2 * depth * total,
            transcendentals=0,
        ),
    )(hidden, weight, *others)


def attention_kernel(len_ref, q_ref, k_ref, v_ref, o_ref, *scratch, band, step, block):
    s_bufs, m_bufs = scratch[:2], scratch[2:4]
    shift, acc, lse_all = scratch[4:]
    count = q_ref.shape[0]
    rows = count * block
    bands = rows // band
    share = band // block
    scale = math.log2(math.e) / math.sqrt(HD)
    piece = math.gcd(step, 1024)
    tiles = piece // LANES

    length = len_ref[0]
    full = length // step
    rest = length - full * step

    def score(r, i, first, masked):
        q = q_ref[r * share : (r + 1) * share, :block, :].reshape(band, HD)
        keys = k_ref[pl.ds(pl.multiple_of(i * step + first, piece), piece), :]
        s = lax.dot_general(q, keys, NT, preferred_element_type=jnp.float32)
        if masked:
            column = first + lax.broadcasted_iota(jnp.int32, (band, piece), 1)
            s = jnp.where(column < rest, s, NEG_BIG)
        s_bufs[r % 2][i, :, first : first + piece] = s
        tops = [s[:, c * LANES : (c + 1) * LANES] for c in range(tiles)]
        while len(tops) > 1:
            tops = [jnp.maximum(a, b) for a, b in zip(tops[0::2], tops[1::2])]
        m_bufs[r % 2][...] = jnp.maximum(m_bufs[r % 2][...], tops[0])

    def weigh(r, i, first):
        s = s_bufs[r % 2][i, :, first : first + piece]
        low = shift[...]
        weights = jnp.concatenate(
            [
                jnp.exp2(s[:, c * LANES : (c + 1) * LANES] * scale - low).astype(jnp.bfloat16)
                for c in range(tiles)
            ],
            axis=1,
        )
        values = v_ref[pl.ds(pl.multiple_of(i * step + first, piece), piece), :]
        wide = jnp.concatenate([values, jnp.ones((piece, LANES), jnp.bfloat16)], axis=1)
        acc[...] += jnp.dot(weights, wide, preferred_element_type=jnp.float32)

    for r in range(bands + 1):
        scores, weighs = r < bands, r > 0
        if scores:
            m_bufs[r % 2][...] = jnp.full((band, LANES), -3e38, jnp.float32)
        if weighs:
            top = jnp.max(m_bufs[(r - 1) % 2][...], axis=1, keepdims=True)
            shift[...] = jnp.broadcast_to(top * scale, (band, LANES))
            acc[...] = jnp.zeros(acc.shape, jnp.float32)

        def both(i, masked):
            for first in range(0, step, piece):
                if weighs:
                    weigh(r - 1, i, first)
                if scores:
                    score(r, i, first, masked)

        def body(i, carry):
            both(i, False)
            return carry

        lax.fori_loop(0, full, body, 0)

        @pl.when(rest > 0)
        def _():
            both(full, True)

        if weighs:
            totals = acc[:, LANES:]
            mean = acc[:, :LANES] / totals * OUTPUT_SCALE
            o_ref[(r - 1) * share : r * share, :block, :] = mean.reshape(share, block, HD)
            lse_all[(r - 1) * band : r * band, :] = shift[...] + jnp.log2(totals)

    per = LANES // block
    row = lax.broadcasted_iota(jnp.int32, (STAT_ROWS, LANES), 0)
    for g in range(rows // LANES):
        level = lse_all[g * LANES : (g + 1) * LANES, :].T[:STAT_ROWS, :]
        exponent = jnp.floor(jnp.log2(jnp.maximum(jnp.abs(level), 1e-30)))
        exponent = jnp.minimum(exponent, 120.0)
        rest_of = level * jnp.exp2(-exponent)
        first = jnp.floor(rest_of * 2.0**9 + 0.5)
        rest_of = rest_of - first * 2.0**-9
        second = jnp.floor(rest_of * 2.0**20 + 0.5)
        third = (rest_of - second * 2.0**-20) * 2.0**31
        stats = jnp.where(row == 0, exponent, jnp.where(row == 1, first, second))
        stats = jnp.where(row >= 3, third, stats)
        for e in range(per):
            o_ref[g * per + e, block:, :] = stats


def attention(queries, block, keys, values, length, head):
    count = queries.shape[0]
    rows, slots = count * block, keys.shape[0]
    band = math.gcd(rows, 256)
    step = math.gcd(slots, 2048)
    return pl.pallas_call(
        functools.partial(attention_kernel, band=band, step=step, block=block),
        grid=(1,),
        out_shape=jax.ShapeDtypeStruct((count, block + STAT_ROWS, HD), jnp.float32),
        in_specs=[smem_spec(), pl.BlockSpec(queries.shape, lambda i: (0, 0, 0))]
        + [pl.BlockSpec((slots, HD), lambda i: (0, head), pipeline_mode=pl.Buffered(1))] * 2,
        out_specs=pl.BlockSpec((count, block + STAT_ROWS, HD), lambda i: (0, 0, 0)),
        scratch_shapes=[
            pltpu.VMEM((slots // step, band, step), jnp.float32),
            pltpu.VMEM((slots // step, band, step), jnp.float32),
            pltpu.VMEM((band, LANES), jnp.float32),
            pltpu.VMEM((band, LANES), jnp.float32),
            pltpu.VMEM((band, LANES), jnp.float32),
            pltpu.VMEM((band, 2 * LANES), jnp.float32),
            pltpu.VMEM((rows, LANES), jnp.float32),
        ],
        compiler_params=pltpu.CompilerParams(vmem_limit_bytes=40 << 20),
        cost_estimate=pl.CostEstimate(
            flops=8 * rows * slots * HD,
            bytes_accessed=4 * slots * HD,
            transcendentals=rows * slots,
        ),
    )(length, queries, keys, values)


def merge_kernel(me_ref, part_ref, q_ref, kv_ref, o_ref, *, head, kv_local, tokens):
    count = part_ref.shape[0]
    block = q_ref.shape[0]
    per = LANES // block
    scale = math.log2(math.e) / math.sqrt(HD)

    keys = kv_ref[head * tokens : (head + 1) * tokens, :]
    second = (kv_local + head) * tokens
    values = kv_ref[second : second + tokens, :]

    s = lax.dot_general(q_ref[...], keys, NT, preferred_element_type=jnp.float32) * scale
    token = lax.rem(me_ref[0] * block, tokens) + lax.broadcasted_iota(jnp.int32, s.shape, 0)
    visible = lax.broadcasted_iota(jnp.int32, s.shape, 1) <= token
    s = jnp.where(visible, s, NEG_BIG)
    new_top = jnp.max(s, axis=1, keepdims=True)
    weights = jnp.where(visible, jnp.exp2(s - new_top), 0.0).astype(jnp.bfloat16)
    new_total = jnp.sum(weights.astype(jnp.float32), axis=1, keepdims=True)
    new_out = jnp.dot(weights, values, preferred_element_type=jnp.float32)

    place = lax.rem(me_ref[0], per)
    lane = lax.broadcasted_iota(jnp.int32, (block, LANES), 1)
    mine = lane == place * block + lax.broadcasted_iota(jnp.int32, (block, LANES), 0)
    levels = []
    for k in range(count):
        stats = part_ref[k, block:, :]
        level = stats[1:2, :] * 2.0**-9 + stats[2:3, :] * 2.0**-20 + stats[3:4, :] * 2.0**-31
        level = jnp.broadcast_to(level * jnp.exp2(stats[0:1, :]), (block, LANES))
        levels.append(jnp.sum(jnp.where(mine, level, 0.0), axis=1, keepdims=True))
    joint = new_top
    for level in levels:
        joint = jnp.maximum(joint, level)
    new_scale = jnp.exp2(new_top - joint)
    whole_out = new_out * new_scale
    whole_total = new_total * new_scale
    for k in range(count):
        factor = jnp.exp2(levels[k] - joint)
        whole_out = whole_out + part_ref[k, :block, :] * (factor * (1.0 / OUTPUT_SCALE))
        whole_total = whole_total + factor
    o_ref[...] = (whole_out / whole_total).astype(jnp.bfloat16)


def merge(me, parts, q_mine, kv, head, kv_local, tokens):
    return pl.pallas_call(
        functools.partial(merge_kernel, head=head, kv_local=kv_local, tokens=tokens),
        out_shape=jax.ShapeDtypeStruct(q_mine.shape, jnp.bfloat16),
        in_specs=[smem_spec()] + [vmem_spec()] * 3,
        out_specs=vmem_spec(),
    )(me, parts, q_mine, kv)


def output_kernel(w_ref, a_ref, *refs, tokens, groups, has_before, chunk):
    before = refs[0] if has_before else None
    o_ref, w_all, sems = refs[-3:]
    copies = []
    for g in range(groups):
        copies.append(
            pltpu.make_async_copy(
                w_ref.at[pl.ds((chunk * groups + g) * HD, HD), :],
                w_all.at[pl.ds(g * HD, HD), :],
                sems.at[g],
            )
        )
        copies[-1].start()
    rows = jnp.concatenate([a_ref[g * tokens : (g + 1) * tokens, :] for g in range(groups)], axis=1)
    for copy in copies:
        copy.wait()
    product = jnp.dot(rows, w_all[...], preferred_element_type=jnp.float32)
    if has_before:
        product = product + before[...]
    o_ref[...] = product


def output_part(weight, attended, tokens, before, chunk):
    groups = QH // KVH
    width = weight.shape[1]
    has_before = before is not None
    return pl.pallas_call(
        functools.partial(
            output_kernel, tokens=tokens, groups=groups, has_before=has_before, chunk=chunk
        ),
        out_shape=jax.ShapeDtypeStruct((tokens, width), jnp.float32),
        in_specs=[pl.BlockSpec(memory_space=pl.ANY)] + [vmem_spec()] * (1 + int(has_before)),
        out_specs=vmem_spec(),
        scratch_shapes=[
            pltpu.VMEM((groups * HD, width), jnp.bfloat16),
            pltpu.SemaphoreType.DMA((groups,)),
        ],
        compiler_params=pltpu.CompilerParams(vmem_limit_bytes=24 << 20),
        cost_estimate=pl.CostEstimate(
            flops=2 * tokens * groups * HD * width,
            bytes_accessed=2 * groups * HD * width,
            transcendentals=0,
        ),
    )(weight, attended, *([before] if has_before else []))


def shards(
    hidden,
    query_weight,
    key_weight,
    value_weight,
    output_weight,
    cache_keys,
    cache_values,
    cache_lens,
):
    tokens = hidden.shape[0]
    count = lax.axis_size("seq")
    heads = lax.axis_size("head")
    kv_local = cache_keys.shape[1] // HD
    columns = (QH // KVH) * HD
    block = (QH // KVH) * tokens // count
    me = lax.axis_index("seq").reshape(1)

    mine = []
    for j in range(kv_local):
        others = [key_weight, value_weight] if j == kv_local - 1 else []
        partial = project(hidden, query_weight, j, columns, others, count)
        mine.append(jnp.sum(to_owners(partial, "seq"), axis=0).astype(jnp.bfloat16))
    queries = [lax.all_gather(rows, "seq") for rows in mine]
    kv = queries[-1][:, block:, :].reshape(-1, HD)

    mixed = None
    for j in range(kv_local):
        parts = attention(queries[j], block, cache_keys, cache_values, cache_lens, j)
        parts = to_owners(parts.astype(jnp.float16), "seq").astype(jnp.float32)
        attended = merge(me, parts, mine[j][:block], kv, j, kv_local, tokens)
        attended = lax.all_gather(attended, "seq", tiled=True)
        mixed = output_part(output_weight, attended, tokens, mixed, j)

    mixed = (mixed * MIXED_SCALE).reshape(heads, tokens // heads, mixed.shape[1])
    mixed = jnp.sum(to_owners(mixed.astype(jnp.float16), "head").astype(jnp.float32), axis=0)
    return (mixed * (1.0 / MIXED_SCALE)).astype(jnp.bfloat16)


def solution(mesh):
    placed = (
        P(None, "seq"),
        P("seq", "head"),
        P("seq", "head"),
        P("seq", "head"),
        P("head", "seq"),
        P("seq", "head"),
        P("seq", "head"),
        P("seq"),
    )
    return jax.shard_map(
        shards, mesh=mesh, in_specs=placed, out_specs=P("head", "seq"), check_vma=False
    )
```

time: 388 us -> 233 us (0.60)
  matrix products: 72.3 us -> 0 us
  waiting for transfers between devices: 82.2 us -> 10.8 us
  other arithmetic: 46.6 us -> 3.99 us
  starting transfers between devices: 0.04 us -> 35.5 us
  Pallas kernels: 0 us -> 17.4 us
  local copies, waits for them, and re-layouts: 33.4 us -> 19.7 us
  between operations: 14.2 us -> 0.78 us
  blocking collectives: 137 us -> 146 us
    psum x1 -> x0, blocking collectives: 75.3 us -> none  [shards(): lax.psum((query_part, key_part, value_part), 'seq')]
    all_gather x2 -> x4, blocking collectives: 62 us -> 137 us  [the longest x2 74.5 us: shards(): queries = [lax.all_gather(rows, 'seq') for rows in mine]]
    dot_general x10 -> x0, matrix products: 72.3 us -> none  [the longest x3 31.6 us: attend(): jnp.einsum('tkgd,ckd->tkgc', q_block, keys3, preferred_element_type=jnp.f...]
    all_gather x1 -> x0, waiting for transfers between devices: 62.1 us -> none  [merged(): gathered = jax.tree.map(lambda a: lax.all_gather(a, axis), part)]
    all_to_all x0 -> x4, starting transfers between devices: none -> 35.5 us  [to_owners(): return lax.all_to_all(array, axis, 0, 0)]
    reduce_sum x3, other arithmetic: 31.6 us -> 0.11 us  [the longest x2 0.07 us: shards(): mine.append(jnp.sum(to_owners(partial, 'seq'), axis=0).astype(jnp.bfloat16))]
    reduce_scatter x1 -> x0, waiting for transfers between devices: 20.1 us -> none  [shards(): lax.psum_scatter(jnp.dot(attended, output_weight, preferred_element_type=...]
    pallas_call x0 -> x8, Pallas kernels: none -> 17.4 us  [the longest x2 9.02 us: attention(): pl.pallas_call(functools.partial(attention_kernel, band=band, step=step,...]
  transfers between devices with their start and end apart: 2 -> 4, of which waited for: 2 -> 1; matrix products, arithmetic and copies ran while one was open for 0% -> 2% of each run, Pallas kernels for 0% -> 6%
where the time goes in v1:
time: 233 us; the launch traced here: 234 us
  blocking collectives  146 us (63%)
  starting transfers between devices  35.5 us (15%)
  local copies, waits for them, and re-layouts  19.7 us (8%)
  Pallas kernels  17.4 us (7%)
  waiting for transfers between devices  10.8 us (5%)
  other arithmetic  3.99 us (2%)
    all_gather x2, blocking collectives, shards(): queries = [lax.all_gather(rows, 'seq') for rows in mine]  74.5 us
    all_gather x2, blocking collectives, shards(): attended = lax.all_gather(attended, 'seq', tiled=True)  62.4 us
    all_to_all x4, starting transfers between devices, to_owners(): return lax.all_to_all(array, axis, 0, 0)  35.5 us
    unnamed x26, local copies, waits for them, and re-layouts  18.5 us
    all_to_all x4, waiting for transfers between devices, to_owners(): return lax.all_to_all(array, axis, 0, 0)  10.8 us
    pallas_call x2, Pallas kernels, attention(): pl.pallas_call(functools.partial(attention_kernel, band=band, step=step,...  9.02 us
    all_to_all x1, blocking collectives, to_owners(): return lax.all_to_all(array, axis, 0, 0)  8.63 us
  transfers between devices with their start and end apart: 4, of which 1 were waited for; matrix products, arithmetic and copies ran while one was open for 2% of the time, Pallas kernels for 6%

profile of v1, /device:TPU:0, one launch (start us, length us, event | category | flops | bytes accessed | tf_op | source)
XLA Modules:
  0.0 233.9 jit_solution(12365407108933676988)
XLA Ops:
  0.0 0.0 copy-start
  0.0 2.2 copy-done
  2.2 0.0 copy-start.4
  2.2 0.9 copy-done.4
  3.1 0.0 copy-start.5
  3.1 0.0 copy-start.6
  3.1 0.0 copy-start.7
  3.1 1.3 shard_map.85
  4.4 7.3 %all-to-all-start.2 = ((f32[8,128,128]{2,1,0:T(8,128)}), f32[8,128,128]{2,1,0:T(8,128)S(1)}, u32[]{:S(2)}, u32[]{:S(2)}) async-start(f32[8,128,128]{2,1,0:T(8,128)} %shard_map.85), calls=%async_computation.2 | async-start | bytes 1048576 | tf_op jit(solution)/shard_map/all_to_all | solution.py:33
  11.7 0.0 copy-done.5
  11.7 0.0 copy-done.6
  11.7 0.0 copy-done.7
  11.7 0.0 copy-start.1
  11.7 2.2 copy-done.1
  13.9 1.5 shard_map.82
  15.3 10.8 %all-to-all-done.2 = f32[8,128,128]{2,1,0:T(8,128)S(1)} async-done(((f32[8,128,128]{2,1,0:T(8,128)}), f32[8,128,128]{2,1,0:T(8,128)S(1)}, u32[]{:S(2)}, u32[]{:S(2)}) %all-to-all-start.2) | async-done | bytes 524320 | tf_op jit(solution)/shard_map/all_to_all | solution.py:33
  26.1 3.6 %all-to-all-start = ((f32[8,192,128]{2,1,0:T(8,128)}), f32[8,192,128]{2,1,0:T(8,128)S(1)}, u32[]{:S(2)}, u32[]{:S(2)}) async-start(f32[8,192,128]{2,1,0:T(8,128)} %shard_map.82), calls=%async_computation | async-start | bytes 1572864 | tf_op jit(solution)/shard_map/all_to_all | solution.py:33
  30.5 0.0 copy-start.12
  30.5 41.4 %all-gather.1 = bf16[1024,128]{1,0:T(8,128)(2,1)S(1)} all-gather(bf16[128,128]{1,0:T(8,128)(2,1)S(1)} %reduce_sum.28.q_ref), channel_id=3, replica_groups=mesh['seq'=8,'head'=4] {'seq'}, dimensions={0}, use_global_device_ids=true | all-gather | bytes 294912 | tf_op jit(solution)/shard_map/all_gather | solution.py:321
  71.9 2.2 copy-done.8
  74.1 2.2 copy-done.10
  76.3 4.4 %shard_map.86 = f32[8,136,128]{2,1,0:T(8,128)S(1)} custom-call(s32[1]{0:T(128)S(6)} %copy.9.len_ref, bf16[8,128,128]{2,1,0:T(8,128)(2,1)S(1)} %bitcast.7, bf16[8192,256]{1,0:T(8,128)(2,1)S(1)} %copy-done.8, bf16[8192,256]{1,0:T(8,128)(2,1)S(1)} %copy-done.10), custom_call_target="tpu_custom_call" | custom-call | flops 8589934592 | bytes 4194304 | tf_op jit(solution)/shard_map/pallas_call | solution.py:177
  80.7 0.0 copy-done.12
  80.7 0.8 convert_element_type.48
  81.5 0.0 all-to-all-done
  81.5 11.5 %all-to-all-start.3 = ((f16[8,136,128]{2,1,0:T(8,128)(2,1)}), f16[8,136,128]{2,1,0:T(8,128)(2,1)S(1)}, u32[]{:S(2)}, u32[]{:S(2)}) async-start(f16[8,136,128]{2,1,0:T(8,128)(2,1)} %convert_element_type.48), calls=%async_computation.3 | async-start | bytes 557056 | tf_op jit(solution)/shard_map/all_to_all | solution.py:33
  93.0 33.1 %all-gather = bf16[1536,128]{1,0:T(8,128)(2,1)S(1)} all-gather(bf16[192,128]{1,0:T(8,128)(2,1)S(1)} %reduce_sum.27), channel_id=2, replica_groups=mesh['seq'=8,'head'=4] {'seq'}, dimensions={0}, use_global_device_ids=true | all-gather | bytes 442368 | tf_op jit(solution)/shard_map/all_gather | solution.py:321
  126.2 2.2 copy-done.9
  128.4 2.2 copy-done.11
  130.5 4.6 %shard_map.83 = f32[8,136,128]{2,1,0:T(8,128)S(1)} custom-call(s32[1]{0:T(128)S(6)} %copy.9.len_ref, bf16[8,192,128]{2,1,0:T(8,128)(2,1)S(1)} %bitcast.5, bf16[8192,256]{1,0:T(8,128)(2,1)S(1)} %copy-done.9, bf16[8192,256]{1,0:T(8,128)(2,1)S(1)} %copy-done.11), custom_call_target="tpu_custom_call" | custom-call | flops 8589934592 | bytes 4194304 | tf_op jit(solution)/shard_map/pallas_call | solution.py:177
  135.2 0.8 convert_element_type.44
  135.9 0.0 all-to-all-done.3
  135.9 13.1 %all-to-all-start.1 = ((f16[8,136,128]{2,1,0:T(8,128)(2,1)}), f16[8,136,128]{2,1,0:T(8,128)(2,1)S(1)}, u32[]{:S(2)}, u32[]{:S(2)}) async-start(f16[8,136,128]{2,1,0:T(8,128)(2,1)} %convert_element_type.44), calls=%async_computation.1 | async-start | bytes 557056 | tf_op jit(solution)/shard_map/all_to_all | solution.py:33
  149.1 0.7 slice.9
  149.7 0.6 slice.8.q_ref
  150.3 0.8 convert_element_type.49.part_ref
  151.2 2.1 shard_map.87
  153.3 31.5 %all_gather.17.a_ref = bf16[1024,128]{1,0:T(8,128)(2,1)S(1)} all-gather(bf16[128,128]{1,0:T(8,128)(2,1)} %shard_map.87), channel_id=1, replica_groups=mesh['seq'=8,'head'=4] {'seq'}, dimensions={0}, use_global_device_ids=true | all-gather | bytes 294912 | tf_op jit(solution)/shard_map/all_gather | solution.py:329
  184.8 2.2 copy-done.2
  187.0 0.7 shard_map.88.refs_0_
  187.7 0.0 all-to-all-done.1
  187.7 0.8 convert_element_type.45.part_ref
  188.5 2.2 shard_map.84
  190.7 30.9 %all_gather.15.a_ref = bf16[1024,128]{1,0:T(8,128)(2,1)S(1)} all-gather(bf16[128,128]{1,0:T(8,128)(2,1)} %shard_map.84), channel_id=1, replica_groups=mesh['seq'=8,'head'=4] {'seq'}, dimensions={0}, use_global_device_ids=true | all-gather | bytes 294912 | tf_op jit(solution)/shard_map/all_gather | solution.py:329
  221.6 2.2 copy-done.3
  223.8 0.7 shard_map.89
  224.6 8.6 %all_to_all.25 = f16[4,32,1024]{2,1,0:T(8,128)(2,1)S(1)} all-to-all(f16[4,32,1024]{2,1,0:T(8,128)(2,1)S(1)} %bitcast.10), channel_id=1, replica_groups=mesh['seq'=8,'head'=4] {'head'}, dimensions={0} | all-to-all | bytes 524288 | tf_op jit(solution)/shard_map/all_to_all | solution.py:33
  233.3 0.6 multiply_convert_fusion.1
  (10 shorter events, 0.2 us)
Async XLA Ops:
  0.0 2.2 copy-start
  2.2 0.9 copy-start.4
  3.1 8.5 %copy-start.5 = (bf16[128,1024]{1,0:T(8,128)(2,1)S(1)}, bf16[128,1024]{1,0:T(8,128)(2,1)}, u32[]{:S(2)}) copy-start(bf16[128,1024]{1,0:T(8,128)(2,1)} %hidden_ref.3) | copy-start | bytes 786436
  3.1 8.5 %copy-start.6 = (bf16[1024,256]{1,0:T(8,128)(2,1)S(1)}, bf16[1024,256]{1,0:T(8,128)(2,1)}, u32[]{:S(2)}) copy-start(bf16[1024,256]{1,0:T(8,128)(2,1)} %refs_1_.1) | copy-start | bytes 1572868
  3.1 8.5 %copy-start.7 = (bf16[1024,256]{1,0:T(8,128)(2,1)S(1)}, bf16[1024,256]{1,0:T(8,128)(2,1)}, u32[]{:S(2)}) copy-start(bf16[1024,256]{1,0:T(8,128)(2,1)} %refs_2_.1) | copy-start | bytes 1572868
  4.4 21.7 %all-to-all-start.2 = ((f32[8,128,128]{2,1,0:T(8,128)}), f32[8,128,128]{2,1,0:T(8,128)S(1)}, u32[]{:S(2)}, u32[]{:S(2)}) async-start(f32[8,128,128]{2,1,0:T(8,128)} %shard_map.85), calls=%async_computation.2 | async-start | bytes 1048576 | tf_op jit(solution)/shard_map/all_to_all | solution.py:33
  11.7 2.2 copy-start.1
  26.1 55.3 %all-to-all-start = ((f32[8,192,128]{2,1,0:T(8,128)}), f32[8,192,128]{2,1,0:T(8,128)S(1)}, u32[]{:S(2)}, u32[]{:S(2)}) async-start(f32[8,192,128]{2,1,0:T(8,128)} %shard_map.82), calls=%async_computation | async-start | bytes 1572864 | tf_op jit(solution)/shard_map/all_to_all | solution.py:33
  30.5 50.2 %copy-start.12 = (bf16[128,128]{1,0:T(8,128)(2,1)}, bf16[128,128]{1,0:T(8,128)(2,1)S(1)}, u32[]{:S(2)}) copy-start(bf16[128,128]{1,0:T(8,128)(2,1)S(1)} %reduce_sum.28.q_ref) | copy-start | bytes 98308
  71.9 2.2 copy-start.8
  74.1 2.2 copy-start.10
  81.5 54.4 %all-to-all-start.3 = ((f16[8,136,128]{2,1,0:T(8,128)(2,1)}), f16[8,136,128]{2,1,0:T(8,128)(2,1)S(1)}, u32[]{:S(2)}, u32[]{:S(2)}) async-start(f16[8,136,128]{2,1,0:T(8,128)(2,1)} %convert_element_type.48), calls=%async_computation.3 | async-start | bytes 557056 | tf_op jit(solution)/shard_map/all_to_all | solution.py:33
  126.2 2.2 copy-start.9
  128.4 2.2 copy-start.11
  135.9 51.8 %all-to-all-start.1 = ((f16[8,136,128]{2,1,0:T(8,128)(2,1)}), f16[8,136,128]{2,1,0:T(8,128)(2,1)S(1)}, u32[]{:S(2)}, u32[]{:S(2)}) async-start(f16[8,136,128]{2,1,0:T(8,128)(2,1)} %convert_element_type.44), calls=%async_computation.1 | async-start | bytes 557056 | tf_op jit(solution)/shard_map/all_to_all | solution.py:33
  184.8 2.2 copy-start.2
  221.6 2.2 copy-start.3

commit v2 on v1

v2 whole, which is shorter than its diff:
```python
import functools
import math

import jax
import jax.numpy as jnp
from jax import lax
from jax.experimental import pallas as pl
from jax.experimental.pallas import tpu as pltpu
from jax.sharding import PartitionSpec as P

QH = 64
KVH = 8
HD = 128

NEG_BIG = -1e30
LANES = 128
STAT_ROWS = 8
VMEM_GRANT = 56 << 20
NT = (((1,), (1,)), ((), ()))

OUTPUT_SCALE = 2.0**12
MIXED_SCALE = 2.0**-3


def vmem_spec():
    return pl.BlockSpec(memory_space=pltpu.VMEM)


def smem_spec():
    return pl.BlockSpec(memory_space=pltpu.SMEM)


def hbm_spec():
    return pl.BlockSpec(memory_space=pl.ANY)


def with_partner(array):
    size = lax.axis_size("seq")
    return lax.ppermute(array, "seq", [(i, i ^ 1) for i in range(size)])


def within_parity(array):
    size = lax.axis_size("seq")
    groups = [list(range(first, size, 2)) for first in range(2)]
    return lax.all_to_all(array, "seq", 0, 0, axis_index_groups=groups)


def spread(block):
    half = lax.axis_size("seq") // 2
    same = within_parity(jnp.broadcast_to(block[None], (half,) + block.shape))
    return same, with_partner(same)


def project_kernel(me_ref, hidden_ref, *refs, blocks, chunk, columns, extra):
    weight_refs, (keep_ref, send_ref, w_all, sems) = refs[: 1 + extra], refs[1 + extra :]
    tokens = hidden_ref.shape[0]
    odd = lax.rem(me_ref[0], 2) == 1
    piece = w_all.shape[2]
    jobs = [(weight_refs[0], chunk * columns + c, 0) for c in range(0, columns, piece)]
    for other in weight_refs[1:]:
        jobs += [(other, c, 1) for c in range(0, other.shape[1], piece)]
    copies = []
    for i, (ref, start, _) in enumerate(jobs):
        copies.append(
            pltpu.make_async_copy(ref.at[:, pl.ds(start, piece)], w_all.at[i], sems.at[i])
        )
        copies[-1].start()
    hidden = hidden_ref[...]
    owner, waiting = [0, 0], [[], []]
    for i, (_, _, kind) in enumerate(jobs):
        block = blocks[kind]
        first = kind * blocks[0]
        copies[i].wait()
        product = jnp.dot(hidden, w_all[i], preferred_element_type=jnp.float32)
        parts = [
            product[e * block : (e + 1) * block, c * LANES : (c + 1) * LANES]
            for c in range(piece // LANES)
            for e in range(tokens // block)
        ]
        waiting[kind] += parts
        while len(waiting[kind]) > 1:
            even_part, odd_part = waiting[kind][:2]
            waiting[kind] = waiting[kind][2:]
            where = (owner[kind] // 2, slice(first, first + block), slice(None))
            keep_ref[where] = jnp.where(odd, odd_part, even_part)
            send_ref[where] = jnp.where(odd, even_part, odd_part)
            owner[kind] += 2


def project(me, hidden, weight, chunk, columns, others, count):
    tokens, depth = hidden.shape
    wide = [columns] + [other.shape[1] for other in others]
    blocks = [columns // LANES * tokens // count]
    if others:
        blocks.append(sum(wide[1:]) // LANES * tokens // count)
    total = sum(wide)
    piece = functools.reduce(math.gcd, wide, 2 * LANES)
    shape = jax.ShapeDtypeStruct((count // 2, sum(blocks), LANES), jnp.float32)
    return pl.pallas_call(
        functools.partial(
            project_kernel, blocks=blocks, chunk=chunk, columns=columns, extra=len(others)
        ),
        out_shape=[shape] * 2,
        in_specs=[smem_spec(), vmem_spec()] + [hbm_spec()] * (1 + len(others)),
        out_specs=[vmem_spec()] * 2,
        scratch_shapes=[
            pltpu.VMEM((total // piece, depth, piece), jnp.bfloat16),
            pltpu.SemaphoreType.DMA((total // piece,)),
        ],
        compiler_params=pltpu.CompilerParams(vmem_limit_bytes=VMEM_GRANT),
        cost_estimate=pl.CostEstimate(
            flops=2 * tokens * depth * total,
            bytes_accessed=2 * depth * total,
            transcendentals=0,
        ),
    )(me, hidden, weight, *others)


def attention_kernel(len_ref, me_ref, *refs, band, step, block, head):
    q_refs, (k_hbm, v_hbm, o_ref) = refs[:2], refs[2:5]
    k_ref, v_ref, sems = refs[5:8]
    s_bufs, m_bufs = refs[8:10], refs[10:12]
    shift, acc, lse_all = refs[12:]
    half = q_refs[0].shape[0]
    rows = 2 * half * block
    bands = rows // band
    share = band // block
    scale = math.log2(math.e) / math.sqrt(HD)
    piece = math.gcd(step, 1024)
    tiles = piece // LANES
    odd = lax.rem(me_ref[0], 2)

    length = len_ref[0]
    full = length // step
    rest = length - full * step

    def copy_in(source, target, which, i):
        where = pl.ds(pl.multiple_of(i * step, step), step)
        return pltpu.make_async_copy(
            source.at[where, pl.ds(head * HD, HD)], target.at[where, :], sems.at[which, i]
        )

    def keys_in(i):
        return copy_in(k_hbm, k_ref, 0, i)

    def values_in(i):
        return copy_in(v_hbm, v_ref, 1, i)

    needed = (length + step - 1) // step

    def start_keys(i, carry):
        keys_in(i).start()
        return carry

    def start_values(i, carry):
        values_in(i).start()
        return carry

    lax.fori_loop(0, needed, start_keys, 0)
    lax.fori_loop(0, needed, start_values, 0)

    def score(r, i, first, masked):
        source = q_refs[r * share // half]
        at = r * share % half
        q = source[at : at + share, :block, :].reshape(band, HD)
        keys = k_ref[pl.ds(pl.multiple_of(i * step + first, piece), piece), :]
        s = lax.dot_general(q, keys, NT, preferred_element_type=jnp.float32)
        if masked:
            column = first + lax.broadcasted_iota(jnp.int32, (band, piece), 1)
            s = jnp.where(column < rest, s, NEG_BIG)
        s_bufs[r % 2][i, :, first : first + piece] = s
        tops = [s[:, c * LANES : (c + 1) * LANES] for c in range(tiles)]
        while len(tops) > 1:
            tops = [jnp.maximum(a, b) for a, b in zip(tops[0::2], tops[1::2])]
        m_bufs[r % 2][...] = jnp.maximum(m_bufs[r % 2][...], tops[0])

    def weigh(r, i, first):
        s = s_bufs[r % 2][i, :, first : first + piece]
        low = shift[...]
        weights = jnp.concatenate(
            [
                jnp.exp2(s[:, c * LANES : (c + 1) * LANES] * scale - low).astype(jnp.bfloat16)
                for c in range(tiles)
            ],
            axis=1,
        )
        values = v_ref[pl.ds(pl.multiple_of(i * step + first, piece), piece), :]
        wide = jnp.concatenate([values, jnp.ones((piece, LANES), jnp.bfloat16)], axis=1)
        acc[...] += jnp.dot(weights, wide, preferred_element_type=jnp.float32)

    for r in range(bands + 1):
        scores, weighs = r < bands, r > 0
        if scores:
            m_bufs[r % 2][...] = jnp.full((band, LANES), -3e38, jnp.float32)
        if weighs:
            top = jnp.max(m_bufs[(r - 1) % 2][...], axis=1, keepdims=True)
            shift[...] = jnp.broadcast_to(top * scale, (band, LANES))
            acc[...] = jnp.zeros(acc.shape, jnp.float32)

        def both(i, masked):
            if r == 0:
                keys_in(i).wait()
            if r == 1:
                values_in(i).wait()
            for first in range(0, step, piece):
                if weighs:
                    weigh(r - 1, i, first)
                if scores:
                    score(r, i, first, masked)

        def body(i, carry):
            both(i, False)
            return carry

        lax.fori_loop(0, full, body, 0)

        @pl.when(rest > 0)
        def _():
            both(full, True)

        if weighs:
            totals = acc[:, LANES:]
            mean = acc[:, :LANES] / totals * OUTPUT_SCALE
            for e in range(share):
                k = (r - 1) * share + e
                owner = 2 * (k % half) + (odd if k < half else 1 - odd)
                o_ref[owner, :block, :] = mean[e * block : (e + 1) * block, :]
            lse_all[(r - 1) * band : r * band, :] = shift[...] + jnp.log2(totals)

    per = LANES // block
    row = lax.broadcasted_iota(jnp.int32, (STAT_ROWS, LANES), 0)
    for g in range(rows // LANES):
        level = lse_all[g * LANES : (g + 1) * LANES, :].T[:STAT_ROWS, :]
        exponent = jnp.floor(jnp.log2(jnp.maximum(jnp.abs(level), 1e-30)))
        exponent = jnp.minimum(exponent, 120.0)
        rest_of = level * jnp.exp2(-exponent)
        first = jnp.floor(rest_of * 2.0**9 + 0.5)
        rest_of = rest_of - first * 2.0**-9
        second = jnp.floor(rest_of * 2.0**20 + 0.5)
        third = (rest_of - second * 2.0**-20) * 2.0**31
        stats = jnp.where(row == 0, exponent, jnp.where(row == 1, first, second))
        stats = jnp.where(row >= 3, third, stats)
        for e in range(per):
            k = g * per + e
            owner = 2 * (k % half) + (odd if k < half else 1 - odd)
            o_ref[owner, block:, :] = stats


def attention(queries, block, keys, values, length, me, head):
    count = 2 * queries[0].shape[0]
    rows, slots = count * block, keys.shape[0]
    band = math.gcd(rows // 2, 256)
    step = math.gcd(slots, 2048)
    return pl.pallas_call(
        functools.partial(attention_kernel, band=band, step=step, block=block, head=head),
        out_shape=jax.ShapeDtypeStruct((count, block + STAT_ROWS, HD), jnp.float32),
        in_specs=[smem_spec()] * 2 + [vmem_spec()] * 2 + [hbm_spec()] * 2,
        out_specs=vmem_spec(),
        scratch_shapes=[
            pltpu.VMEM((slots, HD), jnp.bfloat16),
            pltpu.VMEM((slots, HD), jnp.bfloat16),
            pltpu.SemaphoreType.DMA((2, slots // step)),
            pltpu.VMEM((slots // step, band, step), jnp.float32),
            pltpu.VMEM((slots // step, band, step), jnp.float32),
            pltpu.VMEM((band, LANES), jnp.float32),
            pltpu.VMEM((band, LANES), jnp.float32),
            pltpu.VMEM((band, LANES), jnp.float32),
            pltpu.VMEM((band, 2 * LANES), jnp.float32),
            pltpu.VMEM((rows, LANES), jnp.float32),
        ],
        compiler_params=pltpu.CompilerParams(vmem_limit_bytes=VMEM_GRANT),
        cost_estimate=pl.CostEstimate(
            flops=8 * rows * slots * HD,
            bytes_accessed=4 * slots * HD,
            transcendentals=rows * slots,
        ),
    )(length, me, *queries, keys, values)


def merge_kernel(me_ref, part_ref, q_ref, kv_ref, o_ref, turned, *, head, kv_local, tokens):
    count = part_ref.shape[0]
    block = q_ref.shape[0]
    per = LANES // block
    scale = math.log2(math.e) / math.sqrt(HD)

    keys = kv_ref[head * tokens : (head + 1) * tokens, :]
    second = (kv_local + head) * tokens
    values = kv_ref[second : second + tokens, :]

    s = lax.dot_general(q_ref[...], keys, NT, preferred_element_type=jnp.float32) * scale
    token = lax.rem(me_ref[0] * block, tokens) + lax.broadcasted_iota(jnp.int32, s.shape, 0)
    visible = lax.broadcasted_iota(jnp.int32, s.shape, 1) <= token
    s = jnp.where(visible, s, NEG_BIG)
    new_top = jnp.max(s, axis=1, keepdims=True)
    weights = jnp.where(visible, jnp.exp2(s - new_top), 0.0).astype(jnp.bfloat16)
    new_total = jnp.sum(weights.astype(jnp.float32), axis=1, keepdims=True)
    new_out = jnp.dot(weights, values, preferred_element_type=jnp.float32)

    place = lax.rem(me_ref[0] // 2, per)
    pieces = part_ref[:, block : block + 4, :]
    level = pieces[:, 1, :] * 2.0**-9 + pieces[:, 2, :] * 2.0**-20 + pieces[:, 3, :] * 2.0**-31
    turned[...] = (level * jnp.exp2(pieces[:, 0, :])).T
    levels = turned[pl.ds(pl.multiple_of(place * block, block), block), :]
    joint = jnp.maximum(new_top, jnp.max(levels, axis=1, keepdims=True))
    factors = jnp.exp2(levels - joint)
    new_scale = jnp.exp2(new_top - joint)
    whole_out = new_out * new_scale
    whole_total = new_total * new_scale + jnp.sum(factors, axis=1, keepdims=True)
    scaled = factors * (1.0 / OUTPUT_SCALE)
    for k in range(count):
        whole_out = whole_out + part_ref[k, :block, :] * scaled[:, k : k + 1]
    o_ref[...] = (whole_out / whole_total).astype(jnp.bfloat16)


def merge(me, parts, q_mine, kv, head, kv_local, tokens):
    return pl.pallas_call(
        functools.partial(merge_kernel, head=head, kv_local=kv_local, tokens=tokens),
        out_shape=jax.ShapeDtypeStruct(q_mine.shape, jnp.bfloat16),
        in_specs=[smem_spec()] + [vmem_spec()] * 3,
        out_specs=vmem_spec(),
        scratch_shapes=[pltpu.VMEM((LANES, parts.shape[0]), jnp.float32)],
    )(me, parts, q_mine, kv)


def output_kernel(me_ref, w_ref, *refs, tokens, groups, has_before, chunk):
    a_refs = refs[:2]
    before = refs[2] if has_before else None
    o_ref, w_all, a_all, sems = refs[-4:]
    copies = []
    for g in range(groups):
        copies.append(
            pltpu.make_async_copy(
                w_ref.at[pl.ds((chunk * groups + g) * HD, HD), :],
                w_all.at[pl.ds(g * HD, HD), :],
                sems.at[g],
            )
        )
        copies[-1].start()
    half, block = a_refs[0].shape[:2]
    per = tokens // block
    odd = lax.rem(me_ref[0], 2)
    for a_ref, parity in zip(a_refs, (odd, 1 - odd)):
        for k in range(half):
            owner = 2 * k + parity
            start = pl.multiple_of(lax.rem(owner, per) * block, block)
            a_all[owner // per, pl.ds(start, block), :] = a_ref[k]
    rows = jnp.concatenate([a_all[g] for g in range(groups)], axis=1)
    for copy in copies:
        copy.wait()
    product = jnp.dot(rows, w_all[...], preferred_element_type=jnp.float32)
    if has_before:
        product = product + before[...]
    o_ref[...] = product


def output_part(me, weight, attended, tokens, before, chunk):
    groups = QH // KVH
    width = weight.shape[1]
    has_before = before is not None
    return pl.pallas_call(
        functools.partial(
            output_kernel, tokens=tokens, groups=groups, has_before=has_before, chunk=chunk
        ),
        out_shape=jax.ShapeDtypeStruct((tokens, width), jnp.float32),
        in_specs=[smem_spec(), hbm_spec()] + [vmem_spec()] * (2 + int(has_before)),
        out_specs=vmem_spec(),
        scratch_shapes=[
            pltpu.VMEM((groups * HD, width), jnp.bfloat16),
            pltpu.VMEM((groups, tokens, HD), jnp.bfloat16),
            pltpu.SemaphoreType.DMA((groups,)),
        ],
        compiler_params=pltpu.CompilerParams(vmem_limit_bytes=VMEM_GRANT),
        cost_estimate=pl.CostEstimate(
            flops=2 * tokens * groups * HD * width,
            bytes_accessed=2 * groups * HD * width,
            transcendentals=0,
        ),
    )(me, weight, *attended, *([before] if has_before else []))


def shards(
    hidden,
    query_weight,
    key_weight,
    value_weight,
    output_weight,
    cache_keys,
    cache_values,
    cache_lens,
):
    tokens = hidden.shape[0]
    count = lax.axis_size("seq")
    heads = lax.axis_size("head")
    kv_local = cache_keys.shape[1] // HD
    columns = (QH // KVH) * HD
    block = (QH // KVH) * tokens // count
    me = lax.axis_index("seq").reshape(1)

    mine = []
    for j in range(kv_local):
        others = [key_weight, value_weight] if j == kv_local - 1 else []
        keep, send = project(me, hidden, query_weight, j, columns, others, count)
        total = jnp.sum(within_parity(keep + with_partner(send)), axis=0)
        mine.append(total.astype(jnp.bfloat16))
    queries = [spread(rows) for rows in mine]
    same, other = (rows[:, None, block:, :] for rows in queries[-1])
    even = jnp.concatenate([same, other], axis=1)
    odd = jnp.concatenate([other, same], axis=1)
    kv = jnp.where(me[0] % 2 == 0, even, odd).reshape(-1, HD)

    mixed = None
    for j in range(kv_local):
        parts = attention(queries[j], block, cache_keys, cache_values, cache_lens, me, j)
        parts = lax.all_to_all(parts.astype(jnp.float16), "seq", 0, 0).astype(jnp.float32)
        attended = merge(me, parts, mine[j][:block], kv, j, kv_local, tokens)
        mixed = output_part(me, output_weight, spread(attended), tokens, mixed, j)

    mixed = (mixed * MIXED_SCALE).reshape(heads, tokens // heads, mixed.shape[1])
    mixed = jnp.sum(
        lax.all_to_all(mixed.astype(jnp.float16), "head", 0, 0).astype(jnp.float32), axis=0
    )
    return (mixed * (1.0 / MIXED_SCALE)).astype(jnp.bfloat16)


def solution(mesh):
    placed = (
        P(None, "seq"),
        P("seq", "head"),
        P("seq", "head"),
        P("seq", "head"),
        P("head", "seq"),
        P("seq", "head"),
        P("seq", "head"),
        P("seq"),
    )
    return jax.shard_map(
        shards, mesh=mesh, in_specs=placed, out_specs=P("head", "seq"), check_vma=False
    )
```

time: 233 us -> 160 us (0.69); the launches traced: 234 us -> 158 us
  blocking collectives: 146 us -> 8.63 us
  waiting for transfers between devices: 10.8 us -> 38.1 us
  Pallas kernels: 17.4 us -> 41.4 us
  starting transfers between devices: 35.5 us -> 49.4 us
  local copies, waits for them, and re-layouts: 19.7 us -> 9.84 us
  other arithmetic: 3.99 us -> 9.64 us
    all_gather x4 -> x0, blocking collectives: 137 us -> none  [the longest x2 74.5 us: shards(): queries = [lax.all_gather(rows, 'seq') for rows in mine]]
    all_to_all x4 -> x8, waiting for transfers between devices: 10.8 us -> 33.1 us  [the longest x6 30.6 us: within_parity(): return lax.all_to_all(array, 'seq', 0, 0, axis_index_groups=groups)]
    unnamed x26 -> x18, local copies, waits for them, and re-layouts: 18.5 us -> 2.64 us
    pallas_call x2, Pallas kernels: 9.02 us -> 19.5 us  [attention(): pl.pallas_call(functools.partial(attention_kernel, band=band, step=step,...]
    all_to_all x4 -> x8, starting transfers between devices: 35.5 us -> 43.3 us  [the longest x6 22.4 us: within_parity(): return lax.all_to_all(array, 'seq', 0, 0, axis_index_groups=groups)]
    pallas_call x2, Pallas kernels: 1.38 us -> 7.82 us  [output_part(): pl.pallas_call(functools.partial(output_kernel, tokens=tokens, groups=gro...]
    ppermute x0 -> x6, starting transfers between devices: none -> 6.12 us  [with_partner(): return lax.ppermute(array, 'seq', [(i, i ^ 1) for i in range(size)])]
    broadcast_in_dim x0 -> x6, local copies, waits for them, and re-layouts: none -> 5.93 us  [the longest x4 4.24 us: spread(): same = within_parity(jnp.broadcast_to(block[None], (half,) + block.shape))]
  transfers between devices with their start and end apart: 4 -> 14, of which waited for: 1 -> 9; matrix products, arithmetic and copies ran while one was open for 2% -> 7% of each run, Pallas kernels for 6% -> 21%
where the time goes in v2:
time: 160 us; the launch traced here: 158 us
  starting transfers between devices  49.4 us (31%)
  Pallas kernels  41.4 us (26%)
  waiting for transfers between devices  38.1 us (24%)
  local copies, waits for them, and re-layouts  9.84 us (6%)
  other arithmetic  9.64 us (6%)
  blocking collectives  8.63 us (5%)
    all_to_all x6, waiting for transfers between devices, within_parity(): return lax.all_to_all(array, 'seq', 0, 0, axis_index_groups=groups)  30.6 us
    all_to_all x6, starting transfers between devices, within_parity(): return lax.all_to_all(array, 'seq', 0, 0, axis_index_groups=groups)  22.4 us
    all_to_all x2, starting transfers between devices, shards(): lax.all_to_all(parts.astype(jnp.float16), 'seq', 0, 0).astype(jnp.float32)  20.9 us
    pallas_call x2, Pallas kernels, attention(): pl.pallas_call(functools.partial(attention_kernel, band=band, step=step,...  19.5 us
    all_to_all x1, blocking collectives, shards(): lax.all_to_all(mixed.astype(jnp.float16), 'head', 0, 0).astype(jnp.float32)  8.63 us
    pallas_call x2, Pallas kernels, project(): pl.pallas_call(functools.partial(project_kernel, blocks=blocks, chunk=chu...  8.62 us
    pallas_call x2, Pallas kernels, output_part(): pl.pallas_call(functools.partial(output_kernel, tokens=tokens, groups=gro...  7.82 us
    ppermute x6, starting transfers between devices, with_partner(): return lax.ppermute(array, 'seq', [(i, i ^ 1) for i in range(size)])  6.12 us
  transfers between devices with their start and end apart: 14, of which 9 were waited for; matrix products, arithmetic and copies ran while one was open for 7% of the time, Pallas kernels for 21%

profile of v2, /device:TPU:0, one launch (start us, length us, event | category | flops | bytes accessed | tf_op | source)
XLA Modules:
  0.0 157.9 jit_solution(13422174049708088301)
XLA Ops:
  0.0 4.0 %shard_map.85 = (f32[4,128,128]{2,1,0:T(8,128)}, f32[4,128,128]{2,1,0:T(8,128)}) custom-call(s32[1]{0:T(128)} %bitcast.me_ref, bf16[128,1024]{1,0:T(8,128)(2,1)} %hidden_ref.3, bf16[1024,2048]{1,0:T(8,128)(2,1)} %refs_0_.3), custom_call_target="tpu_custom_call" | custom-call | flops 268435456 | bytes 2097152 | tf_op jit(solution)/shard_map/pallas_call | solution.py:99
  4.0 3.0 %collective-permute-start.3 = (f32[4,128,128]{2,1,0:T(8,128)}, f32[4,128,128]{2,1,0:T(8,128)S(1)}, u32[]{:S(2)}, u32[]{:S(2)}) collective-permute-start(f32[4,128,128]{2,1,0:T(8,128)} %get-tuple-element.12), channel_id=1, source_target_pairs={{0,4},{4,0},{8,12},{12,8},{16,20},{20,16},{24,28},{28,24},{1,5},{5... | collective-permute-start | bytes 786440 | tf_op jit(solution)/shard_map/ppermute | solution.py:39
  7.0 4.6 %shard_map.82 = (f32[4,192,128]{2,1,0:T(8,128)}, f32[4,192,128]{2,1,0:T(8,128)}) custom-call(s32[1]{0:T(128)} %bitcast.me_ref, bf16[128,1024]{1,0:T(8,128)(2,1)} %hidden_ref.3, bf16[1024,2048]{1,0:T(8,128)(2,1)} %refs_0_.3, bf16[1024,256]{1,0:T(8,128)(2,1)} %refs_1_.1, bf16[1024,256]{1,0:T(8,128)(2,1)} %refs_2_.3), custom_call_target="tpu_custom_call" | custom-call | flops 402653184 | bytes 3145728 | tf_op jit(solution)/shard_map/pallas_call | solution.py:99
  11.7 2.0 %collective-permute-done.3 = f32[4,128,128]{2,1,0:T(8,128)S(1)} collective-permute-done((f32[4,128,128]{2,1,0:T(8,128)}, f32[4,128,128]{2,1,0:T(8,128)S(1)}, u32[]{:S(2)}, u32[]{:S(2)}) %collective-permute-start.3) | collective-permute-done | bytes 262176 | tf_op jit(solution)/shard_map/ppermute | solution.py:39
  13.7 0.7 add.12
  14.4 4.9 %all-to-all-start.4 = ((f32[4,128,128]{2,1,0:T(8,128)}), f32[4,128,128]{2,1,0:T(8,128)S(1)}, u32[]{:S(2)}, u32[]{:S(2)}) async-start(f32[4,128,128]{2,1,0:T(8,128)} %add.12), calls=%async_computation.4 | async-start | bytes 524288 | tf_op jit(solution)/shard_map/all_to_all | solution.py:45
  19.4 3.1 %collective-permute-done = f32[4,192,128]{2,1,0:T(8,128)S(1)} collective-permute-done((f32[4,192,128]{2,1,0:T(8,128)}, f32[4,192,128]{2,1,0:T(8,128)S(1)}, u32[]{:S(2)}, u32[]{:S(2)}) %collective-permute-start) | collective-permute-done | bytes 393248 | tf_op jit(solution)/shard_map/ppermute | solution.py:39
  22.5 1.8 %add.10 = f32[4,192,128]{2,1,0:T(8,128)} add(f32[4,192,128]{2,1,0:T(8,128)} %get-tuple-element.9, f32[4,192,128]{2,1,0:T(8,128)S(1)} %collective-permute-done) | non-fusion elementwise | flops 98304 | bytes 1179648 | tf_op jit(solution)/shard_map/add | solution.py:403
  24.3 3.3 %all-to-all-done.4 = f32[4,128,128]{2,1,0:T(8,128)S(1)} async-done(((f32[4,128,128]{2,1,0:T(8,128)}), f32[4,128,128]{2,1,0:T(8,128)S(1)}, u32[]{:S(2)}, u32[]{:S(2)}) %all-to-all-start.4) | async-done | bytes 262176 | tf_op jit(solution)/shard_map/all_to_all | solution.py:45
  27.6 3.5 %all-to-all-start = ((f32[4,192,128]{2,1,0:T(8,128)}), f32[4,192,128]{2,1,0:T(8,128)S(1)}, u32[]{:S(2)}, u32[]{:S(2)}) async-start(f32[4,192,128]{2,1,0:T(8,128)} %add.10), calls=%async_computation | async-start | bytes 786432 | tf_op jit(solution)/shard_map/all_to_all | solution.py:45
  31.1 9.8 %all-to-all-done = f32[4,192,128]{2,1,0:T(8,128)S(1)} async-done(((f32[4,192,128]{2,1,0:T(8,128)}), f32[4,192,128]{2,1,0:T(8,128)S(1)}, u32[]{:S(2)}, u32[]{:S(2)}) %all-to-all-start) | async-done | bytes 393248 | tf_op jit(solution)/shard_map/all_to_all | solution.py:45
  40.8 0.7 broadcast_in_dim.16
  41.5 3.3 %all-to-all-start.5 = ((bf16[4,128,128]{2,1,0:T(8,128)(2,1)}), bf16[4,128,128]{2,1,0:T(8,128)(2,1)S(1)}, u32[]{:S(2)}, u32[]{:S(2)}) async-start(bf16[4,128,128]{2,1,0:T(8,128)(2,1)} %broadcast_in_dim.16), calls=%async_computation.5 | async-start | bytes 262144 | tf_op jit(solution)/shard_map/all_to_all | solution.py:45
  44.9 5.9 %all-to-all-done.5.refs_0_ = bf16[4,128,128]{2,1,0:T(8,128)(2,1)S(1)} async-done(((bf16[4,128,128]{2,1,0:T(8,128)(2,1)}), bf16[4,128,128]{2,1,0:T(8,128)(2,1)S(1)}, u32[]{:S(2)}, u32[]{:S(2)}) %all-to-all-start.5) | async-done | bytes 131104 | tf_op jit(solution)/shard_map/all_to_all | solution.py:45
  50.7 0.7 broadcast_in_dim.12
  51.4 4.0 %all-to-all-start.1 = ((bf16[4,192,128]{2,1,0:T(8,128)(2,1)}), bf16[4,192,128]{2,1,0:T(8,128)(2,1)}, u32[]{:S(2)}, u32[]{:S(2)}) async-start(bf16[4,192,128]{2,1,0:T(8,128)(2,1)} %broadcast_in_dim.12), calls=%async_computation.1 | async-start | bytes 393216 | tf_op jit(solution)/shard_map/all_to_all | solution.py:45
  55.4 0.7 collective-permute-start.4
  56.8 4.9 %all-to-all-done.1.refs_0_ = bf16[4,192,128]{2,1,0:T(8,128)(2,1)} async-done(((bf16[4,192,128]{2,1,0:T(8,128)(2,1)}), bf16[4,192,128]{2,1,0:T(8,128)(2,1)}, u32[]{:S(2)}, u32[]{:S(2)}) %all-to-all-start.1) | async-done | bytes 196640 | tf_op jit(solution)/shard_map/all_to_all | solution.py:45
  61.8 0.6 collective-permute-start.1
  62.4 0.6 copy-done.8
  63.1 9.7 %shard_map.86 = f32[8,136,128]{2,1,0:T(8,128)} custom-call(s32[1]{0:T(128)S(6)} %copy.10.len_ref, s32[1]{0:T(128)} %bitcast.me_ref, bf16[4,128,128]{2,1,0:T(8,128)(2,1)} %copy-done.6, bf16[4,128,128]{2,1,0:T(8,128)(2,1)} %copy-done.8, bf16[8192,256]{1,0:T(8,128)(2,1)} %refs_2_.5, bf16[8192,256]{1,0:T(8,128)(2,1)} %refs_3_.3), custom_call_target="tpu_custom_call" | custom-call | flops 8589934592 | bytes 4194304 | tf_op jit(solution)/shard_map/pallas_call | solution.py:254
  72.7 1.8 %convert_element_type.38 = f16[8,136,128]{2,1,0:T(8,128)(2,1)} convert(f32[8,136,128]{2,1,0:T(8,128)} %shard_map.86) | non-fusion elementwise | flops 139264 | bytes 835584 | tf_op jit(solution)/shard_map/convert_element_type | solution.py:414
  74.5 9.7 %all-to-all-start.6 = ((f16[8,136,128]{2,1,0:T(8,128)(2,1)}), f16[8,136,128]{2,1,0:T(8,128)(2,1)S(1)}, u32[]{:S(2)}, u32[]{:S(2)}) async-start(f16[8,136,128]{2,1,0:T(8,128)(2,1)} %convert_element_type.38), calls=%async_computation.6 | async-start | bytes 557056 | tf_op jit(solution)/shard_map/all_to_all | solution.py:414
  84.2 0.7 copy-done.7
  84.9 9.9 %shard_map.83 = f32[8,136,128]{2,1,0:T(8,128)} custom-call(s32[1]{0:T(128)S(6)} %copy.10.len_ref, s32[1]{0:T(128)} %bitcast.me_ref, bf16[4,192,128]{2,1,0:T(8,128)(2,1)} %all-to-all-done.1.refs_0_, bf16[4,192,128]{2,1,0:T(8,128)(2,1)} %copy-done.7, bf16[8192,256]{1,0:T(8,128)(2,1)} %refs_2_.5, bf16[8192,256]{1,0:T(8,128)(2,1)} %refs_3_.3), custom_call_target="tpu_custom_call" | custom-call | flops 8589934592 | bytes 4194304 | tf_op jit(solution)/shard_map/pallas_call | solution.py:254
  94.8 1.8 %convert_element_type.35 = f16[8,136,128]{2,1,0:T(8,128)(2,1)} convert(f32[8,136,128]{2,1,0:T(8,128)} %shard_map.83) | non-fusion elementwise | flops 139264 | bytes 835584 | tf_op jit(solution)/shard_map/convert_element_type | solution.py:414
  96.6 11.2 %all-to-all-start.2 = ((f16[8,136,128]{2,1,0:T(8,128)(2,1)}), f16[8,136,128]{2,1,0:T(8,128)(2,1)S(1)}, u32[]{:S(2)}, u32[]{:S(2)}) async-start(f16[8,136,128]{2,1,0:T(8,128)(2,1)} %convert_element_type.35), calls=%async_computation.2 | async-start | bytes 557056 | tf_op jit(solution)/shard_map/all_to_all | solution.py:414
  107.8 0.8 slice_bitcast_fusion.1
  108.7 0.8 convert_element_type.39.part_ref
  109.5 0.8 slice_bitcast_fusion
  110.4 0.6 copy.9
  111.0 2.7 %shard_map.87 = bf16[128,128]{1,0:T(8,128)(2,1)} custom-call(s32[1]{0:T(128)} %bitcast.me_ref, f32[8,136,128]{2,1,0:T(8,128)} %convert_element_type.39.part_ref, bf16[128,128]{1,0:T(8,128)(2,1)} %copy-done.2, bf16[512,128]{1,0:T(8,128)(2,1)} %bitcast.7), custom_call_target="tpu_custom_call" | custom-call | tf_op jit(solution)/shard_map/pallas_call | solution.py:316
  113.7 2.4 %all-to-all-done.2 = f16[8,136,128]{2,1,0:T(8,128)(2,1)S(1)} async-done(((f16[8,136,128]{2,1,0:T(8,128)(2,1)}), f16[8,136,128]{2,1,0:T(8,128)(2,1)S(1)}, u32[]{:S(2)}, u32[]{:S(2)}) %all-to-all-start.2) | async-done | bytes 278560 | tf_op jit(solution)/shard_map/all_to_all | solution.py:414
  116.1 1.4 broadcast_in_dim.17
  117.6 3.3 %all-to-all-start.7 = ((bf16[4,128,128]{2,1,0:T(8,128)(2,1)}), bf16[4,128,128]{2,1,0:T(8,128)(2,1)S(1)}, u32[]{:S(2)}, u32[]{:S(2)}) async-start(bf16[4,128,128]{2,1,0:T(8,128)(2,1)} %broadcast_in_dim.17), calls=%async_computation.7 | async-start | bytes 262144 | tf_op jit(solution)/shard_map/all_to_all | solution.py:45
  121.5 0.8 convert_element_type.36.part_ref
  122.4 2.7 %shard_map.84 = bf16[128,128]{1,0:T(8,128)(2,1)} custom-call(s32[1]{0:T(128)} %bitcast.me_ref, f32[8,136,128]{2,1,0:T(8,128)} %convert_element_type.36.part_ref, bf16[128,128]{1,0:T(8,128)(2,1)} %slice.12.q_ref, bf16[512,128]{1,0:T(8,128)(2,1)} %bitcast.8), custom_call_target="tpu_custom_call" | custom-call | tf_op jit(solution)/shard_map/pallas_call | solution.py:316
  125.1 1.7 %all-to-all-done.7.refs_0_ = bf16[4,128,128]{2,1,0:T(8,128)(2,1)S(1)} async-done(((bf16[4,128,128]{2,1,0:T(8,128)(2,1)}), bf16[4,128,128]{2,1,0:T(8,128)(2,1)S(1)}, u32[]{:S(2)}, u32[]{:S(2)}) %all-to-all-start.7) | async-done | bytes 131104 | tf_op jit(solution)/shard_map/all_to_all | solution.py:45
  126.8 1.4 broadcast_in_dim.15
  128.2 3.4 %all-to-all-start.3 = ((bf16[4,128,128]{2,1,0:T(8,128)(2,1)}), bf16[4,128,128]{2,1,0:T(8,128)(2,1)S(1)}, u32[]{:S(2)}, u32[]{:S(2)}) async-start(bf16[4,128,128]{2,1,0:T(8,128)(2,1)} %broadcast_in_dim.15), calls=%async_computation.3 | async-start | bytes 262144 | tf_op jit(solution)/shard_map/all_to_all | solution.py:45
  131.6 0.9 collective-permute-start.5
  132.4 5.1 %all-to-all-done.3.refs_0_ = bf16[4,128,128]{2,1,0:T(8,128)(2,1)S(1)} async-done(((bf16[4,128,128]{2,1,0:T(8,128)(2,1)}), bf16[4,128,128]{2,1,0:T(8,128)(2,1)S(1)}, u32[]{:S(2)}, u32[]{:S(2)}) %all-to-all-start.3) | async-done | bytes 131104 | tf_op jit(solution)/shard_map/all_to_all | solution.py:45
  137.5 0.8 collective-permute-start.2
  138.3 0.7 copy-done.4
  139.0 3.8 %shard_map.88.refs_2_ = f32[128,1024]{1,0:T(8,128)} custom-call(s32[1]{0:T(128)} %bitcast.me_ref, bf16[2048,1024]{1,0:T(8,128)(2,1)} %w_ref.3, bf16[4,128,128]{2,1,0:T(8,128)(2,1)} %copy-done, bf16[4,128,128]{2,1,0:T(8,128)(2,1)} %copy-done.4), custom_call_target="tpu_custom_call" | custom-call | flops 268435456 | bytes 2097152 | tf_op jit(solution)/shard_map/pallas_call | solution.py:360
  143.5 4.0 %shard_map.89 = f32[128,1024]{1,0:T(8,128)} custom-call(s32[1]{0:T(128)} %bitcast.me_ref, bf16[2048,1024]{1,0:T(8,128)(2,1)} %w_ref.3, bf16[4,128,128]{2,1,0:T(8,128)(2,1)} %copy-done.1, bf16[4,128,128]{2,1,0:T(8,128)(2,1)} %copy-done.5, f32[128,1024]{1,0:T(8,128)} %shard_map.88.refs_2_), custom_call_target="tpu_custom_call" | custom-call | flops 268435456 | bytes 2097152 | tf_op jit(solution)/shard_map/pallas_call | solution.py:360
  147.5 1.1 multiply_convert_fusion
  148.6 8.6 %all_to_all.45 = f16[4,32,1024]{2,1,0:T(8,128)(2,1)S(1)} all-to-all(f16[4,32,1024]{2,1,0:T(8,128)(2,1)S(1)} %bitcast.9), channel_id=1, replica_groups=mesh['seq'=8,'head'=4] {'head'}, dimensions={0} | all-to-all | bytes 524288 | tf_op jit(solution)/shard_map/all_to_all | solution.py:420
  (27 shorter events, 2.1 us)
Async XLA Ops:
  4.0 9.7 %copy-start.3 = (f32[4,128,128]{2,1,0:T(8,128)S(1)}, f32[4,128,128]{2,1,0:T(8,128)}, u32[]{:S(2)}) copy-start(f32[4,128,128]{2,1,0:T(8,128)} %get-tuple-element.11) | copy-start | bytes 786436
  4.0 9.7 %collective-permute-start.3 = (f32[4,128,128]{2,1,0:T(8,128)}, f32[4,128,128]{2,1,0:T(8,128)S(1)}, u32[]{:S(2)}, u32[]{:S(2)}) collective-permute-start(f32[4,128,128]{2,1,0:T(8,128)} %get-tuple-element.12), channel_id=1, source_target_pairs={{0,4},{4,0},{8,12},{12,8},{16,20},{20,16},{24,28},{28,24},{1,5},{5... | collective-permute-start | bytes 786440 | tf_op jit(solution)/shard_map/ppermute | solution.py:39
  11.7 10.8 %collective-permute-start = (f32[4,192,128]{2,1,0:T(8,128)}, f32[4,192,128]{2,1,0:T(8,128)S(1)}, u32[]{:S(2)}, u32[]{:S(2)}) collective-permute-start(f32[4,192,128]{2,1,0:T(8,128)} %get-tuple-element.10), channel_id=1, source_target_pairs={{0,4},{4,0},{8,12},{12,8},{16,20},{20,16},{24,28},{28,24},{1,5},{5... | collective-permute-start | bytes 1179656 | tf_op jit(solution)/shard_map/ppermute | solution.py:39
  14.4 13.1 %all-to-all-start.4 = ((f32[4,128,128]{2,1,0:T(8,128)}), f32[4,128,128]{2,1,0:T(8,128)S(1)}, u32[]{:S(2)}, u32[]{:S(2)}) async-start(f32[4,128,128]{2,1,0:T(8,128)} %add.12), calls=%async_computation.4 | async-start | bytes 524288 | tf_op jit(solution)/shard_map/all_to_all | solution.py:45
  27.6 13.3 %all-to-all-start = ((f32[4,192,128]{2,1,0:T(8,128)}), f32[4,192,128]{2,1,0:T(8,128)S(1)}, u32[]{:S(2)}, u32[]{:S(2)}) async-start(f32[4,192,128]{2,1,0:T(8,128)} %add.10), calls=%async_computation | async-start | bytes 786432 | tf_op jit(solution)/shard_map/all_to_all | solution.py:45
  31.1 41.7 %copy-start.2 = (bf16[128,128]{1,0:T(8,128)(2,1)}, bf16[128,128]{1,0:T(8,128)(2,1)S(1)}, u32[]{:S(2)}) copy-start(bf16[128,128]{1,0:T(8,128)(2,1)S(1)} %reduce_sum.28.q_ref) | copy-start | bytes 98308
  41.5 9.2 %all-to-all-start.5 = ((bf16[4,128,128]{2,1,0:T(8,128)(2,1)}), bf16[4,128,128]{2,1,0:T(8,128)(2,1)S(1)}, u32[]{:S(2)}, u32[]{:S(2)}) async-start(bf16[4,128,128]{2,1,0:T(8,128)(2,1)} %broadcast_in_dim.16), calls=%async_computation.5 | async-start | bytes 262144 | tf_op jit(solution)/shard_map/all_to_all | solution.py:45
  50.7 11.7 %copy-start.6 = (bf16[4,128,128]{2,1,0:T(8,128)(2,1)}, bf16[4,128,128]{2,1,0:T(8,128)(2,1)S(1)}, u32[]{:S(2)}) copy-start(bf16[4,128,128]{2,1,0:T(8,128)(2,1)S(1)} %all-to-all-done.5.refs_0_) | copy-start | bytes 393220
  51.4 10.3 %all-to-all-start.1 = ((bf16[4,192,128]{2,1,0:T(8,128)(2,1)}), bf16[4,192,128]{2,1,0:T(8,128)(2,1)}, u32[]{:S(2)}, u32[]{:S(2)}) async-start(bf16[4,192,128]{2,1,0:T(8,128)(2,1)} %broadcast_in_dim.12), calls=%async_computation.1 | async-start | bytes 393216 | tf_op jit(solution)/shard_map/all_to_all | solution.py:45
  55.4 7.0 %collective-permute-start.4 = (bf16[4,128,128]{2,1,0:T(8,128)(2,1)S(1)}, bf16[4,128,128]{2,1,0:T(8,128)(2,1)S(1)}, u32[]{:S(2)}, u32[]{:S(2)}) collective-permute-start(bf16[4,128,128]{2,1,0:T(8,128)(2,1)S(1)} %all-to-all-done.5.refs_0_), channel_id=1, source_target_pairs={{0,4},{4,0},{8,12},{12,8},{16,20},{20,16},{24,28},{28,24},{1,5},{5... | collective-permute-start | bytes 393224 | tf_op jit(solution)/shard_map/ppermute | solution.py:39
  61.8 22.5 %collective-permute-start.1 = (bf16[4,192,128]{2,1,0:T(8,128)(2,1)}, bf16[4,192,128]{2,1,0:T(8,128)(2,1)S(1)}, u32[]{:S(2)}, u32[]{:S(2)}) collective-permute-start(bf16[4,192,128]{2,1,0:T(8,128)(2,1)} %all-to-all-done.1.refs_0_), channel_id=1, source_target_pairs={{0,4},{4,0},{8,12},{12,8},{16,20},{20,16},{24,28},{28,24},{1,5},{5... | collective-permute-start | bytes 589832 | tf_op jit(solution)/shard_map/ppermute | solution.py:39
  62.4 0.7 copy-start.8
  74.5 22.1 %all-to-all-start.6 = ((f16[8,136,128]{2,1,0:T(8,128)(2,1)}), f16[8,136,128]{2,1,0:T(8,128)(2,1)S(1)}, u32[]{:S(2)}, u32[]{:S(2)}) async-start(f16[8,136,128]{2,1,0:T(8,128)(2,1)} %convert_element_type.38), calls=%async_computation.6 | async-start | bytes 557056 | tf_op jit(solution)/shard_map/all_to_all | solution.py:414
  84.2 0.7 copy-start.7
  96.6 19.6 %all-to-all-start.2 = ((f16[8,136,128]{2,1,0:T(8,128)(2,1)}), f16[8,136,128]{2,1,0:T(8,128)(2,1)S(1)}, u32[]{:S(2)}, u32[]{:S(2)}) async-start(f16[8,136,128]{2,1,0:T(8,128)(2,1)} %convert_element_type.35), calls=%async_computation.2 | async-start | bytes 557056 | tf_op jit(solution)/shard_map/all_to_all | solution.py:414
  117.6 9.2 %all-to-all-start.7 = ((bf16[4,128,128]{2,1,0:T(8,128)(2,1)}), bf16[4,128,128]{2,1,0:T(8,128)(2,1)S(1)}, u32[]{:S(2)}, u32[]{:S(2)}) async-start(bf16[4,128,128]{2,1,0:T(8,128)(2,1)} %broadcast_in_dim.17), calls=%async_computation.7 | async-start | bytes 262144 | tf_op jit(solution)/shard_map/all_to_all | solution.py:45
  126.8 11.5 %copy-start = (bf16[4,128,128]{2,1,0:T(8,128)(2,1)}, bf16[4,128,128]{2,1,0:T(8,128)(2,1)S(1)}, u32[]{:S(2)}) copy-start(bf16[4,128,128]{2,1,0:T(8,128)(2,1)S(1)} %all-to-all-done.7.refs_0_) | copy-start | bytes 393220
  128.2 9.3 %all-to-all-start.3 = ((bf16[4,128,128]{2,1,0:T(8,128)(2,1)}), bf16[4,128,128]{2,1,0:T(8,128)(2,1)S(1)}, u32[]{:S(2)}, u32[]{:S(2)}) async-start(bf16[4,128,128]{2,1,0:T(8,128)(2,1)} %broadcast_in_dim.15), calls=%async_computation.3 | async-start | bytes 262144 | tf_op jit(solution)/shard_map/all_to_all | solution.py:45
  131.6 6.8 %collective-permute-start.5 = (bf16[4,128,128]{2,1,0:T(8,128)(2,1)S(1)}, bf16[4,128,128]{2,1,0:T(8,128)(2,1)S(1)}, u32[]{:S(2)}, u32[]{:S(2)}) collective-permute-start(bf16[4,128,128]{2,1,0:T(8,128)(2,1)S(1)} %all-to-all-done.7.refs_0_), channel_id=1, source_target_pairs={{0,4},{4,0},{8,12},{12,8},{16,20},{20,16},{24,28},{28,24},{1,5},{5... | collective-permute-start | bytes 393224 | tf_op jit(solution)/shard_map/ppermute | solution.py:39
  137.5 5.3 %copy-start.1 = (bf16[4,128,128]{2,1,0:T(8,128)(2,1)}, bf16[4,128,128]{2,1,0:T(8,128)(2,1)S(1)}, u32[]{:S(2)}) copy-start(bf16[4,128,128]{2,1,0:T(8,128)(2,1)S(1)} %all-to-all-done.3.refs_0_) | copy-start | bytes 393220
  137.5 5.3 %collective-permute-start.2 = (bf16[4,128,128]{2,1,0:T(8,128)(2,1)S(1)}, bf16[4,128,128]{2,1,0:T(8,128)(2,1)S(1)}, u32[]{:S(2)}, u32[]{:S(2)}) collective-permute-start(bf16[4,128,128]{2,1,0:T(8,128)(2,1)S(1)} %all-to-all-done.3.refs_0_), channel_id=1, source_target_pairs={{0,4},{4,0},{8,12},{12,8},{16,20},{20,16},{24,28},{28,24},{1,5},{5... | collective-permute-start | bytes 393224 | tf_op jit(solution)/shard_map/ppermute | solution.py:39
  138.3 0.7 copy-start.4
  142.8 0.6 copy-start.5

commit v3 on v2

v3 whole, which is shorter than its diff:
```python
import functools
import math

import jax
import jax.numpy as jnp
from jax import lax
from jax.experimental import pallas as pl
from jax.experimental.pallas import tpu as pltpu
from jax.sharding import PartitionSpec as P

QH = 64
KVH = 8
HD = 128

NEG_BIG = -1e30
LANES = 128
STAT_ROWS = 8
VMEM_GRANT = 51 << 20
NT = (((1,), (1,)), ((), ()))

OUTPUT_SCALE = 2.0**12
MIXED_SCALE = 2.0**-3


def vmem_spec():
    return pl.BlockSpec(memory_space=pltpu.VMEM)


def smem_spec():
    return pl.BlockSpec(memory_space=pltpu.SMEM)


def hbm_spec():
    return pl.BlockSpec(memory_space=pl.ANY)


def swap(array, axis, mask):
    size = lax.axis_size(axis)
    return lax.ppermute(array, axis, [(i, i ^ mask) for i in range(size)])


def within_parity(array):
    size = lax.axis_size("seq")
    groups = [list(range(first, size, 2)) for first in range(2)]
    return lax.all_to_all(array, "seq", 0, 0, axis_index_groups=groups)


def spread(copies):
    if copies.shape[0] == lax.axis_size("seq"):
        return [lax.all_to_all(copies, "seq", 0, 0)]
    same = within_parity(copies)
    return [same, swap(same, "seq", 1)]


def project_kernel(me_ref, hidden_ref, q_hbm, k_hbm, v_hbm, *refs, chunks, blocks, pieces):
    outs = refs[: 2 * chunks]
    q_all, k_all, v_all, total, sems = refs[2 * chunks :]
    tokens, depth = hidden_ref.shape
    odd = lax.rem(me_ref[0], 2) == 1
    rows = depth // pieces
    copies = [
        pltpu.make_async_copy(
            q_hbm.at[pl.ds(i * rows, rows), :], q_all.at[pl.ds(i * rows, rows), :], sems.at[i]
        )
        for i in range(pieces)
    ]
    copies.append(pltpu.make_async_copy(k_hbm, k_all, sems.at[pieces]))
    copies.append(pltpu.make_async_copy(v_hbm, v_all, sems.at[pieces + 1]))
    for copy in copies:
        copy.start()

    def deal(product, chunk, kind):
        block = blocks[kind]
        first = kind * blocks[0]
        parts = [
            product[e * block : (e + 1) * block, c * LANES : (c + 1) * LANES]
            for c in range(product.shape[1] // LANES)
            for e in range(tokens // block)
        ]
        keep_ref, send_ref = outs[2 * chunk : 2 * chunk + 2]
        for i, (even_part, odd_part) in enumerate(zip(parts[0::2], parts[1::2])):
            keep_ref[i, first : first + block, :] = jnp.where(odd, odd_part, even_part)
            send_ref[i, first : first + block, :] = jnp.where(odd, even_part, odd_part)

    columns = q_all.shape[1] // chunks
    for i in range(pieces):
        copies[i].wait()
        h = hidden_ref[:, i * rows : (i + 1) * rows]
        for j in range(chunks):
            w = q_all[i * rows : (i + 1) * rows, j * columns : (j + 1) * columns]
            product = jnp.dot(h, w, preferred_element_type=jnp.float32)
            if i > 0:
                product = product + total[j]
            if i < pieces - 1:
                total[j] = product
            else:
                deal(product, j, 0)
    copies[pieces].wait()
    copies[pieces + 1].wait()
    both = [
        jnp.dot(hidden_ref[...], w_all[...], preferred_element_type=jnp.float32)
        for w_all in (k_all, v_all)
    ]
    deal(jnp.concatenate(both, axis=1), chunks - 1, 1)


def project(me, hidden, query_weight, key_weight, value_weight, chunks, count):
    tokens, depth = hidden.shape
    wide, narrow = query_weight.shape[1], key_weight.shape[1]
    pieces = max(1, depth // 256)
    blocks = (wide // chunks // LANES * tokens // count, 2 * narrow // LANES * tokens // count)
    shapes = []
    for j in range(chunks):
        rows = blocks[0] + (blocks[1] if j == chunks - 1 else 0)
        shapes += [jax.ShapeDtypeStruct((count // 2, rows, LANES), jnp.float32)] * 2
    return pl.pallas_call(
        functools.partial(project_kernel, chunks=chunks, blocks=blocks, pieces=pieces),
        out_shape=shapes,
        in_specs=[smem_spec(), vmem_spec()] + [hbm_spec()] * 3,
        out_specs=[vmem_spec()] * len(shapes),
        scratch_shapes=[
            pltpu.VMEM((depth, wide), jnp.bfloat16),
            pltpu.VMEM((depth, narrow), jnp.bfloat16),
            pltpu.VMEM((depth, narrow), jnp.bfloat16),
            pltpu.VMEM((chunks, tokens, wide // chunks), jnp.float32),
            pltpu.SemaphoreType.DMA((pieces + 2,)),
        ],
        compiler_params=pltpu.CompilerParams(vmem_limit_bytes=VMEM_GRANT),
        cost_estimate=pl.CostEstimate(
            flops=2 * tokens * depth * (wide + 2 * narrow),
            bytes_accessed=2 * depth * (wide + 2 * narrow),
            transcendentals=0,
        ),
    )(me, hidden, query_weight, key_weight, value_weight)


def collect_kernel(part_ref, copies_ref):
    total = part_ref[0]
    for k in range(1, part_ref.shape[0]):
        total = total + part_ref[k]
    total = total.astype(jnp.bfloat16)
    for k in range(copies_ref.shape[0]):
        copies_ref[k] = total


def collect(parts, copies):
    return pl.pallas_call(
        collect_kernel,
        out_shape=jax.ShapeDtypeStruct((copies,) + parts.shape[1:], jnp.bfloat16),
        in_specs=[vmem_spec()],
        out_specs=vmem_spec(),
    )(parts)


def attention_kernel(len_ref, me_ref, *refs, sources, band, step, block, head):
    q_refs, refs = refs[:sources], refs[sources:]
    k_hbm, v_hbm, o_ref, k_ref, v_ref, sems = refs[:6]
    s_bufs, m_bufs = refs[6:8], refs[8:10]
    shift, acc, lse_all = refs[10:]
    half = q_refs[0].shape[0]
    rows = sources * half * block
    bands = rows // band
    share = band // block
    scale = math.log2(math.e) / math.sqrt(HD)
    piece = math.gcd(step, 1024)
    tiles = piece // LANES
    odd = lax.rem(me_ref[0], 2)
    lanes = slice(head * HD, (head + 1) * HD)

    def owner_of(k):
        return k if sources == 1 else 2 * (k % half) + (odd if k < half else 1 - odd)

    length = len_ref[0]
    full = length // step
    rest = length - full * step

    def copy_in(source, target, which, i):
        where = pl.ds(pl.multiple_of(i * step, step), step)
        return pltpu.make_async_copy(
            source.at[where, :], target.at[where, :], sems.at[which, i]
        )

    def keys_in(i):
        return copy_in(k_hbm, k_ref, 0, i)

    def values_in(i):
        return copy_in(v_hbm, v_ref, 1, i)

    needed = (length + step - 1) // step

    def start_keys(i, carry):
        keys_in(i).start()
        return carry

    def start_values(i, carry):
        values_in(i).start()
        return carry

    lax.fori_loop(0, needed, start_keys, 0)
    lax.fori_loop(0, needed, start_values, 0)

    def score(r, i, first, masked):
        source = q_refs[r * share // half]
        at = r * share % half
        q = source[at : at + share, :block, :].reshape(band, HD)
        keys = k_ref[pl.ds(pl.multiple_of(i * step + first, piece), piece), lanes]
        s = lax.dot_general(q, keys, NT, preferred_element_type=jnp.float32)
        if masked:
            column = first + lax.broadcasted_iota(jnp.int32, (band, piece), 1)
            s = jnp.where(column < rest, s, NEG_BIG)
        s_bufs[r % 2][i, :, first : first + piece] = s
        tops = [s[:, c * LANES : (c + 1) * LANES] for c in range(tiles)]
        while len(tops) > 1:
            tops = [jnp.maximum(a, b) for a, b in zip(tops[0::2], tops[1::2])]
        m_bufs[r % 2][...] = jnp.maximum(m_bufs[r % 2][...], tops[0])

    def weigh(r, i, first):
        s = s_bufs[r % 2][i, :, first : first + piece]
        low = shift[...]
        weights = jnp.concatenate(
            [
                jnp.exp2(s[:, c * LANES : (c + 1) * LANES] * scale - low).astype(jnp.bfloat16)
                for c in range(tiles)
            ],
            axis=1,
        )
        values = v_ref[pl.ds(pl.multiple_of(i * step + first, piece), piece), lanes]
        wide = jnp.concatenate([values, jnp.ones((piece, LANES), jnp.bfloat16)], axis=1)
        acc[...] += jnp.dot(weights, wide, preferred_element_type=jnp.float32)

    for r in range(bands + 1):
        scores, weighs = r < bands, r > 0
        if scores:
            m_bufs[r % 2][...] = jnp.full((band, LANES), -3e38, jnp.float32)
        if weighs:
            top = jnp.max(m_bufs[(r - 1) % 2][...], axis=1, keepdims=True)
            shift[...] = jnp.broadcast_to(top * scale, (band, LANES))
            acc[...] = jnp.zeros(acc.shape, jnp.float32)

        def both(i, masked):
            if r == 0:
                keys_in(i).wait()
            if r == 1:
                values_in(i).wait()
            for first in range(0, step, piece):
                if weighs:
                    weigh(r - 1, i, first)
                if scores:
                    score(r, i, first, masked)

        def body(i, carry):
            both(i, False)
            return carry

        lax.fori_loop(0, full, body, 0)

        @pl.when(rest > 0)
        def _():
            both(full, True)

        if weighs:
            totals = acc[:, LANES:]
            mean = acc[:, :LANES] / totals * OUTPUT_SCALE
            for e in range(share):
                k = (r - 1) * share + e
                o_ref[owner_of(k), :block, :] = mean[e * block : (e + 1) * block, :]
            lse_all[(r - 1) * band : r * band, :] = shift[...] + jnp.log2(totals)

    per = LANES // block
    row = lax.broadcasted_iota(jnp.int32, (STAT_ROWS, LANES), 0)
    for g in range(rows // LANES):
        level = lse_all[g * LANES : (g + 1) * LANES, :].T[:STAT_ROWS, :]
        exponent = jnp.floor(jnp.log2(jnp.maximum(jnp.abs(level), 1e-30)))
        exponent = jnp.minimum(exponent, 120.0)
        rest_of = level * jnp.exp2(-exponent)
        first = jnp.floor(rest_of * 2.0**9 + 0.5)
        rest_of = rest_of - first * 2.0**-9
        second = jnp.floor(rest_of * 2.0**20 + 0.5)
        third = (rest_of - second * 2.0**-20) * 2.0**31
        stats = jnp.where(row == 0, exponent, jnp.where(row == 1, first, second))
        stats = jnp.where(row >= 3, third, stats)
        for e in range(per):
            k = g * per + e
            o_ref[owner_of(k), block:, :] = stats


def attention(queries, block, keys, values, length, me, head):
    sources = len(queries)
    count = sources * queries[0].shape[0]
    rows, slots = count * block, keys.shape[0]
    band = math.gcd(rows // 2, 256)
    step = math.gcd(slots, 2048)
    return pl.pallas_call(
        functools.partial(
            attention_kernel, sources=sources, band=band, step=step, block=block, head=head
        ),
        out_shape=jax.ShapeDtypeStruct((count, block + STAT_ROWS, HD), jnp.float32),
        in_specs=[smem_spec()] * 2 + [vmem_spec()] * sources + [hbm_spec()] * 2,
        out_specs=vmem_spec(),
        scratch_shapes=[
            pltpu.VMEM(keys.shape, keys.dtype),
            pltpu.VMEM(values.shape, values.dtype),
            pltpu.SemaphoreType.DMA((2, slots // step)),
            pltpu.VMEM((slots // step, band, step), jnp.float32),
            pltpu.VMEM((slots // step, band, step), jnp.float32),
            pltpu.VMEM((band, LANES), jnp.float32),
            pltpu.VMEM((band, LANES), jnp.float32),
            pltpu.VMEM((band, LANES), jnp.float32),
            pltpu.VMEM((band, 2 * LANES), jnp.float32),
            pltpu.VMEM((rows, LANES), jnp.float32),
        ],
        compiler_params=pltpu.CompilerParams(vmem_limit_bytes=VMEM_GRANT),
        cost_estimate=pl.CostEstimate(
            flops=8 * rows * slots * HD,
            bytes_accessed=4 * slots * HD,
            transcendentals=rows * slots,
        ),
    )(length, me, *queries, keys, values)


def merge_kernel(me_ref, part_ref, q_ref, last_ref, copies_ref, turned, kv_all, *, block, tokens, head):
    count = part_ref.shape[0]
    per = LANES // block
    kv_block = last_ref.shape[1] - block
    scale = math.log2(math.e) / math.sqrt(HD)

    for k in range(count):
        rows = last_ref[k, block:, :].astype(jnp.float32)
        kv_all[k * kv_block : (k + 1) * kv_block, :] = rows
    half = kv_all.shape[0] // 2
    keys = kv_all[head * tokens : (head + 1) * tokens, :].astype(jnp.bfloat16)
    values = kv_all[half + head * tokens : half + (head + 1) * tokens, :].astype(jnp.bfloat16)

    s = lax.dot_general(q_ref[0, :block, :], keys, NT, preferred_element_type=jnp.float32) * scale
    token = lax.rem(me_ref[0] * block, tokens) + lax.broadcasted_iota(jnp.int32, s.shape, 0)
    visible = lax.broadcasted_iota(jnp.int32, s.shape, 1) <= token
    s = jnp.where(visible, s, NEG_BIG)
    new_top = jnp.max(s, axis=1, keepdims=True)
    weights = jnp.where(visible, jnp.exp2(s - new_top), 0.0).astype(jnp.bfloat16)
    new_total = jnp.sum(weights.astype(jnp.float32), axis=1, keepdims=True)
    new_out = jnp.dot(weights, values, preferred_element_type=jnp.float32)

    place = lax.rem(me_ref[0] // 2, per)
    pieces = part_ref[:, block : block + 4, :]
    level = pieces[:, 1, :] * 2.0**-9 + pieces[:, 2, :] * 2.0**-20 + pieces[:, 3, :] * 2.0**-31
    turned[...] = (level * jnp.exp2(pieces[:, 0, :])).T
    levels = turned[pl.ds(pl.multiple_of(place * block, block), block), :]
    joint = jnp.maximum(new_top, jnp.max(levels, axis=1, keepdims=True))
    factors = jnp.exp2(levels - joint)
    new_scale = jnp.exp2(new_top - joint)
    whole_out = new_out * new_scale
    whole_total = new_total * new_scale + jnp.sum(factors, axis=1, keepdims=True)
    scaled = factors * (1.0 / OUTPUT_SCALE)
    for k in range(count):
        whole_out = whole_out + part_ref[k, :block, :] * scaled[:, k : k + 1]
    attended = (whole_out / whole_total).astype(jnp.bfloat16)
    for k in range(count):
        copies_ref[k] = attended


def merge(me, parts, mine, last, block, tokens, head):
    count = parts.shape[0]
    kv_rows = count * (last.shape[1] - block)
    return pl.pallas_call(
        functools.partial(merge_kernel, block=block, tokens=tokens, head=head),
        out_shape=jax.ShapeDtypeStruct((count, block, HD), jnp.bfloat16),
        in_specs=[smem_spec()] + [vmem_spec()] * 3,
        out_specs=vmem_spec(),
        scratch_shapes=[
            pltpu.VMEM((LANES, count), jnp.float32),
            pltpu.VMEM((kv_rows, HD), jnp.float32),
        ],
    )(me, parts, mine, last)


def output_kernel(place_ref, w_hbm, a_ref, *refs, tokens, groups, chunk, has_before, last):
    before = refs[0] if has_before else None
    outs, (w_all, total, sems) = refs[int(has_before) : -3], refs[-3:]
    copies = []
    for g in range(groups):
        copies.append(
            pltpu.make_async_copy(
                w_hbm.at[pl.ds((chunk * groups + g) * HD, HD), :],
                w_all.at[pl.ds(g * HD, HD), :],
                sems.at[g],
            )
        )
        copies[-1].start()
    per = a_ref.shape[0] // groups
    pieces = [a_ref[g * per : (g + 1) * per].reshape(tokens, HD) for g in range(groups)]
    product = before[...] if has_before else None
    for g in range(0, groups, 2):
        copies[g].wait()
        copies[g + 1].wait()
        term = jnp.dot(
            jnp.concatenate(pieces[g : g + 2], axis=1),
            w_all[g * HD : (g + 2) * HD, :],
            preferred_element_type=jnp.float32,
        )
        product = term if product is None else product + term
    if not last:
        outs[0][...] = product
        return
    total[...] = product
    keep_ref, send_ref = outs
    share = keep_ref.shape[1]
    odd = lax.rem(place_ref[0], 2)
    for i in range(keep_ref.shape[0]):
        for ref, parity in ((keep_ref, odd), (send_ref, 1 - odd)):
            start = pl.multiple_of((2 * i + parity) * share, share)
            ref[i] = total[pl.ds(start, share), :]


def output_part(place, weight, attended, tokens, before, chunk, heads, last):
    groups = QH // KVH
    width = weight.shape[1]
    has_before = before is not None
    shapes = [jax.ShapeDtypeStruct((tokens, width), jnp.float32)]
    if last:
        shapes = [jax.ShapeDtypeStruct((heads // 2, tokens // heads, width), jnp.float32)] * 2
    return pl.pallas_call(
        functools.partial(
            output_kernel,
            tokens=tokens,
            groups=groups,
            chunk=chunk,
            has_before=has_before,
            last=last,
        ),
        out_shape=shapes,
        in_specs=[smem_spec(), hbm_spec()] + [vmem_spec()] * (1 + int(has_before)),
        out_specs=[vmem_spec()] * len(shapes),
        scratch_shapes=[
            pltpu.VMEM((groups * HD, width), jnp.bfloat16),
            pltpu.VMEM((tokens, width), jnp.float32),
            pltpu.SemaphoreType.DMA((groups,)),
        ],
        compiler_params=pltpu.CompilerParams(vmem_limit_bytes=VMEM_GRANT),
        cost_estimate=pl.CostEstimate(
            flops=2 * tokens * groups * HD * width,
            bytes_accessed=2 * groups * HD * width,
            transcendentals=0,
        ),
    )(place, weight, attended, *([before] if has_before else []))


def shards(
    hidden,
    query_weight,
    key_weight,
    value_weight,
    output_weight,
    cache_keys,
    cache_values,
    cache_lens,
):
    tokens = hidden.shape[0]
    count = lax.axis_size("seq")
    heads = lax.axis_size("head")
    kv_local = cache_keys.shape[1] // HD
    block = (QH // KVH) * tokens // count
    me = lax.axis_index("seq").reshape(1)
    place = lax.axis_index("head").reshape(1)

    halves = project(me, hidden, query_weight, key_weight, value_weight, kv_local, count)
    mine = []
    for j in range(kv_local):
        keep, send = halves[2 * j : 2 * j + 2]
        parts = within_parity(keep + swap(send, "seq", 1))
        mine.append(collect(parts, count if j == kv_local - 1 else count // 2))
    queries = [spread(copies) for copies in mine]

    mixed = None
    for j in range(kv_local):
        parts = attention(queries[j], block, cache_keys, cache_values, cache_lens, me, j)
        parts = lax.all_to_all(parts.astype(jnp.float16), "seq", 0, 0).astype(jnp.float32)
        copies = merge(me, parts, mine[j], queries[-1][0], block, tokens, j)
        last = j == kv_local - 1
        result = output_part(
            place, output_weight, spread(copies)[0], tokens, mixed, j, heads, last
        )
        mixed = result if last else result[0]

    keep, send = mixed
    mixed = keep + swap(send, "head", 1)
    mask = 2
    while mask < heads:
        bit = place[0] // mask % 2
        pairs = mixed.reshape((-1, 2) + mixed.shape[1:])
        keep = lax.dynamic_index_in_dim(pairs, bit, 1, False)
        send = lax.dynamic_index_in_dim(pairs, 1 - bit, 1, False) * MIXED_SCALE
        received = swap(send.astype(jnp.float16), "head", mask).astype(jnp.float32)
        mixed = keep + received * (1.0 / MIXED_SCALE)
        mask *= 2
    return mixed[0].astype(jnp.bfloat16)


def solution(mesh):
    placed = (
        P(None, "seq"),
        P("seq", "head"),
        P("seq", "head"),
        P("seq", "head"),
        P("head", "seq"),
        P("seq", "head"),
        P("seq", "head"),
        P("seq"),
    )
    return jax.shard_map(
        shards, mesh=mesh, in_specs=placed, out_specs=P("head", "seq"), check_vma=False
    )
```

time: 160 us -> 142 us (0.89)
  Pallas kernels: 41.4 us -> 32.2 us
  blocking collectives: 8.63 us -> 0 us
  waiting for transfers between devices: 38.1 us -> 44.5 us
  local copies, waits for them, and re-layouts: 9.84 us -> 4.5 us
  other arithmetic: 9.64 us -> 5.52 us
  starting transfers between devices: 49.4 us -> 53 us
    all_to_all x6 -> x3, waiting for transfers between devices: 30.6 us -> 18.4 us  [within_parity(): return lax.all_to_all(array, 'seq', 0, 0, axis_index_groups=groups)]
    all_to_all x0 -> x3, starting transfers between devices: none -> 11.3 us  [spread(): return [lax.all_to_all(copies, 'seq', 0, 0)]]
    all_to_all x0 -> x3, waiting for transfers between devices: none -> 11.1 us  [spread(): return [lax.all_to_all(copies, 'seq', 0, 0)]]
    all_to_all x6 -> x3, starting transfers between devices: 22.4 us -> 11.9 us  [within_parity(): return lax.all_to_all(array, 'seq', 0, 0, axis_index_groups=groups)]
    all_to_all x1 -> x0, blocking collectives: 8.63 us -> none  [shards(): lax.all_to_all(mixed.astype(jnp.float16), 'head', 0, 0).astype(jnp.float32)]
    broadcast_in_dim x6 -> x0, local copies, waits for them, and re-layouts: 5.93 us -> none  [the longest x4 4.24 us: spread(): same = within_parity(jnp.broadcast_to(block[None], (half,) + block.shape))]
    ppermute x6 -> x5, waiting for transfers between devices: 5.09 us -> 10.5 us  [swap(): return lax.ppermute(array, axis, [(i, i ^ mask) for i in range(size)])]
    pallas_call x6 -> x7, Pallas kernels: 33.6 us -> 28.5 us  [the longest x2 16.3 us: attention(): pl.pallas_call(functools.partial(attention_kernel, sources=sources, band=...]
  transfers between devices with their start and end apart: 14 -> 13, of which waited for: 9 -> 10; matrix products, arithmetic and copies ran while one was open for 7% -> 3% of each run, Pallas kernels for 21% -> 20%
where the time goes in v3:
time: 142 us; the launch traced here: 140 us
  starting transfers between devices  53 us (37%)
  waiting for transfers between devices  44.5 us (31%)
  Pallas kernels  32.2 us (23%)
  other arithmetic  5.52 us (4%)
  local copies, waits for them, and re-layouts  4.5 us (3%)
    all_to_all x2, starting transfers between devices, shards(): lax.all_to_all(parts.astype(jnp.float16), 'seq', 0, 0).astype(jnp.float32)  22 us
    all_to_all x3, waiting for transfers between devices, within_parity(): return lax.all_to_all(array, 'seq', 0, 0, axis_index_groups=groups)  18.4 us
    pallas_call x2, Pallas kernels, attention(): pl.pallas_call(functools.partial(attention_kernel, sources=sources, band=...  16.3 us
    all_to_all x3, starting transfers between devices, within_parity(): return lax.all_to_all(array, 'seq', 0, 0, axis_index_groups=groups)  11.9 us
    all_to_all x3, starting transfers between devices, spread(): return [lax.all_to_all(copies, 'seq', 0, 0)]  11.3 us
    all_to_all x3, waiting for transfers between devices, spread(): return [lax.all_to_all(copies, 'seq', 0, 0)]  11.1 us
    ppermute x5, waiting for transfers between devices, swap(): return lax.ppermute(array, axis, [(i, i ^ mask) for i in range(size)])  10.5 us
    ppermute x5, starting transfers between devices, swap(): return lax.ppermute(array, axis, [(i, i ^ mask) for i in range(size)])  7.76 us
  transfers between devices with their start and end apart: 13, of which 10 were waited for; matrix products, arithmetic and copies ran while one was open for 3% of the time, Pallas kernels for 20%

profile of v3, /device:TPU:0, one launch (start us, length us, event | category | flops | bytes accessed | tf_op | source)
XLA Modules:
  0.0 140.5 jit_solution(14075437058283419365)
XLA Ops:
  0.0 1.0 copy-done.1
  1.0 1.0 copy-done.2
  2.1 0.9 copy-done.3
  3.0 2.8 %shard_map.82 = (f32[4,128,128]{2,1,0:T(8,128)S(1)}, f32[4,128,128]{2,1,0:T(8,128)S(1)}, f32[4,192,128]{2,1,0:T(8,128)S(1)}, f32[4,192,128]{2,1,0:T(8,128)S(1)}) custom-call(s32[1]{0:T(128)} %bitcast.1.me_ref, bf16[128,1024]{1,0:T(8,128)(2,1)S(1)} %copy-done.3, bf16[1024,2048]{1,0:T(8,128)(2,1)} %q_hbm.1, bf16[1024,256]{1,0:T(8,128)(2,1)S(1)} %copy-done.1, ...), custom_call_target="tpu_custom_call" | custom-call | flops 671088640 | bytes 5242880 | tf_op jit(solution)/shard_map/pallas_call | solution.py:116
  5.9 3.0 %collective-permute-start.1 = (f32[4,128,128]{2,1,0:T(8,128)S(1)}, f32[4,128,128]{2,1,0:T(8,128)S(1)}, u32[]{:S(2)}, u32[]{:S(2)}) collective-permute-start(f32[4,128,128]{2,1,0:T(8,128)S(1)} %get-tuple-element.14), channel_id=1, source_target_pairs={{0,4},{4,0},{8,12},{12,8},{16,20},{20,16},{24,28},{28,24},{1,5},{5... | collective-permute-start | bytes 786440 | tf_op jit(solution)/shard_map/ppermute | solution.py:39
  8.9 6.3 %collective-permute-done.1 = f32[4,128,128]{2,1,0:T(8,128)S(1)} collective-permute-done((f32[4,128,128]{2,1,0:T(8,128)S(1)}, f32[4,128,128]{2,1,0:T(8,128)S(1)}, u32[]{:S(2)}, u32[]{:S(2)}) %collective-permute-start.1) | collective-permute-done | bytes 262176 | tf_op jit(solution)/shard_map/ppermute | solution.py:39
  15.2 0.7 add.26
  15.9 5.1 %all-to-all-start.4 = ((f32[4,128,128]{2,1,0:T(8,128)}), f32[4,128,128]{2,1,0:T(8,128)S(1)}, u32[]{:S(2)}, u32[]{:S(2)}) async-start(f32[4,128,128]{2,1,0:T(8,128)} %add.26), calls=%async_computation.4 | async-start | bytes 524288 | tf_op jit(solution)/shard_map/all_to_all | solution.py:45
  21.1 1.5 %collective-permute-start = (f32[4,192,128]{2,1,0:T(8,128)S(1)}, f32[4,192,128]{2,1,0:T(8,128)S(1)}, u32[]{:S(2)}, u32[]{:S(2)}) collective-permute-start(f32[4,192,128]{2,1,0:T(8,128)S(1)} %get-tuple-element.12), channel_id=1, source_target_pairs={{0,4},{4,0},{8,12},{12,8},{16,20},{20,16},{24,28},{28,24},{1,5},{5... | collective-permute-start | bytes 1179656 | tf_op jit(solution)/shard_map/ppermute | solution.py:39
  22.6 6.7 %all-to-all-done.4.part_ref = f32[4,128,128]{2,1,0:T(8,128)S(1)} async-done(((f32[4,128,128]{2,1,0:T(8,128)}), f32[4,128,128]{2,1,0:T(8,128)S(1)}, u32[]{:S(2)}, u32[]{:S(2)}) %all-to-all-start.4) | async-done | bytes 262176 | tf_op jit(solution)/shard_map/all_to_all | solution.py:45
  29.2 0.7 copy-done.5
  30.0 1.6 %shard_map.86.q_ref = bf16[4,128,128]{2,1,0:T(8,128)(2,1)} custom-call(f32[4,128,128]{2,1,0:T(8,128)} %copy-done.5), custom_call_target="tpu_custom_call" | custom-call | tf_op jit(solution)/shard_map/pallas_call | solution.py:147
  31.6 3.3 %all-to-all-start.5 = ((bf16[4,128,128]{2,1,0:T(8,128)(2,1)}), bf16[4,128,128]{2,1,0:T(8,128)(2,1)S(1)}, u32[]{:S(2)}, u32[]{:S(2)}) async-start(bf16[4,128,128]{2,1,0:T(8,128)(2,1)} %shard_map.86.q_ref), calls=%async_computation.5 | async-start | bytes 262144 | tf_op jit(solution)/shard_map/all_to_all | solution.py:45
  34.9 0.0 collective-permute-done
  34.9 0.8 add.25
  35.7 5.1 %all-to-all-done.5.refs_0_ = bf16[4,128,128]{2,1,0:T(8,128)(2,1)S(1)} async-done(((bf16[4,128,128]{2,1,0:T(8,128)(2,1)}), bf16[4,128,128]{2,1,0:T(8,128)(2,1)S(1)}, u32[]{:S(2)}, u32[]{:S(2)}) %all-to-all-start.5) | async-done | bytes 131104 | tf_op jit(solution)/shard_map/all_to_all | solution.py:45
  40.8 3.5 %all-to-all-start = ((f32[4,192,128]{2,1,0:T(8,128)}), f32[4,192,128]{2,1,0:T(8,128)S(1)}, u32[]{:S(2)}, u32[]{:S(2)}) async-start(f32[4,192,128]{2,1,0:T(8,128)} %add.25), calls=%async_computation | async-start | bytes 786432 | tf_op jit(solution)/shard_map/all_to_all | solution.py:45
  44.3 1.6 %collective-permute-start.2 = (bf16[4,128,128]{2,1,0:T(8,128)(2,1)S(1)}, bf16[4,128,128]{2,1,0:T(8,128)(2,1)S(1)}, u32[]{:S(2)}, u32[]{:S(2)}) collective-permute-start(bf16[4,128,128]{2,1,0:T(8,128)(2,1)S(1)} %all-to-all-done.5.refs_0_), channel_id=1, source_target_pairs={{0,4},{4,0},{8,12},{12,8},{16,20},{20,16},{24,28},{28,24},{1,5},{5... | collective-permute-start | bytes 393224 | tf_op jit(solution)/shard_map/ppermute | solution.py:39
  46.5 6.6 %all-to-all-done.part_ref = f32[4,192,128]{2,1,0:T(8,128)S(1)} async-done(((f32[4,192,128]{2,1,0:T(8,128)}), f32[4,192,128]{2,1,0:T(8,128)S(1)}, u32[]{:S(2)}, u32[]{:S(2)}) %all-to-all-start) | async-done | bytes 393248 | tf_op jit(solution)/shard_map/all_to_all | solution.py:45
  53.1 0.8 copy-done.4
  53.9 1.8 %shard_map.83.q_ref = bf16[8,192,128]{2,1,0:T(8,128)(2,1)} custom-call(f32[4,192,128]{2,1,0:T(8,128)} %copy-done.4), custom_call_target="tpu_custom_call" | custom-call | tf_op jit(solution)/shard_map/pallas_call | solution.py:147
  55.6 3.7 %all-to-all-start.1 = ((bf16[8,192,128]{2,1,0:T(8,128)(2,1)}), bf16[8,192,128]{2,1,0:T(8,128)(2,1)S(1)}, u32[]{:S(2)}, u32[]{:S(2)}) async-start(bf16[8,192,128]{2,1,0:T(8,128)(2,1)} %shard_map.83.q_ref), calls=%async_computation.1 | async-start | bytes 786432 | tf_op jit(solution)/shard_map/all_to_all | solution.py:50
  59.3 0.0 collective-permute-done.2.refs_1_
  59.3 8.1 %shard_map.87 = f32[8,136,128]{2,1,0:T(8,128)S(1)} custom-call(s32[1]{0:T(128)S(6)} %copy.9.len_ref, s32[1]{0:T(128)} %bitcast.1.me_ref, bf16[4,128,128]{2,1,0:T(8,128)(2,1)S(1)} %all-to-all-done.5.refs_0_, bf16[4,128,128]{2,1,0:T(8,128)(2,1)S(1)} %collective-permute-done.2.refs_1_, bf16[8192,256]{1,0:T(8,128)(2,1)} %refs_2_.3, bf16[8192,256]{1,0:T(8,128)(2,1)} %refs_3_.1), custom_call_target="tpu_custom_call" | custom-call | flops 8589934592 | bytes 4194304 | tf_op jit(solution)/shard_map/pallas_call | solution.py:293
  67.4 0.8 convert_element_type.28
  68.2 0.4 all-to-all-done.1.refs_0_.last_ref
  68.5 10.8 %all-to-all-start.6 = ((f16[8,136,128]{2,1,0:T(8,128)(2,1)}), f16[8,136,128]{2,1,0:T(8,128)(2,1)S(1)}, u32[]{:S(2)}, u32[]{:S(2)}) async-start(f16[8,136,128]{2,1,0:T(8,128)(2,1)} %convert_element_type.28), calls=%async_computation.6 | async-start | bytes 557056 | tf_op jit(solution)/shard_map/all_to_all | solution.py:476
  79.3 8.2 %shard_map.84 = f32[8,136,128]{2,1,0:T(8,128)S(1)} custom-call(s32[1]{0:T(128)S(6)} %copy.9.len_ref, s32[1]{0:T(128)} %bitcast.1.me_ref, bf16[8,192,128]{2,1,0:T(8,128)(2,1)S(1)} %all-to-all-done.1.refs_0_.last_ref, bf16[8192,256]{1,0:T(8,128)(2,1)} %refs_2_.3, bf16[8192,256]{1,0:T(8,128)(2,1)} %refs_3_.1), custom_call_target="tpu_custom_call" | custom-call | flops 8589934592 | bytes 4194304 | tf_op jit(solution)/shard_map/pallas_call | solution.py:293
  87.6 0.0 copy-done
  87.6 0.8 convert_element_type.26
  88.3 0.0 all-to-all-done.6
  88.3 11.2 %all-to-all-start.2 = ((f16[8,136,128]{2,1,0:T(8,128)(2,1)}), f16[8,136,128]{2,1,0:T(8,128)(2,1)S(1)}, u32[]{:S(2)}, u32[]{:S(2)}) async-start(f16[8,136,128]{2,1,0:T(8,128)(2,1)} %convert_element_type.26), calls=%async_computation.2 | async-start | bytes 557056 | tf_op jit(solution)/shard_map/all_to_all | solution.py:476
  99.5 0.9 convert_element_type.29.part_ref
  100.4 3.0 %shard_map.88 = bf16[8,128,128]{2,1,0:T(8,128)(2,1)} custom-call(s32[1]{0:T(128)} %bitcast.1.me_ref, f32[8,136,128]{2,1,0:T(8,128)} %convert_element_type.29.part_ref, bf16[4,128,128]{2,1,0:T(8,128)(2,1)} %shard_map.86.q_ref, bf16[8,192,128]{2,1,0:T(8,128)(2,1)} %copy-done), custom_call_target="tpu_custom_call" | custom-call | tf_op jit(solution)/shard_map/pallas_call | solution.py:364
  103.4 4.5 %all-to-all-done.2 = f16[8,136,128]{2,1,0:T(8,128)(2,1)S(1)} async-done(((f16[8,136,128]{2,1,0:T(8,128)(2,1)}), f16[8,136,128]{2,1,0:T(8,128)(2,1)S(1)}, u32[]{:S(2)}, u32[]{:S(2)}) %all-to-all-start.2) | async-done | bytes 278560 | tf_op jit(solution)/shard_map/all_to_all | solution.py:476
  107.9 3.4 %all-to-all-start.7 = ((bf16[8,128,128]{2,1,0:T(8,128)(2,1)}), bf16[8,128,128]{2,1,0:T(8,128)(2,1)S(1)}, u32[]{:S(2)}, u32[]{:S(2)}) async-start(bf16[8,128,128]{2,1,0:T(8,128)(2,1)} %shard_map.88), calls=%async_computation.7 | async-start | bytes 524288 | tf_op jit(solution)/shard_map/all_to_all | solution.py:50
  111.3 0.9 convert_element_type.27.part_ref
  112.2 3.0 %shard_map.85 = bf16[8,128,128]{2,1,0:T(8,128)(2,1)} custom-call(s32[1]{0:T(128)} %bitcast.1.me_ref, f32[8,136,128]{2,1,0:T(8,128)} %convert_element_type.27.part_ref, bf16[8,192,128]{2,1,0:T(8,128)(2,1)} %shard_map.83.q_ref, bf16[8,192,128]{2,1,0:T(8,128)(2,1)} %copy-done), custom_call_target="tpu_custom_call" | custom-call | tf_op jit(solution)/shard_map/pallas_call | solution.py:364
  115.2 4.3 %all-to-all-done.7.a_ref = bf16[8,128,128]{2,1,0:T(8,128)(2,1)S(1)} async-done(((bf16[8,128,128]{2,1,0:T(8,128)(2,1)}), bf16[8,128,128]{2,1,0:T(8,128)(2,1)S(1)}, u32[]{:S(2)}, u32[]{:S(2)}) %all-to-all-start.7) | async-done | bytes 262176 | tf_op jit(solution)/shard_map/all_to_all | solution.py:50
  119.5 4.2 %all-to-all-start.3 = ((bf16[8,128,128]{2,1,0:T(8,128)(2,1)}), bf16[8,128,128]{2,1,0:T(8,128)(2,1)S(1)}, u32[]{:S(2)}, u32[]{:S(2)}) async-start(bf16[8,128,128]{2,1,0:T(8,128)(2,1)} %shard_map.85), calls=%async_computation.3 | async-start | bytes 524288 | tf_op jit(solution)/shard_map/all_to_all | solution.py:50
  123.7 1.8 %shard_map.89.refs_0_ = f32[128,1024]{1,0:T(8,128)S(1)} custom-call(s32[1]{0:T(128)} %bitcast.place_ref, bf16[2048,1024]{1,0:T(8,128)(2,1)} %w_hbm.3, bf16[8,128,128]{2,1,0:T(8,128)(2,1)S(1)} %all-to-all-done.7.a_ref), custom_call_target="tpu_custom_call" | custom-call | flops 268435456 | bytes 2097152 | tf_op jit(solution)/shard_map/pallas_call | solution.py:421
  125.5 6.4 %all-to-all-done.3.a_ref = bf16[8,128,128]{2,1,0:T(8,128)(2,1)S(1)} async-done(((bf16[8,128,128]{2,1,0:T(8,128)(2,1)}), bf16[8,128,128]{2,1,0:T(8,128)(2,1)S(1)}, u32[]{:S(2)}, u32[]{:S(2)}) %all-to-all-start.3) | async-done | bytes 262176 | tf_op jit(solution)/shard_map/all_to_all | solution.py:50
  131.9 1.9 %shard_map.90 = (f32[2,32,1024]{2,1,0:T(8,128)S(1)}, f32[2,32,1024]{2,1,0:T(8,128)S(1)}) custom-call(s32[1]{0:T(128)} %bitcast.place_ref, bf16[2048,1024]{1,0:T(8,128)(2,1)} %w_hbm.3, bf16[8,128,128]{2,1,0:T(8,128)(2,1)S(1)} %all-to-all-done.3.a_ref, f32[128,1024]{1,0:T(8,128)S(1)} %shard_map.89.refs_0_), custom_call_target="tpu_custom_call" | custom-call | flops 268435456 | bytes 2097152 | tf_op jit(solution)/shard_map/pallas_call | solution.py:421
  133.8 0.1 collective-permute-start.3
  133.9 1.5 %collective-permute-done.3 = f32[2,32,1024]{2,1,0:T(8,128)S(1)} collective-permute-done((f32[2,32,1024]{2,1,0:T(8,128)S(1)}, f32[2,32,1024]{2,1,0:T(8,128)S(1)}, u32[]{:S(2)}, u32[]{:S(2)}) %collective-permute-start.3) | collective-permute-done | bytes 262176 | tf_op jit(solution)/shard_map/ppermute | solution.py:39
  135.5 1.6 %collective-permute-start.4 = (f16[1,32,1024]{2,1,0:T(8,128)(2,1)S(1)}, f16[1,32,1024]{2,1,0:T(8,128)(2,1)S(1)}, u32[]{:S(2)}, u32[]{:S(2)}) collective-permute-start(f16[1,32,1024]{2,1,0:T(8,128)(2,1)S(1)} %multiply_convert_fusion), channel_id=1, source_target_pairs={{0,2},{1,3},{2,0},{3,1},{4,6},{5,7},{6,4},{7,5},{8,10},{9,11},{10,... | collective-permute-start | bytes 196616 | tf_op jit(solution)/shard_map/ppermute | solution.py:39
  137.1 2.7 %collective-permute-done.4 = f16[1,32,1024]{2,1,0:T(8,128)(2,1)S(1)} collective-permute-done((f16[1,32,1024]{2,1,0:T(8,128)(2,1)S(1)}, f16[1,32,1024]{2,1,0:T(8,128)(2,1)S(1)}, u32[]{:S(2)}, u32[]{:S(2)}) %collective-permute-start.4) | collective-permute-done | bytes 65568 | tf_op jit(solution)/shard_map/ppermute | solution.py:39
  139.8 0.6 fusion
  (8 shorter events, 0.1 us)
Async XLA Ops:
  0.0 1.0 copy-start.1
  1.0 1.0 copy-start.2
  2.1 0.9 copy-start.3
  5.9 9.3 %collective-permute-start.1 = (f32[4,128,128]{2,1,0:T(8,128)S(1)}, f32[4,128,128]{2,1,0:T(8,128)S(1)}, u32[]{:S(2)}, u32[]{:S(2)}) collective-permute-start(f32[4,128,128]{2,1,0:T(8,128)S(1)} %get-tuple-element.14), channel_id=1, source_target_pairs={{0,4},{4,0},{8,12},{12,8},{16,20},{20,16},{24,28},{28,24},{1,5},{5... | collective-permute-start | bytes 786440 | tf_op jit(solution)/shard_map/ppermute | solution.py:39
  15.9 13.3 %all-to-all-start.4 = ((f32[4,128,128]{2,1,0:T(8,128)}), f32[4,128,128]{2,1,0:T(8,128)S(1)}, u32[]{:S(2)}, u32[]{:S(2)}) async-start(f32[4,128,128]{2,1,0:T(8,128)} %add.26), calls=%async_computation.4 | async-start | bytes 524288 | tf_op jit(solution)/shard_map/all_to_all | solution.py:45
  21.1 13.8 %collective-permute-start = (f32[4,192,128]{2,1,0:T(8,128)S(1)}, f32[4,192,128]{2,1,0:T(8,128)S(1)}, u32[]{:S(2)}, u32[]{:S(2)}) collective-permute-start(f32[4,192,128]{2,1,0:T(8,128)S(1)} %get-tuple-element.12), channel_id=1, source_target_pairs={{0,4},{4,0},{8,12},{12,8},{16,20},{20,16},{24,28},{28,24},{1,5},{5... | collective-permute-start | bytes 1179656 | tf_op jit(solution)/shard_map/ppermute | solution.py:39
  29.2 0.7 copy-start.5
  31.6 9.2 %all-to-all-start.5 = ((bf16[4,128,128]{2,1,0:T(8,128)(2,1)}), bf16[4,128,128]{2,1,0:T(8,128)(2,1)S(1)}, u32[]{:S(2)}, u32[]{:S(2)}) async-start(bf16[4,128,128]{2,1,0:T(8,128)(2,1)} %shard_map.86.q_ref), calls=%async_computation.5 | async-start | bytes 262144 | tf_op jit(solution)/shard_map/all_to_all | solution.py:45
  40.8 12.3 %all-to-all-start = ((f32[4,192,128]{2,1,0:T(8,128)}), f32[4,192,128]{2,1,0:T(8,128)S(1)}, u32[]{:S(2)}, u32[]{:S(2)}) async-start(f32[4,192,128]{2,1,0:T(8,128)} %add.25), calls=%async_computation | async-start | bytes 786432 | tf_op jit(solution)/shard_map/all_to_all | solution.py:45
  44.3 15.1 %collective-permute-start.2 = (bf16[4,128,128]{2,1,0:T(8,128)(2,1)S(1)}, bf16[4,128,128]{2,1,0:T(8,128)(2,1)S(1)}, u32[]{:S(2)}, u32[]{:S(2)}) collective-permute-start(bf16[4,128,128]{2,1,0:T(8,128)(2,1)S(1)} %all-to-all-done.5.refs_0_), channel_id=1, source_target_pairs={{0,4},{4,0},{8,12},{12,8},{16,20},{20,16},{24,28},{28,24},{1,5},{5... | collective-permute-start | bytes 393224 | tf_op jit(solution)/shard_map/ppermute | solution.py:39
  53.1 0.8 copy-start.4
  55.6 12.9 %all-to-all-start.1 = ((bf16[8,192,128]{2,1,0:T(8,128)(2,1)}), bf16[8,192,128]{2,1,0:T(8,128)(2,1)S(1)}, u32[]{:S(2)}, u32[]{:S(2)}) async-start(bf16[8,192,128]{2,1,0:T(8,128)(2,1)} %shard_map.83.q_ref), calls=%async_computation.1 | async-start | bytes 786432 | tf_op jit(solution)/shard_map/all_to_all | solution.py:50
  68.5 19.1 %copy-start = (bf16[8,192,128]{2,1,0:T(8,128)(2,1)}, bf16[8,192,128]{2,1,0:T(8,128)(2,1)S(1)}, u32[]{:S(2)}) copy-start(bf16[8,192,128]{2,1,0:T(8,128)(2,1)S(1)} %all-to-all-done.1.refs_0_.last_ref) | copy-start | bytes 1179652
  68.5 19.8 %all-to-all-start.6 = ((f16[8,136,128]{2,1,0:T(8,128)(2,1)}), f16[8,136,128]{2,1,0:T(8,128)(2,1)S(1)}, u32[]{:S(2)}, u32[]{:S(2)}) async-start(f16[8,136,128]{2,1,0:T(8,128)(2,1)} %convert_element_type.28), calls=%async_computation.6 | async-start | bytes 557056 | tf_op jit(solution)/shard_map/all_to_all | solution.py:476
  88.3 19.5 %all-to-all-start.2 = ((f16[8,136,128]{2,1,0:T(8,128)(2,1)}), f16[8,136,128]{2,1,0:T(8,128)(2,1)S(1)}, u32[]{:S(2)}, u32[]{:S(2)}) async-start(f16[8,136,128]{2,1,0:T(8,128)(2,1)} %convert_element_type.26), calls=%async_computation.2 | async-start | bytes 557056 | tf_op jit(solution)/shard_map/all_to_all | solution.py:476
  107.9 11.6 %all-to-all-start.7 = ((bf16[8,128,128]{2,1,0:T(8,128)(2,1)}), bf16[8,128,128]{2,1,0:T(8,128)(2,1)S(1)}, u32[]{:S(2)}, u32[]{:S(2)}) async-start(bf16[8,128,128]{2,1,0:T(8,128)(2,1)} %shard_map.88), calls=%async_computation.7 | async-start | bytes 524288 | tf_op jit(solution)/shard_map/all_to_all | solution.py:50
  119.5 12.5 %all-to-all-start.3 = ((bf16[8,128,128]{2,1,0:T(8,128)(2,1)}), bf16[8,128,128]{2,1,0:T(8,128)(2,1)S(1)}, u32[]{:S(2)}, u32[]{:S(2)}) async-start(bf16[8,128,128]{2,1,0:T(8,128)(2,1)} %shard_map.85), calls=%async_computation.3 | async-start | bytes 524288 | tf_op jit(solution)/shard_map/all_to_all | solution.py:50
  133.8 1.6 %collective-permute-start.3 = (f32[2,32,1024]{2,1,0:T(8,128)S(1)}, f32[2,32,1024]{2,1,0:T(8,128)S(1)}, u32[]{:S(2)}, u32[]{:S(2)}) collective-permute-start(f32[2,32,1024]{2,1,0:T(8,128)S(1)} %get-tuple-element.16), channel_id=1, source_target_pairs={{0,1},{1,0},{2,3},{3,2},{4,5},{5,4},{6,7},{7,6},{8,9},{9,8},{10,11... | collective-permute-start | bytes 786440 | tf_op jit(solution)/shard_map/ppermute | solution.py:39
  135.5 4.3 %collective-permute-start.4 = (f16[1,32,1024]{2,1,0:T(8,128)(2,1)S(1)}, f16[1,32,1024]{2,1,0:T(8,128)(2,1)S(1)}, u32[]{:S(2)}, u32[]{:S(2)}) collective-permute-start(f16[1,32,1024]{2,1,0:T(8,128)(2,1)S(1)} %multiply_convert_fusion), channel_id=1, source_target_pairs={{0,2},{1,3},{2,0},{3,1},{4,6},{5,7},{6,4},{7,5},{8,10},{9,11},{10,... | collective-permute-start | bytes 196616 | tf_op jit(solution)/shard_map/ppermute | solution.py:39

commit v4 on v3

--- a/solution.py
+++ b/solution.py
@@ -16,6 +16,7 @@
 LANES = 128
 STAT_ROWS = 8
 VMEM_GRANT = 51 << 20
+PROJECT_GRANT = 56 << 20
 NT = (((1,), (1,)), ((), ()))
 
 OUTPUT_SCALE = 2.0**12
@@ -39,17 +40,42 @@
     return lax.ppermute(array, axis, [(i, i ^ mask) for i in range(size)])
 
 
-def within_parity(array):
-    size = lax.axis_size("seq")
-    groups = [list(range(first, size, 2)) for first in range(2)]
-    return lax.all_to_all(array, "seq", 0, 0, axis_index_groups=groups)
-
-
-def spread(copies):
-    if copies.shape[0] == lax.axis_size("seq"):
-        return [lax.all_to_all(copies, "seq", 0, 0)]
-    same = within_parity(copies)
-    return [same, swap(same, "seq", 1)]
+def owners_sum(keep, send, me):
+    total = keep + swap(send, "seq", 1)
+    mask = 2
+    while mask < lax.axis_size("seq"):
+        bit = me // mask % 2
+        pairs = total.reshape((-1, 2) + total.shape[1:])
+        keep = lax.dynamic_index_in_dim(pairs, bit, 1, False)
+        send = lax.dynamic_index_in_dim(pairs, 1 - bit, 1, False)
+        total = keep + swap(send, "seq", mask)
+        mask *= 2
+    return total.astype(jnp.bfloat16)
+
+
+def doubling_masks(size):
+    masks = []
+    while size > 2:
+        size //= 2
+        masks.append(size)
+    return masks
+
+
+def gather_doubling(block):
+    for mask in doubling_masks(lax.axis_size("seq")):
+        block = jnp.concatenate([block, swap(block, "seq", mask)])
+    return [block, swap(block, "seq", 1)]
+
+
+def doubling_offsets(size):
+    offsets = [0]
+    for mask in doubling_masks(size):
+        offsets = offsets + [offset ^ mask for offset in offsets]
+    return offsets + [offset ^ 1 for offset in offsets]
+
+
+def gather_at_once(copies):
+    return lax.all_to_all(copies, "seq", 0, 0)
 
 
 def project_kernel(me_ref, hidden_ref, q_hbm, k_hbm, v_hbm, *refs, chunks, blocks, pieces):
@@ -125,31 +151,13 @@
             pltpu.VMEM((chunks, tokens, wide // chunks), jnp.float32),
             pltpu.SemaphoreType.DMA((pieces + 2,)),
         ],
-        compiler_params=pltpu.CompilerParams(vmem_limit_bytes=VMEM_GRANT),
+        compiler_params=pltpu.CompilerParams(vmem_limit_bytes=PROJECT_GRANT),
         cost_estimate=pl.CostEstimate(
             flops=2 * tokens * depth * (wide + 2 * narrow),
             bytes_accessed=2 * depth * (wide + 2 * narrow),
             transcendentals=0,
         ),
     )(me, hidden, query_weight, key_weight, value_weight)
-
-
-def collect_kernel(part_ref, copies_ref):
-    total = part_ref[0]
-    for k in range(1, part_ref.shape[0]):
-        total = total + part_ref[k]
-    total = total.astype(jnp.bfloat16)
-    for k in range(copies_ref.shape[0]):
-        copies_ref[k] = total
-
-
-def collect(parts, copies):
-    return pl.pallas_call(
-        collect_kernel,
-        out_shape=jax.ShapeDtypeStruct((copies,) + parts.shape[1:], jnp.bfloat16),
-        in_specs=[vmem_spec()],
-        out_specs=vmem_spec(),
-    )(parts)
 
 
 def attention_kernel(len_ref, me_ref, *refs, sources, band, step, block, head):
@@ -164,11 +172,11 @@
     scale = math.log2(math.e) / math.sqrt(HD)
     piece = math.gcd(step, 1024)
     tiles = piece // LANES
-    odd = lax.rem(me_ref[0], 2)
     lanes = slice(head * HD, (head + 1) * HD)
+    offsets = doubling_offsets(sources * half)
 
     def owner_of(k):
-        return k if sources == 1 else 2 * (k % half) + (odd if k < half else 1 - odd)
+        return k if sources == 1 else me_ref[0] ^ offsets[k]
 
     length = len_ref[0]
     full = length // step
@@ -261,10 +269,13 @@
         if weighs:
             totals = acc[:, LANES:]
             mean = acc[:, :LANES] / totals * OUTPUT_SCALE
+            levels = shift[...] + jnp.log2(totals)
             for e in range(share):
                 k = (r - 1) * share + e
-                o_ref[owner_of(k), :block, :] = mean[e * block : (e + 1) * block, :]
-            lse_all[(r - 1) * band : r * band, :] = shift[...] + jnp.log2(totals)
+                owner = owner_of(k)
+                here = slice(e * block, (e + 1) * block)
+                o_ref[owner, :block, :] = mean[here, :]
+                lse_all[pl.ds(pl.multiple_of(owner * block, block), block), :] = levels[here, :]
 
     per = LANES // block
     row = lax.broadcasted_iota(jnp.int32, (STAT_ROWS, LANES), 0)
@@ -280,15 +291,14 @@
         stats = jnp.where(row == 0, exponent, jnp.where(row == 1, first, second))
         stats = jnp.where(row >= 3, third, stats)
         for e in range(per):
-            k = g * per + e
-            o_ref[owner_of(k), block:, :] = stats
+            o_ref[g * per + e, block:, :] = stats
 
 
 def attention(queries, block, keys, values, length, me, head):
     sources = len(queries)
     count = sources * queries[0].shape[0]
     rows, slots = count * block, keys.shape[0]
-    band = math.gcd(rows // 2, 256)
+    band = math.gcd(rows // 2, 512)
     step = math.gcd(slots, 2048)
     return pl.pallas_call(
         functools.partial(
@@ -340,7 +350,7 @@
     new_total = jnp.sum(weights.astype(jnp.float32), axis=1, keepdims=True)
     new_out = jnp.dot(weights, values, preferred_element_type=jnp.float32)
 
-    place = lax.rem(me_ref[0] // 2, per)
+    place = lax.rem(me_ref[0], per)
     pieces = part_ref[:, block : block + 4, :]
     level = pieces[:, 1, :] * 2.0**-9 + pieces[:, 2, :] * 2.0**-20 + pieces[:, 3, :] * 2.0**-31
     turned[...] = (level * jnp.exp2(pieces[:, 0, :])).T
@@ -463,12 +473,14 @@
     place = lax.axis_index("head").reshape(1)
 
     halves = project(me, hidden, query_weight, key_weight, value_weight, kv_local, count)
-    mine = []
+    mine, queries = [], []
     for j in range(kv_local):
-        keep, send = halves[2 * j : 2 * j + 2]
-        parts = within_parity(keep + swap(send, "seq", 1))
-        mine.append(collect(parts, count if j == kv_local - 1 else count // 2))
-    queries = [spread(copies) for copies in mine]
+        mine.append(owners_sum(halves[2 * j], halves[2 * j + 1], me[0]))
+        if j < kv_local - 1:
+            queries.append(gather_doubling(mine[j]))
+        else:
+            copies = jnp.broadcast_to(mine[j], (count,) + mine[j].shape[1:])
+            queries.append([gather_at_once(copies)])
 
     mixed = None
     for j in range(kv_local):
@@ -477,7 +489,7 @@
         copies = merge(me, parts, mine[j], queries[-1][0], block, tokens, j)
         last = j == kv_local - 1
         result = output_part(
-            place, output_weight, spread(copies)[0], tokens, mixed, j, heads, last
+            place, output_weight, gather_at_once(copies), tokens, mixed, j, heads, last
         )
         mixed = result if last else result[0]
 

time: 142 us -> 129 us (0.908)
  waiting for transfers between devices: 44.5 us -> 39.1 us
  local copies, waits for them, and re-layouts: 4.5 us -> 0.89 us
  Pallas kernels: 32.2 us -> 28.8 us
  starting transfers between devices: 53 us -> 51.4 us
    all_to_all x6 -> x3, waiting for transfers between devices: 29.5 us -> 12 us  [gather_at_once(): return lax.all_to_all(copies, 'seq', 0, 0)]
    ppermute x5 -> x11, starting transfers between devices: 7.76 us -> 20.2 us  [swap(): return lax.ppermute(array, axis, [(i, i ^ mask) for i in range(size)])]
    ppermute x5 -> x11, waiting for transfers between devices: 10.5 us -> 22.2 us  [swap(): return lax.ppermute(array, axis, [(i, i ^ mask) for i in range(size)])]
    all_to_all x6 -> x3, starting transfers between devices: 23.2 us -> 11.6 us  [gather_at_once(): return lax.all_to_all(copies, 'seq', 0, 0)]
    unnamed x12 -> x6, local copies, waits for them, and re-layouts: 4.5 us -> 0.01 us
    pallas_call x2 -> x0, Pallas kernels: 3.39 us -> none  [collect(): pl.pallas_call(collect_kernel, out_shape=jax.ShapeDtypeStruct((copies,) +...]
    all_to_all x2, starting transfers between devices: 22 us -> 19.6 us  [shards(): lax.all_to_all(parts.astype(jnp.float16), 'seq', 0, 0).astype(jnp.float32)]
    pallas_call x1, Pallas kernels: 2.85 us -> 4.68 us  [project(): pl.pallas_call(functools.partial(project_kernel, chunks=chunks, blocks=bl...]
  transfers between devices with their start and end apart: 13 -> 16, of which waited for: 10 -> 13; matrix products, arithmetic and copies ran while one was open for 3% -> 4% of each run, Pallas kernels for 20% -> 17%
where the time goes in v4:
time: 129 us; the launch traced here: 127 us
  starting transfers between devices  51.4 us (40%)
  waiting for transfers between devices  39.1 us (30%)
  Pallas kernels  28.8 us (22%)
  other arithmetic  6.01 us (5%)
    ppermute x11, waiting for transfers between devices, swap(): return lax.ppermute(array, axis, [(i, i ^ mask) for i in range(size)])  22.2 us
    ppermute x11, starting transfers between devices, swap(): return lax.ppermute(array, axis, [(i, i ^ mask) for i in range(size)])  20.2 us
    all_to_all x2, starting transfers between devices, shards(): lax.all_to_all(parts.astype(jnp.float16), 'seq', 0, 0).astype(jnp.float32)  19.6 us
    pallas_call x2, Pallas kernels, attention(): pl.pallas_call(functools.partial(attention_kernel, sources=sources, band=...  14.6 us
    all_to_all x3, waiting for transfers between devices, gather_at_once(): return lax.all_to_all(copies, 'seq', 0, 0)  12 us
    all_to_all x3, starting transfers between devices, gather_at_once(): return lax.all_to_all(copies, 'seq', 0, 0)  11.6 us
    pallas_call x2, Pallas kernels, merge(): pl.pallas_call(functools.partial(merge_kernel, block=block, tokens=tokens...  5.79 us
    all_to_all x2, waiting for transfers between devices, shards(): lax.all_to_all(parts.astype(jnp.float16), 'seq', 0, 0).astype(jnp.float32)  4.91 us
  transfers between devices with their start and end apart: 16, of which 13 were waited for; matrix products, arithmetic and copies ran while one was open for 4% of the time, Pallas kernels for 17%

profile of v4, /device:TPU:0, one launch (start us, length us, event | category | flops | bytes accessed | tf_op | source)
XLA Modules:
  0.0 127.1 jit_solution(17619016732618671759)
XLA Ops:
  0.0 4.7 %shard_map.82 = (f32[4,128,128]{2,1,0:T(8,128)}, f32[4,128,128]{2,1,0:T(8,128)}, f32[4,192,128]{2,1,0:T(8,128)}, f32[4,192,128]{2,1,0:T(8,128)}) custom-call(s32[1]{0:T(128)} %bitcast.1.me_ref, bf16[128,1024]{1,0:T(8,128)(2,1)} %hidden_ref.1, bf16[1024,2048]{1,0:T(8,128)(2,1)} %q_hbm.1, bf16[1024,256]{1,0:T(8,128)(2,1)} %k_hbm.1, bf16[1024,256]{1,0:T(8,128)(2,1)} %v_hbm.1), custom_call_target="tpu_custom_call" | custom-call | flops 671088640 | bytes 5242880 | tf_op jit(solution)/shard_map/pallas_call | solution.py:142
  4.7 3.0 %collective-permute-start.3 = (f32[4,128,128]{2,1,0:T(8,128)}, f32[4,128,128]{2,1,0:T(8,128)S(1)}, u32[]{:S(2)}, u32[]{:S(2)}) collective-permute-start(f32[4,128,128]{2,1,0:T(8,128)} %get-tuple-element.14), channel_id=1, source_target_pairs={{0,4},{4,0},{8,12},{12,8},{16,20},{20,16},{24,28},{28,24},{1,5},{5... | collective-permute-start | bytes 786440 | tf_op jit(solution)/shard_map/ppermute | solution.py:40
  7.7 6.5 %collective-permute-done.3 = f32[4,128,128]{2,1,0:T(8,128)S(1)} collective-permute-done((f32[4,128,128]{2,1,0:T(8,128)}, f32[4,128,128]{2,1,0:T(8,128)S(1)}, u32[]{:S(2)}, u32[]{:S(2)}) %collective-permute-start.3) | collective-permute-done | bytes 262176 | tf_op jit(solution)/shard_map/ppermute | solution.py:40
  14.2 1.0 add.78
  15.2 1.9 %collective-permute-start.4 = (f32[2,128,128]{2,1,0:T(8,128)S(1)}, f32[2,128,128]{2,1,0:T(8,128)S(1)}, u32[]{:S(2)}, u32[]{:S(2)}) collective-permute-start(f32[2,128,128]{2,1,0:T(8,128)S(1)} %dynamic-slice_bitcast_fusion.1), channel_id=1, source_target_pairs={{0,8},{4,12},{8,0},{12,4},{16,24},{20,28},{24,16},{28,20},{1,9},{5... | collective-permute-start | bytes 393224 | tf_op jit(solution)/shard_map/ppermute | solution.py:40
  17.1 1.5 %collective-permute-start = (f32[4,192,128]{2,1,0:T(8,128)}, f32[4,192,128]{2,1,0:T(8,128)S(1)}, u32[]{:S(2)}, u32[]{:S(2)}) collective-permute-start(f32[4,192,128]{2,1,0:T(8,128)} %get-tuple-element.12), channel_id=1, source_target_pairs={{0,4},{4,0},{8,12},{12,8},{16,20},{20,16},{24,28},{28,24},{1,5},{5... | collective-permute-start | bytes 1179656 | tf_op jit(solution)/shard_map/ppermute | solution.py:40
  18.6 1.6 %collective-permute-done.4 = f32[2,128,128]{2,1,0:T(8,128)S(1)} collective-permute-done((f32[2,128,128]{2,1,0:T(8,128)S(1)}, f32[2,128,128]{2,1,0:T(8,128)S(1)}, u32[]{:S(2)}, u32[]{:S(2)}) %collective-permute-start.4) | collective-permute-done | bytes 131104 | tf_op jit(solution)/shard_map/ppermute | solution.py:40
  20.3 2.9 %collective-permute-start.5 = (f32[1,128,128]{2,1,0:T(8,128)S(1)}, f32[1,128,128]{2,1,0:T(8,128)S(1)}, u32[]{:S(2)}, u32[]{:S(2)}) collective-permute-start(f32[1,128,128]{2,1,0:T(8,128)S(1)} %constant_dynamic-slice_fusion), channel_id=1, source_target_pairs={{0,16},{4,20},{8,24},{12,28},{16,0},{20,4},{24,8},{28,12},{1,17},{... | collective-permute-start | bytes 196616 | tf_op jit(solution)/shard_map/ppermute | solution.py:40
  23.2 3.8 %collective-permute-done = f32[4,192,128]{2,1,0:T(8,128)S(1)} collective-permute-done((f32[4,192,128]{2,1,0:T(8,128)}, f32[4,192,128]{2,1,0:T(8,128)S(1)}, u32[]{:S(2)}, u32[]{:S(2)}) %collective-permute-start) | collective-permute-done | bytes 393248 | tf_op jit(solution)/shard_map/ppermute | solution.py:40
  27.0 1.0 add.69
  28.1 0.6 collective-permute-start.1
  28.7 0.0 collective-permute-done.5
  28.7 2.6 %collective-permute-start.6 = (bf16[1,128,128]{2,1,0:T(8,128)(2,1)S(1)}, bf16[1,128,128]{2,1,0:T(8,128)(2,1)S(1)}, u32[]{:S(2)}, u32[]{:S(2)}) collective-permute-start(bf16[1,128,128]{2,1,0:T(8,128)(2,1)S(1)} %add_convert_fusion.2.q_ref), channel_id=1, source_target_pairs={{0,16},{4,20},{8,24},{12,28},{16,0},{20,4},{24,8},{28,12},{1,17},{... | collective-permute-start | bytes 98312 | tf_op jit(solution)/shard_map/ppermute | solution.py:40
  32.0 1.7 %collective-permute-done.6 = bf16[1,128,128]{2,1,0:T(8,128)(2,1)S(1)} collective-permute-done((bf16[1,128,128]{2,1,0:T(8,128)(2,1)S(1)}, bf16[1,128,128]{2,1,0:T(8,128)(2,1)S(1)}, u32[]{:S(2)}, u32[]{:S(2)}) %collective-permute-start.6) | collective-permute-done | bytes 32800 | tf_op jit(solution)/shard_map/ppermute | solution.py:40
  33.7 4.2 %collective-permute-start.7 = (bf16[2,128,128]{2,1,0:T(8,128)(2,1)S(1)}, bf16[2,128,128]{2,1,0:T(8,128)(2,1)S(1)}, u32[]{:S(2)}, u32[]{:S(2)}) collective-permute-start(bf16[2,128,128]{2,1,0:T(8,128)(2,1)S(1)} %pad_maximum_fusion.1), channel_id=1, source_target_pairs={{0,8},{4,12},{8,0},{12,4},{16,24},{20,28},{24,16},{28,20},{1,9},{5... | collective-permute-start | bytes 196616 | tf_op jit(solution)/shard_map/ppermute | solution.py:40
  37.9 0.0 collective-permute-done.1
  38.0 0.3 collective-permute-start.2
  38.2 1.9 %collective-permute-done.7 = bf16[2,128,128]{2,1,0:T(8,128)(2,1)S(1)} collective-permute-done((bf16[2,128,128]{2,1,0:T(8,128)(2,1)S(1)}, bf16[2,128,128]{2,1,0:T(8,128)(2,1)S(1)}, u32[]{:S(2)}, u32[]{:S(2)}) %collective-permute-start.7) | collective-permute-done | bytes 65568 | tf_op jit(solution)/shard_map/ppermute | solution.py:40
  40.2 1.6 %collective-permute-start.8 = (bf16[4,128,128]{2,1,0:T(8,128)(2,1)S(1)}, bf16[4,128,128]{2,1,0:T(8,128)(2,1)S(1)}, u32[]{:S(2)}, u32[]{:S(2)}) collective-permute-start(bf16[4,128,128]{2,1,0:T(8,128)(2,1)S(1)} %pad_maximum_fusion.refs_0_), channel_id=1, source_target_pairs={{0,4},{4,0},{8,12},{12,8},{16,20},{20,16},{24,28},{28,24},{1,5},{5... | collective-permute-start | bytes 393224 | tf_op jit(solution)/shard_map/ppermute | solution.py:40
  41.7 2.3 %collective-permute-done.2 = f32[1,192,128]{2,1,0:T(8,128)S(1)} collective-permute-done((f32[1,192,128]{2,1,0:T(8,128)S(1)}, f32[1,192,128]{2,1,0:T(8,128)S(1)}, u32[]{:S(2)}, u32[]{:S(2)}) %collective-permute-start.2) | collective-permute-done | bytes 98336 | tf_op jit(solution)/shard_map/ppermute | solution.py:40
  44.1 0.0 copy-start.2
  44.1 0.8 broadcast_in_dim.8
  44.9 3.5 %all-to-all-start = ((bf16[8,192,128]{2,1,0:T(8,128)(2,1)}), bf16[8,192,128]{2,1,0:T(8,128)(2,1)S(1)}, u32[]{:S(2)}, u32[]{:S(2)}) async-start(bf16[8,192,128]{2,1,0:T(8,128)(2,1)} %broadcast_in_dim.8), calls=%async_computation | async-start | bytes 786432 | tf_op jit(solution)/shard_map/all_to_all | solution.py:78
  48.4 0.0 collective-permute-done.8.refs_1_
  48.4 7.3 %shard_map.85 = f32[8,136,128]{2,1,0:T(8,128)S(1)} custom-call(s32[1]{0:T(128)S(6)} %copy.17.len_ref, s32[1]{0:T(128)} %bitcast.1.me_ref, bf16[4,128,128]{2,1,0:T(8,128)(2,1)S(1)} %pad_maximum_fusion.refs_0_, bf16[4,128,128]{2,1,0:T(8,128)(2,1)S(1)} %collective-permute-done.8.refs_1_, bf16[8192,256]{1,0:T(8,128)(2,1)} %refs_2_.3, bf16[8192,256]{1,0:T(8,128)(2,1)} %refs_3_.1), custom_call_target="tpu_custom_call" | custom-call | flops 8589934592 | bytes 4194304 | tf_op jit(solution)/shard_map/pallas_call | solution.py:303
  55.7 0.7 convert_element_type.36
  56.4 1.1 all-to-all-done.refs_0_.last_ref
  57.5 9.3 %all-to-all-start.3 = ((f16[8,136,128]{2,1,0:T(8,128)(2,1)}), f16[8,136,128]{2,1,0:T(8,128)(2,1)S(1)}, u32[]{:S(2)}, u32[]{:S(2)}) async-start(f16[8,136,128]{2,1,0:T(8,128)(2,1)} %convert_element_type.36), calls=%async_computation.3 | async-start | bytes 557056 | tf_op jit(solution)/shard_map/all_to_all | solution.py:488
  66.8 7.4 %shard_map.83 = f32[8,136,128]{2,1,0:T(8,128)S(1)} custom-call(s32[1]{0:T(128)S(6)} %copy.17.len_ref, s32[1]{0:T(128)} %bitcast.1.me_ref, bf16[8,192,128]{2,1,0:T(8,128)(2,1)S(1)} %all-to-all-done.refs_0_.last_ref, bf16[8192,256]{1,0:T(8,128)(2,1)} %refs_2_.3, bf16[8192,256]{1,0:T(8,128)(2,1)} %refs_3_.1), custom_call_target="tpu_custom_call" | custom-call | flops 8589934592 | bytes 4194304 | tf_op jit(solution)/shard_map/pallas_call | solution.py:303
  74.2 0.7 convert_element_type.33
  74.9 0.2 all-to-all-done.3
  75.1 10.3 %all-to-all-start.1 = ((f16[8,136,128]{2,1,0:T(8,128)(2,1)}), f16[8,136,128]{2,1,0:T(8,128)(2,1)S(1)}, u32[]{:S(2)}, u32[]{:S(2)}) async-start(f16[8,136,128]{2,1,0:T(8,128)(2,1)} %convert_element_type.33), calls=%async_computation.1 | async-start | bytes 557056 | tf_op jit(solution)/shard_map/all_to_all | solution.py:488
  85.4 0.9 convert_element_type.37.part_ref
  86.3 2.9 %shard_map.86 = bf16[8,128,128]{2,1,0:T(8,128)(2,1)} custom-call(s32[1]{0:T(128)} %bitcast.1.me_ref, f32[8,136,128]{2,1,0:T(8,128)} %convert_element_type.37.part_ref, bf16[1,128,128]{2,1,0:T(8,128)(2,1)} %copy-done.1, bf16[8,192,128]{2,1,0:T(8,128)(2,1)} %copy-done), custom_call_target="tpu_custom_call" | custom-call | tf_op jit(solution)/shard_map/pallas_call | solution.py:374
  89.2 4.7 %all-to-all-done.1 = f16[8,136,128]{2,1,0:T(8,128)(2,1)S(1)} async-done(((f16[8,136,128]{2,1,0:T(8,128)(2,1)}), f16[8,136,128]{2,1,0:T(8,128)(2,1)S(1)}, u32[]{:S(2)}, u32[]{:S(2)}) %all-to-all-start.1) | async-done | bytes 278560 | tf_op jit(solution)/shard_map/all_to_all | solution.py:488
  93.9 3.4 %all-to-all-start.4 = ((bf16[8,128,128]{2,1,0:T(8,128)(2,1)}), bf16[8,128,128]{2,1,0:T(8,128)(2,1)S(1)}, u32[]{:S(2)}, u32[]{:S(2)}) async-start(bf16[8,128,128]{2,1,0:T(8,128)(2,1)} %shard_map.86), calls=%async_computation.4 | async-start | bytes 524288 | tf_op jit(solution)/shard_map/all_to_all | solution.py:78
  97.3 0.9 convert_element_type.34.part_ref
  98.1 2.9 %shard_map.84 = bf16[8,128,128]{2,1,0:T(8,128)(2,1)} custom-call(s32[1]{0:T(128)} %bitcast.1.me_ref, f32[8,136,128]{2,1,0:T(8,128)} %convert_element_type.34.part_ref, bf16[1,192,128]{2,1,0:T(8,128)(2,1)} %copy-done.2, bf16[8,192,128]{2,1,0:T(8,128)(2,1)} %copy-done), custom_call_target="tpu_custom_call" | custom-call | tf_op jit(solution)/shard_map/pallas_call | solution.py:374
  101.0 4.5 %all-to-all-done.4.a_ref = bf16[8,128,128]{2,1,0:T(8,128)(2,1)S(1)} async-done(((bf16[8,128,128]{2,1,0:T(8,128)(2,1)}), bf16[8,128,128]{2,1,0:T(8,128)(2,1)S(1)}, u32[]{:S(2)}, u32[]{:S(2)}) %all-to-all-start.4) | async-done | bytes 262176 | tf_op jit(solution)/shard_map/all_to_all | solution.py:78
  105.5 4.8 %all-to-all-start.2 = ((bf16[8,128,128]{2,1,0:T(8,128)(2,1)}), bf16[8,128,128]{2,1,0:T(8,128)(2,1)S(1)}, u32[]{:S(2)}, u32[]{:S(2)}) async-start(bf16[8,128,128]{2,1,0:T(8,128)(2,1)} %shard_map.84), calls=%async_computation.2 | async-start | bytes 524288 | tf_op jit(solution)/shard_map/all_to_all | solution.py:78
  110.3 1.8 %shard_map.87.refs_0_ = f32[128,1024]{1,0:T(8,128)S(1)} custom-call(s32[1]{0:T(128)} %bitcast.place_ref, bf16[2048,1024]{1,0:T(8,128)(2,1)} %w_hbm.3, bf16[8,128,128]{2,1,0:T(8,128)(2,1)S(1)} %all-to-all-done.4.a_ref), custom_call_target="tpu_custom_call" | custom-call | flops 268435456 | bytes 2097152 | tf_op jit(solution)/shard_map/pallas_call | solution.py:431
  112.2 6.4 %all-to-all-done.2.a_ref = bf16[8,128,128]{2,1,0:T(8,128)(2,1)S(1)} async-done(((bf16[8,128,128]{2,1,0:T(8,128)(2,1)}), bf16[8,128,128]{2,1,0:T(8,128)(2,1)S(1)}, u32[]{:S(2)}, u32[]{:S(2)}) %all-to-all-start.2) | async-done | bytes 262176 | tf_op jit(solution)/shard_map/all_to_all | solution.py:78
  118.5 1.9 %shard_map.88 = (f32[2,32,1024]{2,1,0:T(8,128)S(1)}, f32[2,32,1024]{2,1,0:T(8,128)S(1)}) custom-call(s32[1]{0:T(128)} %bitcast.place_ref, bf16[2048,1024]{1,0:T(8,128)(2,1)} %w_hbm.3, bf16[8,128,128]{2,1,0:T(8,128)(2,1)S(1)} %all-to-all-done.2.a_ref, f32[128,1024]{1,0:T(8,128)S(1)} %shard_map.87.refs_0_), custom_call_target="tpu_custom_call" | custom-call | flops 268435456 | bytes 2097152 | tf_op jit(solution)/shard_map/pallas_call | solution.py:431
  120.4 0.1 collective-permute-start.9
  120.5 1.5 %collective-permute-done.9 = f32[2,32,1024]{2,1,0:T(8,128)S(1)} collective-permute-done((f32[2,32,1024]{2,1,0:T(8,128)S(1)}, f32[2,32,1024]{2,1,0:T(8,128)S(1)}, u32[]{:S(2)}, u32[]{:S(2)}) %collective-permute-start.9) | collective-permute-done | bytes 262176 | tf_op jit(solution)/shard_map/ppermute | solution.py:40
  122.1 1.6 %collective-permute-start.10 = (f16[1,32,1024]{2,1,0:T(8,128)(2,1)S(1)}, f16[1,32,1024]{2,1,0:T(8,128)(2,1)S(1)}, u32[]{:S(2)}, u32[]{:S(2)}) collective-permute-start(f16[1,32,1024]{2,1,0:T(8,128)(2,1)S(1)} %multiply_convert_fusion), channel_id=1, source_target_pairs={{0,2},{1,3},{2,0},{3,1},{4,6},{5,7},{6,4},{7,5},{8,10},{9,11},{10,... | collective-permute-start | bytes 196616 | tf_op jit(solution)/shard_map/ppermute | solution.py:40
  123.7 2.7 %collective-permute-done.10 = f16[1,32,1024]{2,1,0:T(8,128)(2,1)S(1)} collective-permute-done((f16[1,32,1024]{2,1,0:T(8,128)(2,1)S(1)}, f16[1,32,1024]{2,1,0:T(8,128)(2,1)S(1)}, u32[]{:S(2)}, u32[]{:S(2)}) %collective-permute-start.10) | collective-permute-done | bytes 65568 | tf_op jit(solution)/shard_map/ppermute | solution.py:40
  126.4 0.6 fusion
  (17 shorter events, 0.2 us)
Async XLA Ops:
  4.7 9.5 %collective-permute-start.3 = (f32[4,128,128]{2,1,0:T(8,128)}, f32[4,128,128]{2,1,0:T(8,128)S(1)}, u32[]{:S(2)}, u32[]{:S(2)}) collective-permute-start(f32[4,128,128]{2,1,0:T(8,128)} %get-tuple-element.14), channel_id=1, source_target_pairs={{0,4},{4,0},{8,12},{12,8},{16,20},{20,16},{24,28},{28,24},{1,5},{5... | collective-permute-start | bytes 786440 | tf_op jit(solution)/shard_map/ppermute | solution.py:40
  15.2 5.0 %collective-permute-start.4 = (f32[2,128,128]{2,1,0:T(8,128)S(1)}, f32[2,128,128]{2,1,0:T(8,128)S(1)}, u32[]{:S(2)}, u32[]{:S(2)}) collective-permute-start(f32[2,128,128]{2,1,0:T(8,128)S(1)} %dynamic-slice_bitcast_fusion.1), channel_id=1, source_target_pairs={{0,8},{4,12},{8,0},{12,4},{16,24},{20,28},{24,16},{28,20},{1,9},{5... | collective-permute-start | bytes 393224 | tf_op jit(solution)/shard_map/ppermute | solution.py:40
  17.1 9.9 %collective-permute-start = (f32[4,192,128]{2,1,0:T(8,128)}, f32[4,192,128]{2,1,0:T(8,128)S(1)}, u32[]{:S(2)}, u32[]{:S(2)}) collective-permute-start(f32[4,192,128]{2,1,0:T(8,128)} %get-tuple-element.12), channel_id=1, source_target_pairs={{0,4},{4,0},{8,12},{12,8},{16,20},{20,16},{24,28},{28,24},{1,5},{5... | collective-permute-start | bytes 1179656 | tf_op jit(solution)/shard_map/ppermute | solution.py:40
  20.3 8.4 %collective-permute-start.5 = (f32[1,128,128]{2,1,0:T(8,128)S(1)}, f32[1,128,128]{2,1,0:T(8,128)S(1)}, u32[]{:S(2)}, u32[]{:S(2)}) collective-permute-start(f32[1,128,128]{2,1,0:T(8,128)S(1)} %constant_dynamic-slice_fusion), channel_id=1, source_target_pairs={{0,16},{4,20},{8,24},{12,28},{16,0},{20,4},{24,8},{28,12},{1,17},{... | collective-permute-start | bytes 196616 | tf_op jit(solution)/shard_map/ppermute | solution.py:40
  28.1 9.8 %collective-permute-start.1 = (f32[2,192,128]{2,1,0:T(8,128)S(1)}, f32[2,192,128]{2,1,0:T(8,128)S(1)}, u32[]{:S(2)}, u32[]{:S(2)}) collective-permute-start(f32[2,192,128]{2,1,0:T(8,128)S(1)} %dynamic-slice_bitcast_fusion), channel_id=1, source_target_pairs={{0,8},{4,12},{8,0},{12,4},{16,24},{20,28},{24,16},{28,20},{1,9},{5... | collective-permute-start | bytes 589832 | tf_op jit(solution)/shard_map/ppermute | solution.py:40
  28.7 26.9 %copy-start.1 = (bf16[1,128,128]{2,1,0:T(8,128)(2,1)}, bf16[1,128,128]{2,1,0:T(8,128)(2,1)S(1)}, u32[]{:S(2)}) copy-start(bf16[1,128,128]{2,1,0:T(8,128)(2,1)S(1)} %add_convert_fusion.2.q_ref) | copy-start | bytes 98308
  28.7 5.0 %collective-permute-start.6 = (bf16[1,128,128]{2,1,0:T(8,128)(2,1)S(1)}, bf16[1,128,128]{2,1,0:T(8,128)(2,1)S(1)}, u32[]{:S(2)}, u32[]{:S(2)}) collective-permute-start(bf16[1,128,128]{2,1,0:T(8,128)(2,1)S(1)} %add_convert_fusion.2.q_ref), channel_id=1, source_target_pairs={{0,16},{4,20},{8,24},{12,28},{16,0},{20,4},{24,8},{28,12},{1,17},{... | collective-permute-start | bytes 98312 | tf_op jit(solution)/shard_map/ppermute | solution.py:40
  33.7 6.5 %collective-permute-start.7 = (bf16[2,128,128]{2,1,0:T(8,128)(2,1)S(1)}, bf16[2,128,128]{2,1,0:T(8,128)(2,1)S(1)}, u32[]{:S(2)}, u32[]{:S(2)}) collective-permute-start(bf16[2,128,128]{2,1,0:T(8,128)(2,1)S(1)} %pad_maximum_fusion.1), channel_id=1, source_target_pairs={{0,8},{4,12},{8,0},{12,4},{16,24},{20,28},{24,16},{28,20},{1,9},{5... | collective-permute-start | bytes 196616 | tf_op jit(solution)/shard_map/ppermute | solution.py:40
  38.0 6.1 %collective-permute-start.2 = (f32[1,192,128]{2,1,0:T(8,128)S(1)}, f32[1,192,128]{2,1,0:T(8,128)S(1)}, u32[]{:S(2)}, u32[]{:S(2)}) collective-permute-start(f32[1,192,128]{2,1,0:T(8,128)S(1)} %constant_dynamic-slice_fusion.1), channel_id=1, source_target_pairs={{0,16},{4,20},{8,24},{12,28},{16,0},{20,4},{24,8},{28,12},{1,17},{... | collective-permute-start | bytes 294920 | tf_op jit(solution)/shard_map/ppermute | solution.py:40
  40.2 8.2 %collective-permute-start.8 = (bf16[4,128,128]{2,1,0:T(8,128)(2,1)S(1)}, bf16[4,128,128]{2,1,0:T(8,128)(2,1)S(1)}, u32[]{:S(2)}, u32[]{:S(2)}) collective-permute-start(bf16[4,128,128]{2,1,0:T(8,128)(2,1)S(1)} %pad_maximum_fusion.refs_0_), channel_id=1, source_target_pairs={{0,4},{4,0},{8,12},{12,8},{16,20},{20,16},{24,28},{28,24},{1,5},{5... | collective-permute-start | bytes 393224 | tf_op jit(solution)/shard_map/ppermute | solution.py:40
  44.1 11.6 %copy-start.2 = (bf16[1,192,128]{2,1,0:T(8,128)(2,1)}, bf16[1,192,128]{2,1,0:T(8,128)(2,1)S(1)}, u32[]{:S(2)}) copy-start(bf16[1,192,128]{2,1,0:T(8,128)(2,1)S(1)} %add_convert_fusion.1.q_ref) | copy-start | bytes 147460
  44.9 12.6 %all-to-all-start = ((bf16[8,192,128]{2,1,0:T(8,128)(2,1)}), bf16[8,192,128]{2,1,0:T(8,128)(2,1)S(1)}, u32[]{:S(2)}, u32[]{:S(2)}) async-start(bf16[8,192,128]{2,1,0:T(8,128)(2,1)} %broadcast_in_dim.8), calls=%async_computation | async-start | bytes 786432 | tf_op jit(solution)/shard_map/all_to_all | solution.py:78
  57.5 16.7 %copy-start = (bf16[8,192,128]{2,1,0:T(8,128)(2,1)}, bf16[8,192,128]{2,1,0:T(8,128)(2,1)S(1)}, u32[]{:S(2)}) copy-start(bf16[8,192,128]{2,1,0:T(8,128)(2,1)S(1)} %all-to-all-done.refs_0_.last_ref) | copy-start | bytes 1179652
  57.5 17.6 %all-to-all-start.3 = ((f16[8,136,128]{2,1,0:T(8,128)(2,1)}), f16[8,136,128]{2,1,0:T(8,128)(2,1)S(1)}, u32[]{:S(2)}, u32[]{:S(2)}) async-start(f16[8,136,128]{2,1,0:T(8,128)(2,1)} %convert_element_type.36), calls=%async_computation.3 | async-start | bytes 557056 | tf_op jit(solution)/shard_map/all_to_all | solution.py:488
  75.1 18.7 %all-to-all-start.1 = ((f16[8,136,128]{2,1,0:T(8,128)(2,1)}), f16[8,136,128]{2,1,0:T(8,128)(2,1)S(1)}, u32[]{:S(2)}, u32[]{:S(2)}) async-start(f16[8,136,128]{2,1,0:T(8,128)(2,1)} %convert_element_type.33), calls=%async_computation.1 | async-start | bytes 557056 | tf_op jit(solution)/shard_map/all_to_all | solution.py:488
  93.9 11.7 %all-to-all-start.4 = ((bf16[8,128,128]{2,1,0:T(8,128)(2,1)}), bf16[8,128,128]{2,1,0:T(8,128)(2,1)S(1)}, u32[]{:S(2)}, u32[]{:S(2)}) async-start(bf16[8,128,128]{2,1,0:T(8,128)(2,1)} %shard_map.86), calls=%async_computation.4 | async-start | bytes 524288 | tf_op jit(solution)/shard_map/all_to_all | solution.py:78
  105.5 13.0 %all-to-all-start.2 = ((bf16[8,128,128]{2,1,0:T(8,128)(2,1)}), bf16[8,128,128]{2,1,0:T(8,128)(2,1)S(1)}, u32[]{:S(2)}, u32[]{:S(2)}) async-start(bf16[8,128,128]{2,1,0:T(8,128)(2,1)} %shard_map.84), calls=%async_computation.2 | async-start | bytes 524288 | tf_op jit(solution)/shard_map/all_to_all | solution.py:78
  120.4 1.6 %collective-permute-start.9 = (f32[2,32,1024]{2,1,0:T(8,128)S(1)}, f32[2,32,1024]{2,1,0:T(8,128)S(1)}, u32[]{:S(2)}, u32[]{:S(2)}) collective-permute-start(f32[2,32,1024]{2,1,0:T(8,128)S(1)} %get-tuple-element.16), channel_id=1, source_target_pairs={{0,1},{1,0},{2,3},{3,2},{4,5},{5,4},{6,7},{7,6},{8,9},{9,8},{10,11... | collective-permute-start | bytes 786440 | tf_op jit(solution)/shard_map/ppermute | solution.py:40
  122.1 4.3 %collective-permute-start.10 = (f16[1,32,1024]{2,1,0:T(8,128)(2,1)S(1)}, f16[1,32,1024]{2,1,0:T(8,128)(2,1)S(1)}, u32[]{:S(2)}, u32[]{:S(2)}) collective-permute-start(f16[1,32,1024]{2,1,0:T(8,128)(2,1)S(1)} %multiply_convert_fusion), channel_id=1, source_target_pairs={{0,2},{1,3},{2,0},{3,1},{4,6},{5,7},{6,4},{7,5},{8,10},{9,11},{10,... | collective-permute-start | bytes 196616 | tf_op jit(solution)/shard_map/ppermute | solution.py:40

commit v5 on v4

--- a/solution.py
+++ b/solution.py
@@ -78,24 +78,29 @@
     return lax.all_to_all(copies, "seq", 0, 0)
 
 
-def project_kernel(me_ref, hidden_ref, q_hbm, k_hbm, v_hbm, *refs, chunks, blocks, pieces):
-    outs = refs[: 2 * chunks]
-    q_all, k_all, v_all, total, sems = refs[2 * chunks :]
+def project_kernel(me_ref, hidden_ref, *refs, extra, chunk, blocks, pieces):
+    weight_refs, refs = refs[: 1 + extra], refs[1 + extra :]
+    keep_ref, send_ref, q_all, *others_all, sems = refs
     tokens, depth = hidden_ref.shape
     odd = lax.rem(me_ref[0], 2) == 1
     rows = depth // pieces
+    columns = q_all.shape[1]
     copies = [
         pltpu.make_async_copy(
-            q_hbm.at[pl.ds(i * rows, rows), :], q_all.at[pl.ds(i * rows, rows), :], sems.at[i]
+            weight_refs[0].at[pl.ds(i * rows, rows), pl.ds(chunk * columns, columns)],
+            q_all.at[pl.ds(i * rows, rows), :],
+            sems.at[i],
         )
         for i in range(pieces)
     ]
-    copies.append(pltpu.make_async_copy(k_hbm, k_all, sems.at[pieces]))
-    copies.append(pltpu.make_async_copy(v_hbm, v_all, sems.at[pieces + 1]))
+    for i in range(extra):
+        copies.append(
+            pltpu.make_async_copy(weight_refs[1 + i], others_all[i], sems.at[pieces + i])
+        )
     for copy in copies:
         copy.start()
 
-    def deal(product, chunk, kind):
+    def deal(product, kind):
         block = blocks[kind]
         first = kind * blocks[0]
         parts = [
@@ -103,61 +108,50 @@
             for c in range(product.shape[1] // LANES)
             for e in range(tokens // block)
         ]
-        keep_ref, send_ref = outs[2 * chunk : 2 * chunk + 2]
         for i, (even_part, odd_part) in enumerate(zip(parts[0::2], parts[1::2])):
             keep_ref[i, first : first + block, :] = jnp.where(odd, odd_part, even_part)
             send_ref[i, first : first + block, :] = jnp.where(odd, even_part, odd_part)
 
-    columns = q_all.shape[1] // chunks
+    total = None
     for i in range(pieces):
         copies[i].wait()
-        h = hidden_ref[:, i * rows : (i + 1) * rows]
-        for j in range(chunks):
-            w = q_all[i * rows : (i + 1) * rows, j * columns : (j + 1) * columns]
-            product = jnp.dot(h, w, preferred_element_type=jnp.float32)
-            if i > 0:
-                product = product + total[j]
-            if i < pieces - 1:
-                total[j] = product
-            else:
-                deal(product, j, 0)
-    copies[pieces].wait()
-    copies[pieces + 1].wait()
-    both = [
-        jnp.dot(hidden_ref[...], w_all[...], preferred_element_type=jnp.float32)
-        for w_all in (k_all, v_all)
-    ]
-    deal(jnp.concatenate(both, axis=1), chunks - 1, 1)
-
-
-def project(me, hidden, query_weight, key_weight, value_weight, chunks, count):
+        here = slice(i * rows, (i + 1) * rows)
+        term = jnp.dot(hidden_ref[:, here], q_all[here, :], preferred_element_type=jnp.float32)
+        total = term if total is None else total + term
+    deal(total, 0)
+    if extra:
+        both = []
+        for i in range(extra):
+            copies[pieces + i].wait()
+            both.append(
+                jnp.dot(hidden_ref[...], others_all[i][...], preferred_element_type=jnp.float32)
+            )
+        deal(jnp.concatenate(both, axis=1), 1)
+
+
+def project(me, hidden, query_weight, others, chunk, columns, count):
     tokens, depth = hidden.shape
-    wide, narrow = query_weight.shape[1], key_weight.shape[1]
+    wide = columns + sum(other.shape[1] for other in others)
     pieces = max(1, depth // 256)
-    blocks = (wide // chunks // LANES * tokens // count, 2 * narrow // LANES * tokens // count)
-    shapes = []
-    for j in range(chunks):
-        rows = blocks[0] + (blocks[1] if j == chunks - 1 else 0)
-        shapes += [jax.ShapeDtypeStruct((count // 2, rows, LANES), jnp.float32)] * 2
+    blocks = [width // LANES * tokens // count for width in (columns, wide - columns)]
+    shape = jax.ShapeDtypeStruct((count // 2, sum(blocks), LANES), jnp.float32)
     return pl.pallas_call(
-        functools.partial(project_kernel, chunks=chunks, blocks=blocks, pieces=pieces),
-        out_shape=shapes,
-        in_specs=[smem_spec(), vmem_spec()] + [hbm_spec()] * 3,
-        out_specs=[vmem_spec()] * len(shapes),
-        scratch_shapes=[
-            pltpu.VMEM((depth, wide), jnp.bfloat16),
-            pltpu.VMEM((depth, narrow), jnp.bfloat16),
-            pltpu.VMEM((depth, narrow), jnp.bfloat16),
-            pltpu.VMEM((chunks, tokens, wide // chunks), jnp.float32),
-            pltpu.SemaphoreType.DMA((pieces + 2,)),
-        ],
+        functools.partial(
+            project_kernel, extra=len(others), chunk=chunk, blocks=blocks, pieces=pieces
+        ),
+        out_shape=[shape] * 2,
+        in_specs=[smem_spec(), vmem_spec()] + [hbm_spec()] * (1 + len(others)),
+        out_specs=[vmem_spec()] * 2,
+        scratch_shapes=[pltpu.VMEM((depth, columns), jnp.bfloat16)]
+        + [pltpu.VMEM(other.shape, jnp.bfloat16) for other in others]
+        + [pltpu.SemaphoreType.DMA((pieces + len(others),))],
         compiler_params=pltpu.CompilerParams(vmem_limit_bytes=PROJECT_GRANT),
         cost_estimate=pl.CostEstimate(
-            flops=2 * tokens * depth * (wide + 2 * narrow),
-            bytes_accessed=2 * depth * (wide + 2 * narrow),
+            flops=2 * tokens * depth * wide,
+            bytes_accessed=2 * depth * wide,
             transcendentals=0,
         ),
-    )(me, hidden, query_weight, key_weight, value_weight)
+    )(me, hidden, query_weight, *others)
 
 
 def attention_kernel(len_ref, me_ref, *refs, sources, band, step, block, head):
@@ -328,29 +322,46 @@
     )(length, me, *queries, keys, values)
 
 
-def merge_kernel(me_ref, part_ref, q_ref, last_ref, copies_ref, turned, kv_all, *, block, tokens, head):
-    count = part_ref.shape[0]
-    per = LANES // block
+def fresh_kernel(me_ref, q_ref, last_ref, out_ref, stat_ref, kv_all, *, block, tokens, head):
     kv_block = last_ref.shape[1] - block
-    scale = math.log2(math.e) / math.sqrt(HD)
-
-    for k in range(count):
+    for k in range(last_ref.shape[0]):
         rows = last_ref[k, block:, :].astype(jnp.float32)
         kv_all[k * kv_block : (k + 1) * kv_block, :] = rows
     half = kv_all.shape[0] // 2
     keys = kv_all[head * tokens : (head + 1) * tokens, :].astype(jnp.bfloat16)
     values = kv_all[half + head * tokens : half + (head + 1) * tokens, :].astype(jnp.bfloat16)
 
-    s = lax.dot_general(q_ref[0, :block, :], keys, NT, preferred_element_type=jnp.float32) * scale
+    s = lax.dot_general(q_ref[0, :block, :], keys, NT, preferred_element_type=jnp.float32)
+    s = s * (math.log2(math.e) / math.sqrt(HD))
     token = lax.rem(me_ref[0] * block, tokens) + lax.broadcasted_iota(jnp.int32, s.shape, 0)
     visible = lax.broadcasted_iota(jnp.int32, s.shape, 1) <= token
     s = jnp.where(visible, s, NEG_BIG)
-    new_top = jnp.max(s, axis=1, keepdims=True)
-    weights = jnp.where(visible, jnp.exp2(s - new_top), 0.0).astype(jnp.bfloat16)
-    new_total = jnp.sum(weights.astype(jnp.float32), axis=1, keepdims=True)
-    new_out = jnp.dot(weights, values, preferred_element_type=jnp.float32)
-
-    place = lax.rem(me_ref[0], per)
+    top = jnp.max(s, axis=1, keepdims=True)
+    weights = jnp.where(visible, jnp.exp2(s - top), 0.0).astype(jnp.bfloat16)
+    total = jnp.sum(weights.astype(jnp.float32), axis=1, keepdims=True)
+    out_ref[...] = jnp.dot(weights, values, preferred_element_type=jnp.float32)
+    lane = lax.broadcasted_iota(jnp.int32, stat_ref.shape, 1)
+    stat_ref[...] = jnp.where(lane < LANES // 2, top, total)
+
+
+def fresh(me, mine, last, block, tokens, head):
+    kv_rows = last.shape[0] * (last.shape[1] - block)
+    return pl.pallas_call(
+        functools.partial(fresh_kernel, block=block, tokens=tokens, head=head),
+        out_shape=[jax.ShapeDtypeStruct((block, HD), jnp.float32)] * 2,
+        in_specs=[smem_spec()] + [vmem_spec()] * 2,
+        out_specs=[vmem_spec()] * 2,
+        scratch_shapes=[pltpu.VMEM((kv_rows, HD), jnp.float32)],
+    )(me, mine, last)
+
+
+def merge_kernel(me_ref, part_ref, out_ref, stat_ref, copies_ref, turned):
+    count = part_ref.shape[0]
+    block = out_ref.shape[0]
+    new_top = stat_ref[:, 0:1]
+    new_total = stat_ref[:, LANES // 2 : LANES // 2 + 1]
+
+    place = lax.rem(me_ref[0], LANES // block)
     pieces = part_ref[:, block : block + 4, :]
     level = pieces[:, 1, :] * 2.0**-9 + pieces[:, 2, :] * 2.0**-20 + pieces[:, 3, :] * 2.0**-31
     turned[...] = (level * jnp.exp2(pieces[:, 0, :])).T
@@ -358,34 +369,32 @@
     joint = jnp.maximum(new_top, jnp.max(levels, axis=1, keepdims=True))
     factors = jnp.exp2(levels - joint)
     new_scale = jnp.exp2(new_top - joint)
-    whole_out = new_out * new_scale
+    whole_out = out_ref[...] * new_scale
     whole_total = new_total * new_scale + jnp.sum(factors, axis=1, keepdims=True)
     scaled = factors * (1.0 / OUTPUT_SCALE)
     for k in range(count):
         whole_out = whole_out + part_ref[k, :block, :] * scaled[:, k : k + 1]
     attended = (whole_out / whole_total).astype(jnp.bfloat16)
-    for k in range(count):
+    for k in range(copies_ref.shape[0]):
         copies_ref[k] = attended
 
 
-def merge(me, parts, mine, last, block, tokens, head):
-    count = parts.shape[0]
-    kv_rows = count * (last.shape[1] - block)
+def merge(me, parts, new_out, new_stat, copies):
     return pl.pallas_call(
-        functools.partial(merge_kernel, block=block, tokens=tokens, head=head),
-        out_shape=jax.ShapeDtypeStruct((count, block, HD), jnp.bfloat16),
+        merge_kernel,
+        out_shape=jax.ShapeDtypeStruct((copies,) + new_out.shape, jnp.bfloat16),
         in_specs=[smem_spec()] + [vmem_spec()] * 3,
         out_specs=vmem_spec(),
-        scratch_shapes=[
-            pltpu.VMEM((LANES, count), jnp.float32),
-            pltpu.VMEM((kv_rows, HD), jnp.float32),
-        ],
-    )(me, parts, mine, last)
-
-
-def output_kernel(place_ref, w_hbm, a_ref, *refs, tokens, groups, chunk, has_before, last):
+        scratch_shapes=[pltpu.VMEM((LANES, parts.shape[0]), jnp.float32)],
+    )(me, parts, new_out, new_stat)
+
+
+def output_kernel(
+    me_ref, place_ref, w_hbm, *refs, sources, tokens, groups, chunk, has_before, last
+):
+    a_refs, refs = refs[:sources], refs[sources:]
     before = refs[0] if has_before else None
-    outs, (w_all, total, sems) = refs[int(has_before) : -3], refs[-3:]
+    outs, (w_all, a_all, total, sems) = refs[int(has_before) : -4], refs[-4:]
     copies = []
     for g in range(groups):
         copies.append(
@@ -396,8 +405,16 @@
             )
         )
         copies[-1].start()
-    per = a_ref.shape[0] // groups
-    pieces = [a_ref[g * per : (g + 1) * per].reshape(tokens, HD) for g in range(groups)]
+    half, block = a_refs[0].shape[:2]
+    per = sources * half // groups
+    if sources == 1:
+        pieces = [a_refs[0][g * per : (g + 1) * per].reshape(tokens, HD) for g in range(groups)]
+    else:
+        for k, offset in enumerate(doubling_offsets(sources * half)):
+            owner = me_ref[0] ^ offset
+            start = pl.multiple_of(lax.rem(owner, per) * block, block)
+            a_all[owner // per, pl.ds(start, block), :] = a_refs[k // half][k % half]
+        pieces = [a_all[g] for g in range(groups)]
     product = before[...] if has_before else None
     for g in range(0, groups, 2):
         copies[g].wait()
@@ -421,7 +438,7 @@
             ref[i] = total[pl.ds(start, share), :]
 
 
-def output_part(place, weight, attended, tokens, before, chunk, heads, last):
+def output_part(me, place, weight, attended, tokens, before, chunk, heads, last):
     groups = QH // KVH
     width = weight.shape[1]
     has_before = before is not None
@@ -431,6 +448,7 @@
     return pl.pallas_call(
         functools.partial(
             output_kernel,
+            sources=len(attended),
             tokens=tokens,
             groups=groups,
             chunk=chunk,
@@ -438,10 +456,13 @@
             last=last,
         ),
         out_shape=shapes,
-        in_specs=[smem_spec(), hbm_spec()] + [vmem_spec()] * (1 + int(has_before)),
+        in_specs=[smem_spec()] * 2
+        + [hbm_spec()]
+        + [vmem_spec()] * (len(attended) + int(has_before)),
         out_specs=[vmem_spec()] * len(shapes),
         scratch_shapes=[
             pltpu.VMEM((groups * HD, width), jnp.bfloat16),
+            pltpu.VMEM((groups, tokens, HD), jnp.bfloat16),
             pltpu.VMEM((tokens, width), jnp.float32),
             pltpu.SemaphoreType.DMA((groups,)),
         ],
@@ -451,7 +472,7 @@
             bytes_accessed=2 * groups * HD * width,
             transcendentals=0,
         ),
-    )(place, weight, attended, *([before] if has_before else []))
+    )(me, place, weight, *attended, *([before] if has_before else []))
 
 
 def shards(
@@ -468,28 +489,33 @@
     count = lax.axis_size("seq")
     heads = lax.axis_size("head")
     kv_local = cache_keys.shape[1] // HD
+    columns = (QH // KVH) * HD
     block = (QH // KVH) * tokens // count
     me = lax.axis_index("seq").reshape(1)
     place = lax.axis_index("head").reshape(1)
 
-    halves = project(me, hidden, query_weight, key_weight, value_weight, kv_local, count)
     mine, queries = [], []
     for j in range(kv_local):
-        mine.append(owners_sum(halves[2 * j], halves[2 * j + 1], me[0]))
-        if j < kv_local - 1:
-            queries.append(gather_doubling(mine[j]))
-        else:
+        last = j == kv_local - 1
+        others = [key_weight, value_weight] if last else []
+        keep, send = project(me, hidden, query_weight, others, j, columns, count)
+        mine.append(owners_sum(keep, send, me[0]))
+        if last:
             copies = jnp.broadcast_to(mine[j], (count,) + mine[j].shape[1:])
             queries.append([gather_at_once(copies)])
+        else:
+            queries.append(gather_doubling(mine[j]))
 
     mixed = None
     for j in range(kv_local):
+        last = j == kv_local - 1
         parts = attention(queries[j], block, cache_keys, cache_values, cache_lens, me, j)
         parts = lax.all_to_all(parts.astype(jnp.float16), "seq", 0, 0).astype(jnp.float32)
-        copies = merge(me, parts, mine[j], queries[-1][0], block, tokens, j)
-        last = j == kv_local - 1
+        new_out, new_stat = fresh(me, mine[j], queries[-1][0], block, tokens, j)
+        copies = merge(me, parts, new_out, new_stat, count if last else 1)
+        attended = [gather_at_once(copies)] if last else gather_doubling(copies)
         result = output_part(
-            place, output_weight, gather_at_once(copies), tokens, mixed, j, heads, last
+            me, place, output_weight, attended, tokens, mixed, j, heads, last
         )
         mixed = result if last else result[0]
 

time: 129 us -> 129 us (level); the launches traced: 127 us -> 129 us
  Pallas kernels: 28.8 us -> 45.9 us
  waiting for transfers between devices: 39.1 us -> 27.8 us
  starting transfers between devices: 51.4 us -> 46 us
  other arithmetic: 6.01 us -> 7.6 us
    all_to_all x3 -> x2, waiting for transfers between devices: 12 us -> 0.01 us  [gather_at_once(): return lax.all_to_all(copies, 'seq', 0, 0)]
    pallas_call x2, Pallas kernels: 14.6 us -> 25.4 us  [attention(): pl.pallas_call(functools.partial(attention_kernel, sources=sources, band=...]
    all_to_all x2, starting transfers between devices: 19.6 us -> 11.9 us  [shards(): lax.all_to_all(parts.astype(jnp.float16), 'seq', 0, 0).astype(jnp.float32)]
    ppermute x11 -> x14, starting transfers between devices: 20.2 us -> 27 us  [swap(): return lax.ppermute(array, axis, [(i, i ^ mask) for i in range(size)])]
    pallas_call x5 -> x8, Pallas kernels: 14.2 us -> 20.5 us  [the longest x2 7.79 us: project(): pl.pallas_call(functools.partial(project_kernel, extra=len(others), chunk...]
    ppermute x11 -> x14, waiting for transfers between devices: 22.2 us -> 27.8 us  [swap(): return lax.ppermute(array, axis, [(i, i ^ mask) for i in range(size)])]
    all_to_all x2, waiting for transfers between devices: 4.91 us -> 0.01 us  [shards(): lax.all_to_all(parts.astype(jnp.float16), 'seq', 0, 0).astype(jnp.float32)]
    all_to_all x3 -> x2, starting transfers between devices: 11.6 us -> 7.09 us  [gather_at_once(): return lax.all_to_all(copies, 'seq', 0, 0)]
  transfers between devices with their start and end apart: 16 -> 18, of which waited for: 13 -> 9; matrix products, arithmetic and copies ran while one was open for 4% -> 5% of each run, Pallas kernels for 17% -> 31%
where the time goes in v5:
time: 129 us
  starting transfers between devices  46 us (36%)
  Pallas kernels  45.9 us (36%)
  waiting for transfers between devices  27.8 us (22%)
  other arithmetic  7.6 us (6%)
    ppermute x14, waiting for transfers between devices, swap(): return lax.ppermute(array, axis, [(i, i ^ mask) for i in range(size)])  27.8 us
    ppermute x14, starting transfers between devices, swap(): return lax.ppermute(array, axis, [(i, i ^ mask) for i in range(size)])  27 us
    pallas_call x2, Pallas kernels, attention(): pl.pallas_call(functools.partial(attention_kernel, sources=sources, band=...  25.4 us
    all_to_all x2, starting transfers between devices, shards(): lax.all_to_all(parts.astype(jnp.float16), 'seq', 0, 0).astype(jnp.float32)  11.9 us
    pallas_call x2, Pallas kernels, project(): pl.pallas_call(functools.partial(project_kernel, extra=len(others), chunk...  7.79 us
    all_to_all x2, starting transfers between devices, gather_at_once(): return lax.all_to_all(copies, 'seq', 0, 0)  7.09 us
    pallas_call x2, Pallas kernels, merge(): pl.pallas_call(merge_kernel, out_shape=jax.ShapeDtypeStruct((copies,) + n...  4.97 us
    pallas_call x2, Pallas kernels, fresh(): pl.pallas_call(functools.partial(fresh_kernel, block=block, tokens=tokens...  4.03 us
  transfers between devices with their start and end apart: 18, of which 9 were waited for; matrix products, arithmetic and copies ran while one was open for 5% of the time, Pallas kernels for 31%

profile of v5, /device:TPU:0, one launch (start us, length us, event | category | flops | bytes accessed | tf_op | source)
XLA Modules:
  0.0 129.1 jit_solution(7500414973747970816)
XLA Ops:
  0.0 3.6 %shard_map.86 = (f32[4,128,128]{2,1,0:T(8,128)}, f32[4,128,128]{2,1,0:T(8,128)}) custom-call(s32[1]{0:T(128)} %bitcast.me_ref, bf16[128,1024]{1,0:T(8,128)(2,1)} %hidden_ref.3, bf16[1024,2048]{1,0:T(8,128)(2,1)} %refs_0_.3), custom_call_target="tpu_custom_call" | custom-call | flops 268435456 | bytes 2097152 | tf_op jit(solution)/shard_map/pallas_call | solution.py:138
  3.6 3.0 %collective-permute-start.3 = (f32[4,128,128]{2,1,0:T(8,128)}, f32[4,128,128]{2,1,0:T(8,128)S(1)}, u32[]{:S(2)}, u32[]{:S(2)}) collective-permute-start(f32[4,128,128]{2,1,0:T(8,128)} %get-tuple-element.20), channel_id=1, source_target_pairs={{0,4},{4,0},{8,12},{12,8},{16,20},{20,16},{24,28},{28,24},{1,5},{5... | collective-permute-start | bytes 786440 | tf_op jit(solution)/shard_map/ppermute | solution.py:40
  6.6 6.5 %collective-permute-done.3 = f32[4,128,128]{2,1,0:T(8,128)S(1)} collective-permute-done((f32[4,128,128]{2,1,0:T(8,128)}, f32[4,128,128]{2,1,0:T(8,128)S(1)}, u32[]{:S(2)}, u32[]{:S(2)}) %collective-permute-start.3) | collective-permute-done | bytes 262176 | tf_op jit(solution)/shard_map/ppermute | solution.py:40
  13.1 1.0 add.78
  14.1 1.9 %collective-permute-start.4 = (f32[2,128,128]{2,1,0:T(8,128)S(1)}, f32[2,128,128]{2,1,0:T(8,128)S(1)}, u32[]{:S(2)}, u32[]{:S(2)}) collective-permute-start(f32[2,128,128]{2,1,0:T(8,128)S(1)} %dynamic-slice_bitcast_fusion.1), channel_id=1, source_target_pairs={{0,8},{4,12},{8,0},{12,4},{16,24},{20,28},{24,16},{28,20},{1,9},{5... | collective-permute-start | bytes 393224 | tf_op jit(solution)/shard_map/ppermute | solution.py:40
  16.0 4.2 %shard_map.82 = (f32[4,192,128]{2,1,0:T(8,128)}, f32[4,192,128]{2,1,0:T(8,128)}) custom-call(s32[1]{0:T(128)} %bitcast.me_ref, bf16[128,1024]{1,0:T(8,128)(2,1)} %hidden_ref.3, bf16[1024,2048]{1,0:T(8,128)(2,1)} %refs_0_.3, bf16[1024,256]{1,0:T(8,128)(2,1)} %refs_1_.2, bf16[1024,256]{1,0:T(8,128)(2,1)} %refs_2_.3), custom_call_target="tpu_custom_call" | custom-call | flops 402653184 | bytes 3145728 | tf_op jit(solution)/shard_map/pallas_call | solution.py:138
  20.2 1.6 %collective-permute-start = (f32[4,192,128]{2,1,0:T(8,128)}, f32[4,192,128]{2,1,0:T(8,128)S(1)}, u32[]{:S(2)}, u32[]{:S(2)}) collective-permute-start(f32[4,192,128]{2,1,0:T(8,128)} %get-tuple-element.16), channel_id=1, source_target_pairs={{0,4},{4,0},{8,12},{12,8},{16,20},{20,16},{24,28},{28,24},{1,5},{5... | collective-permute-start | bytes 1179656 | tf_op jit(solution)/shard_map/ppermute | solution.py:40
  21.8 0.0 collective-permute-done.4
  21.8 2.7 %collective-permute-start.5 = (f32[1,128,128]{2,1,0:T(8,128)S(1)}, f32[1,128,128]{2,1,0:T(8,128)S(1)}, u32[]{:S(2)}, u32[]{:S(2)}) collective-permute-start(f32[1,128,128]{2,1,0:T(8,128)S(1)} %constant_dynamic-slice_fusion), channel_id=1, source_target_pairs={{0,16},{4,20},{8,24},{12,28},{16,0},{20,4},{24,8},{28,12},{1,17},{... | collective-permute-start | bytes 196616 | tf_op jit(solution)/shard_map/ppermute | solution.py:40
  24.5 5.7 %collective-permute-done = f32[4,192,128]{2,1,0:T(8,128)S(1)} collective-permute-done((f32[4,192,128]{2,1,0:T(8,128)}, f32[4,192,128]{2,1,0:T(8,128)S(1)}, u32[]{:S(2)}, u32[]{:S(2)}) %collective-permute-start) | collective-permute-done | bytes 393248 | tf_op jit(solution)/shard_map/ppermute | solution.py:40
  30.2 1.0 add.69
  31.3 0.6 collective-permute-start.1
  31.9 2.6 %collective-permute-start.6 = (bf16[1,128,128]{2,1,0:T(8,128)(2,1)S(1)}, bf16[1,128,128]{2,1,0:T(8,128)(2,1)S(1)}, u32[]{:S(2)}, u32[]{:S(2)}) collective-permute-start(bf16[1,128,128]{2,1,0:T(8,128)(2,1)S(1)} %add_convert_fusion.2.q_ref), channel_id=1, source_target_pairs={{0,16},{4,20},{8,24},{12,28},{16,0},{20,4},{24,8},{28,12},{1,17},{... | collective-permute-start | bytes 98312 | tf_op jit(solution)/shard_map/ppermute | solution.py:40
  35.1 1.8 %collective-permute-done.6 = bf16[1,128,128]{2,1,0:T(8,128)(2,1)S(1)} collective-permute-done((bf16[1,128,128]{2,1,0:T(8,128)(2,1)S(1)}, bf16[1,128,128]{2,1,0:T(8,128)(2,1)S(1)}, u32[]{:S(2)}, u32[]{:S(2)}) %collective-permute-start.6) | collective-permute-done | bytes 32800 | tf_op jit(solution)/shard_map/ppermute | solution.py:40
  36.9 4.2 %collective-permute-start.7 = (bf16[2,128,128]{2,1,0:T(8,128)(2,1)S(1)}, bf16[2,128,128]{2,1,0:T(8,128)(2,1)S(1)}, u32[]{:S(2)}, u32[]{:S(2)}) collective-permute-start(bf16[2,128,128]{2,1,0:T(8,128)(2,1)S(1)} %pad_maximum_fusion.2), channel_id=1, source_target_pairs={{0,8},{4,12},{8,0},{12,4},{16,24},{20,28},{24,16},{28,20},{1,9},{5... | collective-permute-start | bytes 196616 | tf_op jit(solution)/shard_map/ppermute | solution.py:40
  41.1 0.3 collective-permute-start.2
  41.4 1.9 %collective-permute-done.7 = bf16[2,128,128]{2,1,0:T(8,128)(2,1)S(1)} collective-permute-done((bf16[2,128,128]{2,1,0:T(8,128)(2,1)S(1)}, bf16[2,128,128]{2,1,0:T(8,128)(2,1)S(1)}, u32[]{:S(2)}, u32[]{:S(2)}) %collective-permute-start.7) | collective-permute-done | bytes 65568 | tf_op jit(solution)/shard_map/ppermute | solution.py:40
  43.4 1.6 %collective-permute-start.8 = (bf16[4,128,128]{2,1,0:T(8,128)(2,1)S(1)}, bf16[4,128,128]{2,1,0:T(8,128)(2,1)S(1)}, u32[]{:S(2)}, u32[]{:S(2)}) collective-permute-start(bf16[4,128,128]{2,1,0:T(8,128)(2,1)S(1)} %pad_maximum_fusion.refs_0_), channel_id=1, source_target_pairs={{0,4},{4,0},{8,12},{12,8},{16,20},{20,16},{24,28},{28,24},{1,5},{5... | collective-permute-start | bytes 393224 | tf_op jit(solution)/shard_map/ppermute | solution.py:40
  44.9 2.3 %collective-permute-done.2 = f32[1,192,128]{2,1,0:T(8,128)S(1)} collective-permute-done((f32[1,192,128]{2,1,0:T(8,128)S(1)}, f32[1,192,128]{2,1,0:T(8,128)S(1)}, u32[]{:S(2)}, u32[]{:S(2)}) %collective-permute-start.2) | collective-permute-done | bytes 98336 | tf_op jit(solution)/shard_map/ppermute | solution.py:40
  47.3 0.8 broadcast_in_dim.8
  48.1 3.5 %all-to-all-start = ((bf16[8,192,128]{2,1,0:T(8,128)(2,1)}), bf16[8,192,128]{2,1,0:T(8,128)(2,1)S(1)}, u32[]{:S(2)}, u32[]{:S(2)}) async-start(bf16[8,192,128]{2,1,0:T(8,128)(2,1)} %broadcast_in_dim.8), calls=%async_computation | async-start | bytes 786432 | tf_op jit(solution)/shard_map/all_to_all | solution.py:78
  51.5 12.7 %shard_map.87 = f32[8,136,128]{2,1,0:T(8,128)S(1)} custom-call(s32[1]{0:T(128)S(6)} %copy.17.len_ref, s32[1]{0:T(128)} %bitcast.me_ref, bf16[4,128,128]{2,1,0:T(8,128)(2,1)S(1)} %pad_maximum_fusion.refs_0_, bf16[4,128,128]{2,1,0:T(8,128)(2,1)S(1)} %collective-permute-done.8.refs_1_, bf16[8192,256]{1,0:T(8,128)(2,1)} %refs_2_.5, bf16[8192,256]{1,0:T(8,128)(2,1)} %refs_3_.1), custom_call_target="tpu_custom_call" | custom-call | flops 8589934592 | bytes 4194304 | tf_op jit(solution)/shard_map/pallas_call | solution.py:297
  64.2 0.8 convert_element_type.36
  65.0 5.9 %all-to-all-start.3 = ((f16[8,136,128]{2,1,0:T(8,128)(2,1)}), f16[8,136,128]{2,1,0:T(8,128)(2,1)S(1)}, u32[]{:S(2)}, u32[]{:S(2)}) async-start(f16[8,136,128]{2,1,0:T(8,128)(2,1)} %convert_element_type.36), calls=%async_computation.3 | async-start | bytes 557056 | tf_op jit(solution)/shard_map/all_to_all | solution.py:513
  70.9 12.8 %shard_map.83 = f32[8,136,128]{2,1,0:T(8,128)S(1)} custom-call(s32[1]{0:T(128)S(6)} %copy.17.len_ref, s32[1]{0:T(128)} %bitcast.me_ref, bf16[8,192,128]{2,1,0:T(8,128)(2,1)S(1)} %all-to-all-done.refs_0_.last_ref, bf16[8192,256]{1,0:T(8,128)(2,1)} %refs_2_.5, bf16[8192,256]{1,0:T(8,128)(2,1)} %refs_3_.1), custom_call_target="tpu_custom_call" | custom-call | flops 8589934592 | bytes 4194304 | tf_op jit(solution)/shard_map/pallas_call | solution.py:297
  83.7 0.7 convert_element_type.33
  84.4 6.0 %all-to-all-start.1 = ((f16[8,136,128]{2,1,0:T(8,128)(2,1)}), f16[8,136,128]{2,1,0:T(8,128)(2,1)S(1)}, u32[]{:S(2)}, u32[]{:S(2)}) async-start(f16[8,136,128]{2,1,0:T(8,128)(2,1)} %convert_element_type.33), calls=%async_computation.1 | async-start | bytes 557056 | tf_op jit(solution)/shard_map/all_to_all | solution.py:513
  90.4 0.9 convert_element_type.37.part_ref
  91.3 2.0 %shard_map.88 = (f32[128,128]{1,0:T(8,128)}, f32[128,128]{1,0:T(8,128)}) custom-call(s32[1]{0:T(128)} %bitcast.me_ref, bf16[1,128,128]{2,1,0:T(8,128)(2,1)} %copy-done.1, bf16[8,192,128]{2,1,0:T(8,128)(2,1)} %copy-done), custom_call_target="tpu_custom_call" | custom-call | tf_op jit(solution)/shard_map/pallas_call | solution.py:349
  93.3 2.4 %shard_map.89 = bf16[1,128,128]{2,1,0:T(8,128)(2,1)} custom-call(s32[1]{0:T(128)} %bitcast.me_ref, f32[8,136,128]{2,1,0:T(8,128)} %convert_element_type.37.part_ref, f32[128,128]{1,0:T(8,128)} %get-tuple-element.21.out_ref, f32[128,128]{1,0:T(8,128)} %get-tuple-element.22.stat_ref), custom_call_target="tpu_custom_call" | custom-call | tf_op jit(solution)/shard_map/pallas_call | solution.py:383
  95.8 2.9 %collective-permute-start.9 = (bf16[1,128,128]{2,1,0:T(8,128)(2,1)}, bf16[1,128,128]{2,1,0:T(8,128)(2,1)S(1)}, u32[]{:S(2)}, u32[]{:S(2)}) collective-permute-start(bf16[1,128,128]{2,1,0:T(8,128)(2,1)} %shard_map.89), channel_id=1, source_target_pairs={{0,16},{4,20},{8,24},{12,28},{16,0},{20,4},{24,8},{28,12},{1,17},{... | collective-permute-start | bytes 98312 | tf_op jit(solution)/shard_map/ppermute | solution.py:40
  98.7 2.0 %shard_map.84 = (f32[128,128]{1,0:T(8,128)}, f32[128,128]{1,0:T(8,128)}) custom-call(s32[1]{0:T(128)} %bitcast.me_ref, bf16[1,192,128]{2,1,0:T(8,128)(2,1)} %copy-done.2, bf16[8,192,128]{2,1,0:T(8,128)(2,1)} %copy-done), custom_call_target="tpu_custom_call" | custom-call | tf_op jit(solution)/shard_map/pallas_call | solution.py:349
  100.7 0.9 convert_element_type.34.part_ref
  101.6 2.5 %shard_map.85 = bf16[8,128,128]{2,1,0:T(8,128)(2,1)} custom-call(s32[1]{0:T(128)} %bitcast.me_ref, f32[8,136,128]{2,1,0:T(8,128)} %convert_element_type.34.part_ref, f32[128,128]{1,0:T(8,128)} %get-tuple-element.17.out_ref, f32[128,128]{1,0:T(8,128)} %get-tuple-element.18.stat_ref), custom_call_target="tpu_custom_call" | custom-call | tf_op jit(solution)/shard_map/pallas_call | solution.py:383
  104.1 3.6 %all-to-all-start.2 = ((bf16[8,128,128]{2,1,0:T(8,128)(2,1)}), bf16[8,128,128]{2,1,0:T(8,128)(2,1)S(1)}, u32[]{:S(2)}, u32[]{:S(2)}) async-start(bf16[8,128,128]{2,1,0:T(8,128)(2,1)} %shard_map.85), calls=%async_computation.2 | async-start | bytes 524288 | tf_op jit(solution)/shard_map/all_to_all | solution.py:78
  107.8 0.8 pad_maximum_fusion.3
  108.5 2.0 %collective-permute-start.10 = (bf16[2,128,128]{2,1,0:T(8,128)(2,1)S(1)}, bf16[2,128,128]{2,1,0:T(8,128)(2,1)S(1)}, u32[]{:S(2)}, u32[]{:S(2)}) collective-permute-start(bf16[2,128,128]{2,1,0:T(8,128)(2,1)S(1)} %pad_maximum_fusion.3), channel_id=1, source_target_pairs={{0,8},{4,12},{8,0},{12,4},{16,24},{20,28},{24,16},{28,20},{1,9},{5... | collective-permute-start | bytes 196616 | tf_op jit(solution)/shard_map/ppermute | solution.py:40
  110.5 2.4 %collective-permute-done.10 = bf16[2,128,128]{2,1,0:T(8,128)(2,1)S(1)} collective-permute-done((bf16[2,128,128]{2,1,0:T(8,128)(2,1)S(1)}, bf16[2,128,128]{2,1,0:T(8,128)(2,1)S(1)}, u32[]{:S(2)}, u32[]{:S(2)}) %collective-permute-start.10) | collective-permute-done | bytes 65568 | tf_op jit(solution)/shard_map/ppermute | solution.py:40
  112.9 0.8 pad_maximum_fusion.1.refs_0_
  113.7 2.1 %collective-permute-start.11 = (bf16[4,128,128]{2,1,0:T(8,128)(2,1)S(1)}, bf16[4,128,128]{2,1,0:T(8,128)(2,1)S(1)}, u32[]{:S(2)}, u32[]{:S(2)}) collective-permute-start(bf16[4,128,128]{2,1,0:T(8,128)(2,1)S(1)} %pad_maximum_fusion.1.refs_0_), channel_id=1, source_target_pairs={{0,4},{4,0},{8,12},{12,8},{16,20},{20,16},{24,28},{28,24},{1,5},{5... | collective-permute-start | bytes 393224 | tf_op jit(solution)/shard_map/ppermute | solution.py:40
  115.8 3.0 %collective-permute-done.11.refs_1_ = bf16[4,128,128]{2,1,0:T(8,128)(2,1)S(1)} collective-permute-done((bf16[4,128,128]{2,1,0:T(8,128)(2,1)S(1)}, bf16[4,128,128]{2,1,0:T(8,128)(2,1)S(1)}, u32[]{:S(2)}, u32[]{:S(2)}) %collective-permute-start.11) | collective-permute-done | bytes 131104 | tf_op jit(solution)/shard_map/ppermute | solution.py:40
  118.7 1.8 %shard_map.90.refs_1_ = f32[128,1024]{1,0:T(8,128)S(1)} custom-call(s32[1]{0:T(128)} %bitcast.me_ref, s32[1]{0:T(128)} %bitcast.1.place_ref, bf16[2048,1024]{1,0:T(8,128)(2,1)} %w_hbm.3, bf16[4,128,128]{2,1,0:T(8,128)(2,1)S(1)} %pad_maximum_fusion.1.refs_0_, bf16[4,128,128]{2,1,0:T(8,128)(2,1)S(1)} %collective-permute-done.11.refs_1_), custom_call_target="tpu_custom_call" | custom-call | flops 268435456 | bytes 2097152 | tf_op jit(solution)/shard_map/pallas_call | solution.py:448
  120.6 1.9 %shard_map.91 = (f32[2,32,1024]{2,1,0:T(8,128)S(1)}, f32[2,32,1024]{2,1,0:T(8,128)S(1)}) custom-call(s32[1]{0:T(128)} %bitcast.me_ref, s32[1]{0:T(128)} %bitcast.1.place_ref, bf16[2048,1024]{1,0:T(8,128)(2,1)} %w_hbm.3, bf16[8,128,128]{2,1,0:T(8,128)(2,1)S(1)} %all-to-all-done.2.refs_0_, f32[128,1024]{1,0:T(8,128)S(1)} %shard_map.90.refs_1_), custom_call_target="tpu_custom_call" | custom-call | flops 268435456 | bytes 2097152 | tf_op jit(solution)/shard_map/pallas_call | solution.py:448
  122.4 0.1 collective-permute-start.12
  122.6 1.5 %collective-permute-done.12 = f32[2,32,1024]{2,1,0:T(8,128)S(1)} collective-permute-done((f32[2,32,1024]{2,1,0:T(8,128)S(1)}, f32[2,32,1024]{2,1,0:T(8,128)S(1)}, u32[]{:S(2)}, u32[]{:S(2)}) %collective-permute-start.12) | collective-permute-done | bytes 262176 | tf_op jit(solution)/shard_map/ppermute | solution.py:40
  124.1 1.6 %collective-permute-start.13 = (f16[1,32,1024]{2,1,0:T(8,128)(2,1)S(1)}, f16[1,32,1024]{2,1,0:T(8,128)(2,1)S(1)}, u32[]{:S(2)}, u32[]{:S(2)}) collective-permute-start(f16[1,32,1024]{2,1,0:T(8,128)(2,1)S(1)} %multiply_convert_fusion), channel_id=1, source_target_pairs={{0,2},{1,3},{2,0},{3,1},{4,6},{5,7},{6,4},{7,5},{8,10},{9,11},{10,... | collective-permute-start | bytes 196616 | tf_op jit(solution)/shard_map/ppermute | solution.py:40
  125.7 2.7 %collective-permute-done.13 = f16[1,32,1024]{2,1,0:T(8,128)(2,1)S(1)} collective-permute-done((f16[1,32,1024]{2,1,0:T(8,128)(2,1)S(1)}, f16[1,32,1024]{2,1,0:T(8,128)(2,1)S(1)}, u32[]{:S(2)}, u32[]{:S(2)}) %collective-permute-start.13) | collective-permute-done | bytes 65568 | tf_op jit(solution)/shard_map/ppermute | solution.py:40
  128.4 0.6 fusion
  (26 shorter events, 0.2 us)
Async XLA Ops:
  3.6 9.5 %collective-permute-start.3 = (f32[4,128,128]{2,1,0:T(8,128)}, f32[4,128,128]{2,1,0:T(8,128)S(1)}, u32[]{:S(2)}, u32[]{:S(2)}) collective-permute-start(f32[4,128,128]{2,1,0:T(8,128)} %get-tuple-element.20), channel_id=1, source_target_pairs={{0,4},{4,0},{8,12},{12,8},{16,20},{20,16},{24,28},{28,24},{1,5},{5... | collective-permute-start | bytes 786440 | tf_op jit(solution)/shard_map/ppermute | solution.py:40
  14.1 7.7 %collective-permute-start.4 = (f32[2,128,128]{2,1,0:T(8,128)S(1)}, f32[2,128,128]{2,1,0:T(8,128)S(1)}, u32[]{:S(2)}, u32[]{:S(2)}) collective-permute-start(f32[2,128,128]{2,1,0:T(8,128)S(1)} %dynamic-slice_bitcast_fusion.1), channel_id=1, source_target_pairs={{0,8},{4,12},{8,0},{12,4},{16,24},{20,28},{24,16},{28,20},{1,9},{5... | collective-permute-start | bytes 393224 | tf_op jit(solution)/shard_map/ppermute | solution.py:40
  20.2 10.0 %collective-permute-start = (f32[4,192,128]{2,1,0:T(8,128)}, f32[4,192,128]{2,1,0:T(8,128)S(1)}, u32[]{:S(2)}, u32[]{:S(2)}) collective-permute-start(f32[4,192,128]{2,1,0:T(8,128)} %get-tuple-element.16), channel_id=1, source_target_pairs={{0,4},{4,0},{8,12},{12,8},{16,20},{20,16},{24,28},{28,24},{1,5},{5... | collective-permute-start | bytes 1179656 | tf_op jit(solution)/shard_map/ppermute | solution.py:40
  21.8 10.0 %collective-permute-start.5 = (f32[1,128,128]{2,1,0:T(8,128)S(1)}, f32[1,128,128]{2,1,0:T(8,128)S(1)}, u32[]{:S(2)}, u32[]{:S(2)}) collective-permute-start(f32[1,128,128]{2,1,0:T(8,128)S(1)} %constant_dynamic-slice_fusion), channel_id=1, source_target_pairs={{0,16},{4,20},{8,24},{12,28},{16,0},{20,4},{24,8},{28,12},{1,17},{... | collective-permute-start | bytes 196616 | tf_op jit(solution)/shard_map/ppermute | solution.py:40
  31.3 9.8 %collective-permute-start.1 = (f32[2,192,128]{2,1,0:T(8,128)S(1)}, f32[2,192,128]{2,1,0:T(8,128)S(1)}, u32[]{:S(2)}, u32[]{:S(2)}) collective-permute-start(f32[2,192,128]{2,1,0:T(8,128)S(1)} %dynamic-slice_bitcast_fusion), channel_id=1, source_target_pairs={{0,8},{4,12},{8,0},{12,4},{16,24},{20,28},{24,16},{28,20},{1,9},{5... | collective-permute-start | bytes 589832 | tf_op jit(solution)/shard_map/ppermute | solution.py:40
  31.9 32.3 %copy-start.1 = (bf16[1,128,128]{2,1,0:T(8,128)(2,1)}, bf16[1,128,128]{2,1,0:T(8,128)(2,1)S(1)}, u32[]{:S(2)}) copy-start(bf16[1,128,128]{2,1,0:T(8,128)(2,1)S(1)} %add_convert_fusion.2.q_ref) | copy-start | bytes 98308
  31.9 5.0 %collective-permute-start.6 = (bf16[1,128,128]{2,1,0:T(8,128)(2,1)S(1)}, bf16[1,128,128]{2,1,0:T(8,128)(2,1)S(1)}, u32[]{:S(2)}, u32[]{:S(2)}) collective-permute-start(bf16[1,128,128]{2,1,0:T(8,128)(2,1)S(1)} %add_convert_fusion.2.q_ref), channel_id=1, source_target_pairs={{0,16},{4,20},{8,24},{12,28},{16,0},{20,4},{24,8},{28,12},{1,17},{... | collective-permute-start | bytes 98312 | tf_op jit(solution)/shard_map/ppermute | solution.py:40
  36.9 6.4 %collective-permute-start.7 = (bf16[2,128,128]{2,1,0:T(8,128)(2,1)S(1)}, bf16[2,128,128]{2,1,0:T(8,128)(2,1)S(1)}, u32[]{:S(2)}, u32[]{:S(2)}) collective-permute-start(bf16[2,128,128]{2,1,0:T(8,128)(2,1)S(1)} %pad_maximum_fusion.2), channel_id=1, source_target_pairs={{0,8},{4,12},{8,0},{12,4},{16,24},{20,28},{24,16},{28,20},{1,9},{5... | collective-permute-start | bytes 196616 | tf_op jit(solution)/shard_map/ppermute | solution.py:40
  41.1 6.1 %collective-permute-start.2 = (f32[1,192,128]{2,1,0:T(8,128)S(1)}, f32[1,192,128]{2,1,0:T(8,128)S(1)}, u32[]{:S(2)}, u32[]{:S(2)}) collective-permute-start(f32[1,192,128]{2,1,0:T(8,128)S(1)} %constant_dynamic-slice_fusion.1), channel_id=1, source_target_pairs={{0,16},{4,20},{8,24},{12,28},{16,0},{20,4},{24,8},{28,12},{1,17},{... | collective-permute-start | bytes 294920 | tf_op jit(solution)/shard_map/ppermute | solution.py:40
  43.4 8.2 %collective-permute-start.8 = (bf16[4,128,128]{2,1,0:T(8,128)(2,1)S(1)}, bf16[4,128,128]{2,1,0:T(8,128)(2,1)S(1)}, u32[]{:S(2)}, u32[]{:S(2)}) collective-permute-start(bf16[4,128,128]{2,1,0:T(8,128)(2,1)S(1)} %pad_maximum_fusion.refs_0_), channel_id=1, source_target_pairs={{0,4},{4,0},{8,12},{12,8},{16,20},{20,16},{24,28},{28,24},{1,5},{5... | collective-permute-start | bytes 393224 | tf_op jit(solution)/shard_map/ppermute | solution.py:40
  47.3 17.0 %copy-start.2 = (bf16[1,192,128]{2,1,0:T(8,128)(2,1)}, bf16[1,192,128]{2,1,0:T(8,128)(2,1)S(1)}, u32[]{:S(2)}) copy-start(bf16[1,192,128]{2,1,0:T(8,128)(2,1)S(1)} %add_convert_fusion.1.q_ref) | copy-start | bytes 147460
  48.1 16.9 %all-to-all-start = ((bf16[8,192,128]{2,1,0:T(8,128)(2,1)}), bf16[8,192,128]{2,1,0:T(8,128)(2,1)S(1)}, u32[]{:S(2)}, u32[]{:S(2)}) async-start(bf16[8,192,128]{2,1,0:T(8,128)(2,1)} %broadcast_in_dim.8), calls=%async_computation | async-start | bytes 786432 | tf_op jit(solution)/shard_map/all_to_all | solution.py:78
  65.0 18.7 %copy-start = (bf16[8,192,128]{2,1,0:T(8,128)(2,1)}, bf16[8,192,128]{2,1,0:T(8,128)(2,1)S(1)}, u32[]{:S(2)}) copy-start(bf16[8,192,128]{2,1,0:T(8,128)(2,1)S(1)} %all-to-all-done.refs_0_.last_ref) | copy-start | bytes 1179652
  65.0 19.4 %all-to-all-start.3 = ((f16[8,136,128]{2,1,0:T(8,128)(2,1)}), f16[8,136,128]{2,1,0:T(8,128)(2,1)S(1)}, u32[]{:S(2)}, u32[]{:S(2)}) async-start(f16[8,136,128]{2,1,0:T(8,128)(2,1)} %convert_element_type.36), calls=%async_computation.3 | async-start | bytes 557056 | tf_op jit(solution)/shard_map/all_to_all | solution.py:513
  84.4 16.3 %all-to-all-start.1 = ((f16[8,136,128]{2,1,0:T(8,128)(2,1)}), f16[8,136,128]{2,1,0:T(8,128)(2,1)S(1)}, u32[]{:S(2)}, u32[]{:S(2)}) async-start(f16[8,136,128]{2,1,0:T(8,128)(2,1)} %convert_element_type.33), calls=%async_computation.1 | async-start | bytes 557056 | tf_op jit(solution)/shard_map/all_to_all | solution.py:513
  95.8 12.0 %collective-permute-start.9 = (bf16[1,128,128]{2,1,0:T(8,128)(2,1)}, bf16[1,128,128]{2,1,0:T(8,128)(2,1)S(1)}, u32[]{:S(2)}, u32[]{:S(2)}) collective-permute-start(bf16[1,128,128]{2,1,0:T(8,128)(2,1)} %shard_map.89), channel_id=1, source_target_pairs={{0,16},{4,20},{8,24},{12,28},{16,0},{20,4},{24,8},{28,12},{1,17},{... | collective-permute-start | bytes 98312 | tf_op jit(solution)/shard_map/ppermute | solution.py:40
  104.1 16.4 %all-to-all-start.2 = ((bf16[8,128,128]{2,1,0:T(8,128)(2,1)}), bf16[8,128,128]{2,1,0:T(8,128)(2,1)S(1)}, u32[]{:S(2)}, u32[]{:S(2)}) async-start(bf16[8,128,128]{2,1,0:T(8,128)(2,1)} %shard_map.85), calls=%async_computation.2 | async-start | bytes 524288 | tf_op jit(solution)/shard_map/all_to_all | solution.py:78
  108.5 4.4 %collective-permute-start.10 = (bf16[2,128,128]{2,1,0:T(8,128)(2,1)S(1)}, bf16[2,128,128]{2,1,0:T(8,128)(2,1)S(1)}, u32[]{:S(2)}, u32[]{:S(2)}) collective-permute-start(bf16[2,128,128]{2,1,0:T(8,128)(2,1)S(1)} %pad_maximum_fusion.3), channel_id=1, source_target_pairs={{0,8},{4,12},{8,0},{12,4},{16,24},{20,28},{24,16},{28,20},{1,9},{5... | collective-permute-start | bytes 196616 | tf_op jit(solution)/shard_map/ppermute | solution.py:40
  113.7 5.0 %collective-permute-start.11 = (bf16[4,128,128]{2,1,0:T(8,128)(2,1)S(1)}, bf16[4,128,128]{2,1,0:T(8,128)(2,1)S(1)}, u32[]{:S(2)}, u32[]{:S(2)}) collective-permute-start(bf16[4,128,128]{2,1,0:T(8,128)(2,1)S(1)} %pad_maximum_fusion.1.refs_0_), channel_id=1, source_target_pairs={{0,4},{4,0},{8,12},{12,8},{16,20},{20,16},{24,28},{28,24},{1,5},{5... | collective-permute-start | bytes 393224 | tf_op jit(solution)/shard_map/ppermute | solution.py:40
  122.4 1.6 %collective-permute-start.12 = (f32[2,32,1024]{2,1,0:T(8,128)S(1)}, f32[2,32,1024]{2,1,0:T(8,128)S(1)}, u32[]{:S(2)}, u32[]{:S(2)}) collective-permute-start(f32[2,32,1024]{2,1,0:T(8,128)S(1)} %get-tuple-element.24), channel_id=1, source_target_pairs={{0,1},{1,0},{2,3},{3,2},{4,5},{5,4},{6,7},{7,6},{8,9},{9,8},{10,11... | collective-permute-start | bytes 786440 | tf_op jit(solution)/shard_map/ppermute | solution.py:40
  124.1 4.3 %collective-permute-start.13 = (f16[1,32,1024]{2,1,0:T(8,128)(2,1)S(1)}, f16[1,32,1024]{2,1,0:T(8,128)(2,1)S(1)}, u32[]{:S(2)}, u32[]{:S(2)}) collective-permute-start(f16[1,32,1024]{2,1,0:T(8,128)(2,1)S(1)} %multiply_convert_fusion), channel_id=1, source_target_pairs={{0,2},{1,3},{2,0},{3,1},{4,6},{5,7},{6,4},{7,5},{8,10},{9,11},{10,... | collective-permute-start | bytes 196616 | tf_op jit(solution)/shard_map/ppermute | solution.py:40

commit v6 on v5

--- a/solution.py
+++ b/solution.py
@@ -40,17 +40,34 @@
     return lax.ppermute(array, axis, [(i, i ^ mask) for i in range(size)])
 
 
-def owners_sum(keep, send, me):
-    total = keep + swap(send, "seq", 1)
+def halve_kernel(me_ref, keep_ref, received_ref, *refs, mask):
+    next_keep_ref, next_send_ref = refs[-2:]
+    odd = lax.rem(me_ref[0] // mask, 2) == 1
+    for i in range(next_keep_ref.shape[0]):
+        even_part = keep_ref[2 * i] + received_ref[2 * i]
+        odd_part = keep_ref[2 * i + 1] + received_ref[2 * i + 1]
+        next_keep_ref[i] = jnp.where(odd, odd_part, even_part)
+        next_send_ref[i] = jnp.where(odd, even_part, odd_part)
+
+
+def halve(me, keep, received, mask, after):
+    shape = jax.ShapeDtypeStruct((keep.shape[0] // 2,) + keep.shape[1:], keep.dtype)
+    return pl.pallas_call(
+        functools.partial(halve_kernel, mask=mask),
+        out_shape=[shape] * 2,
+        in_specs=[smem_spec()] + [vmem_spec()] * 2 + [hbm_spec()] * len(after),
+        out_specs=[vmem_spec()] * 2,
+    )(me, keep, received, *after)
+
+
+def owners_sum(keep, send, me, after):
+    received = swap(send, "seq", 1)
     mask = 2
     while mask < lax.axis_size("seq"):
-        bit = me // mask % 2
-        pairs = total.reshape((-1, 2) + total.shape[1:])
-        keep = lax.dynamic_index_in_dim(pairs, bit, 1, False)
-        send = lax.dynamic_index_in_dim(pairs, 1 - bit, 1, False)
-        total = keep + swap(send, "seq", mask)
-        mask *= 2
-    return total.astype(jnp.bfloat16)
+        keep, send = halve(me, keep, received, mask, after)
+        received = swap(send, "seq", mask)
+        mask, after = 2 * mask, []
+    return (keep + received).astype(jnp.bfloat16)
 
 
 def doubling_masks(size):
@@ -65,6 +82,34 @@
     for mask in doubling_masks(lax.axis_size("seq")):
         block = jnp.concatenate([block, swap(block, "seq", mask)])
     return [block, swap(block, "seq", 1)]
+
+
+def gather_but_last(block):
+    masks = doubling_masks(lax.axis_size("seq"))
+    for mask in masks[:-1]:
+        block = jnp.concatenate([block, swap(block, "seq", mask)])
+    return block, swap(block, "seq", masks[-1])
+
+
+def pack_kernel(first_ref, second_ref, attended_ref, doubled_ref, copies_ref):
+    half = first_ref.shape[0]
+    doubled_ref[:half] = first_ref[...]
+    doubled_ref[half:] = second_ref[...]
+    for k in range(copies_ref.shape[0]):
+        copies_ref[k] = attended_ref[0]
+
+
+def pack(first, second, attended, copies):
+    shape = first.shape[1:]
+    return pl.pallas_call(
+        pack_kernel,
+        out_shape=[
+            jax.ShapeDtypeStruct((2 * first.shape[0],) + shape, first.dtype),
+            jax.ShapeDtypeStruct((copies,) + shape, first.dtype),
+        ],
+        in_specs=[vmem_spec()] * 3,
+        out_specs=[vmem_spec()] * 2,
+    )(first, second, attended)
 
 
 def doubling_offsets(size):
@@ -322,40 +367,45 @@
     )(length, me, *queries, keys, values)
 
 
-def fresh_kernel(me_ref, q_ref, last_ref, out_ref, stat_ref, kv_all, *, block, tokens, head):
+def fresh_kernel(me_ref, *refs, heads, block, tokens):
+    q_refs, last_ref, outs, kv_all = refs[:heads], refs[heads], refs[heads + 1 : -1], refs[-1]
     kv_block = last_ref.shape[1] - block
     for k in range(last_ref.shape[0]):
         rows = last_ref[k, block:, :].astype(jnp.float32)
         kv_all[k * kv_block : (k + 1) * kv_block, :] = rows
-    half = kv_all.shape[0] // 2
-    keys = kv_all[head * tokens : (head + 1) * tokens, :].astype(jnp.bfloat16)
-    values = kv_all[half + head * tokens : half + (head + 1) * tokens, :].astype(jnp.bfloat16)
-
-    s = lax.dot_general(q_ref[0, :block, :], keys, NT, preferred_element_type=jnp.float32)
-    s = s * (math.log2(math.e) / math.sqrt(HD))
-    token = lax.rem(me_ref[0] * block, tokens) + lax.broadcasted_iota(jnp.int32, s.shape, 0)
-    visible = lax.broadcasted_iota(jnp.int32, s.shape, 1) <= token
-    s = jnp.where(visible, s, NEG_BIG)
-    top = jnp.max(s, axis=1, keepdims=True)
-    weights = jnp.where(visible, jnp.exp2(s - top), 0.0).astype(jnp.bfloat16)
-    total = jnp.sum(weights.astype(jnp.float32), axis=1, keepdims=True)
-    out_ref[...] = jnp.dot(weights, values, preferred_element_type=jnp.float32)
-    lane = lax.broadcasted_iota(jnp.int32, stat_ref.shape, 1)
-    stat_ref[...] = jnp.where(lane < LANES // 2, top, total)
-
-
-def fresh(me, mine, last, block, tokens, head):
+    half = heads * tokens
+    for head in range(heads):
+        q_ref, (out_ref, stat_ref) = q_refs[head], outs[2 * head : 2 * head + 2]
+        first = head * tokens
+        keys = kv_all[first : first + tokens, :].astype(jnp.bfloat16)
+        values = kv_all[half + first : half + first + tokens, :].astype(jnp.bfloat16)
+        s = lax.dot_general(q_ref[0, :block, :], keys, NT, preferred_element_type=jnp.float32)
+        s = s * (math.log2(math.e) / math.sqrt(HD))
+        token = lax.rem(me_ref[0] * block, tokens) + lax.broadcasted_iota(jnp.int32, s.shape, 0)
+        visible = lax.broadcasted_iota(jnp.int32, s.shape, 1) <= token
+        s = jnp.where(visible, s, NEG_BIG)
+        top = jnp.max(s, axis=1, keepdims=True)
+        weights = jnp.where(visible, jnp.exp2(s - top), 0.0).astype(jnp.bfloat16)
+        total = jnp.sum(weights.astype(jnp.float32), axis=1, keepdims=True)
+        out_ref[...] = jnp.dot(weights, values, preferred_element_type=jnp.float32)
+        lane = lax.broadcasted_iota(jnp.int32, stat_ref.shape, 1)
+        stat_ref[...] = jnp.where(lane < LANES // 2, top, total)
+
+
+def fresh(me, mine, last, block, tokens):
+    heads = len(mine)
     kv_rows = last.shape[0] * (last.shape[1] - block)
     return pl.pallas_call(
-        functools.partial(fresh_kernel, block=block, tokens=tokens, head=head),
-        out_shape=[jax.ShapeDtypeStruct((block, HD), jnp.float32)] * 2,
-        in_specs=[smem_spec()] + [vmem_spec()] * 2,
-        out_specs=[vmem_spec()] * 2,
+        functools.partial(fresh_kernel, heads=heads, block=block, tokens=tokens),
+        out_shape=[jax.ShapeDtypeStruct((block, HD), jnp.float32)] * (2 * heads),
+        in_specs=[smem_spec()] + [vmem_spec()] * (heads + 1),
+        out_specs=[vmem_spec()] * (2 * heads),
         scratch_shapes=[pltpu.VMEM((kv_rows, HD), jnp.float32)],
-    )(me, mine, last)
-
-
-def merge_kernel(me_ref, part_ref, out_ref, stat_ref, copies_ref, turned):
+    )(me, *mine, last)
+
+
+def merge_kernel(me_ref, part_ref, out_ref, stat_ref, *refs):
+    copies_ref, turned = refs[-2:]
     count = part_ref.shape[0]
     block = out_ref.shape[0]
     new_top = stat_ref[:, 0:1]
@@ -379,14 +429,14 @@
         copies_ref[k] = attended
 
 
-def merge(me, parts, new_out, new_stat, copies):
+def merge(me, parts, new_out, new_stat, copies, after):
     return pl.pallas_call(
         merge_kernel,
         out_shape=jax.ShapeDtypeStruct((copies,) + new_out.shape, jnp.bfloat16),
-        in_specs=[smem_spec()] + [vmem_spec()] * 3,
+        in_specs=[smem_spec()] + [vmem_spec()] * 3 + [hbm_spec()] * len(after),
         out_specs=vmem_spec(),
         scratch_shapes=[pltpu.VMEM((LANES, parts.shape[0]), jnp.float32)],
-    )(me, parts, new_out, new_stat)
+    )(me, parts, new_out, new_stat, *after)
 
 
 def output_kernel(
@@ -494,29 +544,40 @@
     me = lax.axis_index("seq").reshape(1)
     place = lax.axis_index("head").reshape(1)
 
+    halves = []
+    for j in range(kv_local):
+        others = [key_weight, value_weight] if j == kv_local - 1 else []
+        halves.append(project(me, hidden, query_weight, others, j, columns, count))
     mine, queries = [], []
     for j in range(kv_local):
         last = j == kv_local - 1
-        others = [key_weight, value_weight] if last else []
-        keep, send = project(me, hidden, query_weight, others, j, columns, count)
-        mine.append(owners_sum(keep, send, me[0]))
+        mine.append(owners_sum(*halves[j], me, [] if last else [halves[j + 1][1]]))
         if last:
             copies = jnp.broadcast_to(mine[j], (count,) + mine[j].shape[1:])
             queries.append([gather_at_once(copies)])
         else:
             queries.append(gather_doubling(mine[j]))
 
-    mixed = None
+    fresh_parts = fresh(me, mine, queries[-1][0], block, tokens)
+    mixed, waiting = None, None
     for j in range(kv_local):
         last = j == kv_local - 1
         parts = attention(queries[j], block, cache_keys, cache_values, cache_lens, me, j)
         parts = lax.all_to_all(parts.astype(jnp.float16), "seq", 0, 0).astype(jnp.float32)
-        new_out, new_stat = fresh(me, mine[j], queries[-1][0], block, tokens, j)
-        copies = merge(me, parts, new_out, new_stat, count if last else 1)
-        attended = [gather_at_once(copies)] if last else gather_doubling(copies)
-        result = output_part(
-            me, place, output_weight, attended, tokens, mixed, j, heads, last
-        )
+        after = [waiting[0]] if last and waiting else []
+        copies = 1 if waiting or not last else count
+        attended = merge(me, parts, *fresh_parts[2 * j : 2 * j + 2], copies, after)
+        if j == kv_local - 2:
+            waiting = gather_but_last(attended)
+            continue
+        if last and waiting:
+            doubled, attended = pack(*waiting, attended, count)
+            before = [doubled, swap(doubled, "seq", 1)]
+            mixed = output_part(
+                me, place, output_weight, before, tokens, mixed, j - 1, heads, False
+            )[0]
+        rows = [gather_at_once(attended)] if last else gather_doubling(attended)
+        result = output_part(me, place, output_weight, rows, tokens, mixed, j, heads, last)
         mixed = result if last else result[0]
 
     keep, send = mixed

time: 129 us -> 135 us (1.047)
  Pallas kernels: 45.9 us -> 52.7 us
  local copies, waits for them, and re-layouts: 0.88 us -> 5.15 us
  waiting for transfers between devices: 27.8 us -> 24.6 us
    pallas_call x2 -> x6, Pallas kernels: 4.03 us -> 11 us  [the longest x4 7.04 us: halve(): pl.pallas_call(functools.partial(halve_kernel, mask=mask), out_shape=[sha...]
    unnamed x6 -> x20, local copies, waits for them, and re-layouts: 0.01 us -> 4.34 us
    ppermute x14, waiting for transfers between devices: 27.8 us -> 24.5 us  [swap(): return lax.ppermute(array, axis, [(i, i ^ mask) for i in range(size)])]
    all_to_all x2, starting transfers between devices: 7.09 us -> 9.88 us  [gather_at_once(): return lax.all_to_all(copies, 'seq', 0, 0)]
    ppermute x14, starting transfers between devices: 27 us -> 24.6 us  [swap(): return lax.ppermute(array, axis, [(i, i ^ mask) for i in range(size)])]
    add x4 -> x0, other arithmetic: 2.05 us -> none  [the longest x2 2.02 us: owners_sum(): total = keep + swap(send, 'seq', 1)]
    convert_element_type x2, other arithmetic: 0.03 us -> 1.76 us  [owners_sum(): return (keep + received).astype(jnp.bfloat16)]
    all_to_all x2, starting transfers between devices: 11.9 us -> 10.2 us  [shards(): lax.all_to_all(parts.astype(jnp.float16), 'seq', 0, 0).astype(jnp.float32)]
  transfers between devices with their start and end apart: 18 -> 18, of which waited for: 9 -> 9; matrix products, arithmetic and copies ran while one was open for 5% -> 5% of each run, Pallas kernels for 31% -> 33%
where the time goes in v6:
time: 135 us; the launch traced here: 134 us
  Pallas kernels  52.7 us (39%)
  starting transfers between devices  44.7 us (33%)
  waiting for transfers between devices  24.6 us (18%)
  other arithmetic  6.41 us (5%)
  local copies, waits for them, and re-layouts  5.15 us (4%)
    pallas_call x2, Pallas kernels, attention(): pl.pallas_call(functools.partial(attention_kernel, sources=sources, band=...  25.4 us
    ppermute x14, starting transfers between devices, swap(): return lax.ppermute(array, axis, [(i, i ^ mask) for i in range(size)])  24.6 us
    ppermute x14, waiting for transfers between devices, swap(): return lax.ppermute(array, axis, [(i, i ^ mask) for i in range(size)])  24.5 us
    all_to_all x2, starting transfers between devices, shards(): lax.all_to_all(parts.astype(jnp.float16), 'seq', 0, 0).astype(jnp.float32)  10.2 us
    all_to_all x2, starting transfers between devices, gather_at_once(): return lax.all_to_all(copies, 'seq', 0, 0)  9.88 us
    pallas_call x2, Pallas kernels, project(): pl.pallas_call(functools.partial(project_kernel, extra=len(others), chunk...  7.75 us
    pallas_call x4, Pallas kernels, halve(): pl.pallas_call(functools.partial(halve_kernel, mask=mask), out_shape=[sha...  7.04 us
    pallas_call x2, Pallas kernels, merge(): pl.pallas_call(merge_kernel, out_shape=jax.ShapeDtypeStruct((copies,) + n...  4.88 us
  transfers between devices with their start and end apart: 18, of which 9 were waited for; matrix products, arithmetic and copies ran while one was open for 5% of the time, Pallas kernels for 33%

profile of v6, /device:TPU:0, one launch (start us, length us, event | category | flops | bytes accessed | tf_op | source)
XLA Modules:
  0.0 134.3 jit_solution(3088062027561640957)
XLA Ops:
  0.0 3.5 %shard_map.82 = (f32[4,128,128]{2,1,0:T(8,128)}, f32[4,128,128]{2,1,0:T(8,128)}) custom-call(s32[1]{0:T(128)} %bitcast.me_ref, bf16[128,1024]{1,0:T(8,128)(2,1)} %hidden_ref.3, bf16[1024,2048]{1,0:T(8,128)(2,1)} %refs_0_.3), custom_call_target="tpu_custom_call" | custom-call | flops 268435456 | bytes 2097152 | tf_op jit(solution)/shard_map/pallas_call | solution.py:183
  3.5 3.0 %collective-permute-start = (f32[4,128,128]{2,1,0:T(8,128)}, f32[4,128,128]{2,1,0:T(8,128)S(1)}, u32[]{:S(2)}, u32[]{:S(2)}) collective-permute-start(f32[4,128,128]{2,1,0:T(8,128)} %get-tuple-element.26), channel_id=1, source_target_pairs={{0,4},{4,0},{8,12},{12,8},{16,20},{20,16},{24,28},{28,24},{1,5},{5... | collective-permute-start | bytes 786440 | tf_op jit(solution)/shard_map/ppermute | solution.py:40
  6.5 4.2 %shard_map.83 = (f32[4,192,128]{2,1,0:T(8,128)}, f32[4,192,128]{2,1,0:T(8,128)}) custom-call(s32[1]{0:T(128)} %bitcast.me_ref, bf16[128,1024]{1,0:T(8,128)(2,1)} %hidden_ref.3, bf16[1024,2048]{1,0:T(8,128)(2,1)} %refs_0_.3, bf16[1024,256]{1,0:T(8,128)(2,1)} %refs_1_.2, bf16[1024,256]{1,0:T(8,128)(2,1)} %refs_2_.3), custom_call_target="tpu_custom_call" | custom-call | flops 402653184 | bytes 3145728 | tf_op jit(solution)/shard_map/pallas_call | solution.py:183
  10.8 2.3 %collective-permute-done.received_ref = f32[4,128,128]{2,1,0:T(8,128)S(1)} collective-permute-done((f32[4,128,128]{2,1,0:T(8,128)}, f32[4,128,128]{2,1,0:T(8,128)S(1)}, u32[]{:S(2)}, u32[]{:S(2)}) %collective-permute-start) | collective-permute-done | bytes 262176 | tf_op jit(solution)/shard_map/ppermute | solution.py:40
  13.8 1.8 %shard_map.84 = (f32[2,128,128]{2,1,0:T(8,128)}, f32[2,128,128]{2,1,0:T(8,128)}) custom-call(s32[1]{0:T(128)} %bitcast.me_ref, f32[4,128,128]{2,1,0:T(8,128)} %get-tuple-element.25.keep_ref, f32[4,128,128]{2,1,0:T(8,128)} %copy-done.6, f32[4,192,128]{2,1,0:T(8,128)} %get-tuple-element.27.refs_0_), custom_call_target="tpu_custom_call" | custom-call | tf_op jit(solution)/shard_map/pallas_call | solution.py:55
  15.5 1.8 %collective-permute-start.1 = (f32[2,128,128]{2,1,0:T(8,128)}, f32[2,128,128]{2,1,0:T(8,128)S(1)}, u32[]{:S(2)}, u32[]{:S(2)}) collective-permute-start(f32[2,128,128]{2,1,0:T(8,128)} %get-tuple-element.29), channel_id=1, source_target_pairs={{0,8},{4,12},{8,0},{12,4},{16,24},{20,28},{24,16},{28,20},{1,9},{5... | collective-permute-start | bytes 393224 | tf_op jit(solution)/shard_map/ppermute | solution.py:40
  17.4 1.5 %collective-permute-start.6 = (f32[4,192,128]{2,1,0:T(8,128)}, f32[4,192,128]{2,1,0:T(8,128)S(1)}, u32[]{:S(2)}, u32[]{:S(2)}) collective-permute-start(f32[4,192,128]{2,1,0:T(8,128)} %get-tuple-element.27.refs_0_), channel_id=1, source_target_pairs={{0,4},{4,0},{8,12},{12,8},{16,20},{20,16},{24,28},{28,24},{1,5},{5... | collective-permute-start | bytes 1179656 | tf_op jit(solution)/shard_map/ppermute | solution.py:40
  18.8 1.9 %collective-permute-done.1.received_ref = f32[2,128,128]{2,1,0:T(8,128)S(1)} collective-permute-done((f32[2,128,128]{2,1,0:T(8,128)}, f32[2,128,128]{2,1,0:T(8,128)S(1)}, u32[]{:S(2)}, u32[]{:S(2)}) %collective-permute-start.1) | collective-permute-done | bytes 131104 | tf_op jit(solution)/shard_map/ppermute | solution.py:40
  21.4 1.6 %shard_map.85 = (f32[1,128,128]{2,1,0:T(8,128)}, f32[1,128,128]{2,1,0:T(8,128)}) custom-call(s32[1]{0:T(128)} %bitcast.me_ref, f32[2,128,128]{2,1,0:T(8,128)} %get-tuple-element.28.keep_ref, f32[2,128,128]{2,1,0:T(8,128)} %copy-done.8), custom_call_target="tpu_custom_call" | custom-call | tf_op jit(solution)/shard_map/pallas_call | solution.py:55
  23.0 2.8 %collective-permute-start.2 = (f32[1,128,128]{2,1,0:T(8,128)}, f32[1,128,128]{2,1,0:T(8,128)S(1)}, u32[]{:S(2)}, u32[]{:S(2)}) collective-permute-start(f32[1,128,128]{2,1,0:T(8,128)} %get-tuple-element.31), channel_id=1, source_target_pairs={{0,16},{4,20},{8,24},{12,28},{16,0},{20,4},{24,8},{28,12},{1,17},{... | collective-permute-start | bytes 196616 | tf_op jit(solution)/shard_map/ppermute | solution.py:40
  25.8 2.5 %collective-permute-done.2 = f32[1,128,128]{2,1,0:T(8,128)S(1)} collective-permute-done((f32[1,128,128]{2,1,0:T(8,128)}, f32[1,128,128]{2,1,0:T(8,128)S(1)}, u32[]{:S(2)}, u32[]{:S(2)}) %collective-permute-start.2) | collective-permute-done | bytes 65568 | tf_op jit(solution)/shard_map/ppermute | solution.py:40
  28.4 0.9 add_convert_fusion.2.refs_0_
  29.2 3.0 %collective-permute-start.3 = (bf16[1,128,128]{2,1,0:T(8,128)(2,1)S(1)}, bf16[1,128,128]{2,1,0:T(8,128)(2,1)S(1)}, u32[]{:S(2)}, u32[]{:S(2)}) collective-permute-start(bf16[1,128,128]{2,1,0:T(8,128)(2,1)S(1)} %add_convert_fusion.2.refs_0_), channel_id=1, source_target_pairs={{0,16},{4,20},{8,24},{12,28},{16,0},{20,4},{24,8},{28,12},{1,17},{... | collective-permute-start | bytes 98312 | tf_op jit(solution)/shard_map/ppermute | solution.py:40
  32.2 0.8 copy-done.5
  33.0 1.9 %shard_map.87 = (f32[2,192,128]{2,1,0:T(8,128)}, f32[2,192,128]{2,1,0:T(8,128)}) custom-call(s32[1]{0:T(128)} %bitcast.me_ref, f32[4,192,128]{2,1,0:T(8,128)} %get-tuple-element.32.keep_ref, f32[4,192,128]{2,1,0:T(8,128)} %copy-done.5), custom_call_target="tpu_custom_call" | custom-call | tf_op jit(solution)/shard_map/pallas_call | solution.py:55
  34.9 2.1 %collective-permute-start.7 = (f32[2,192,128]{2,1,0:T(8,128)}, f32[2,192,128]{2,1,0:T(8,128)S(1)}, u32[]{:S(2)}, u32[]{:S(2)}) collective-permute-start(f32[2,192,128]{2,1,0:T(8,128)} %get-tuple-element.34), channel_id=1, source_target_pairs={{0,8},{4,12},{8,0},{12,4},{16,24},{20,28},{24,16},{28,20},{1,9},{5... | collective-permute-start | bytes 589832 | tf_op jit(solution)/shard_map/ppermute | solution.py:40
  37.7 3.2 %collective-permute-done.7.received_ref = f32[2,192,128]{2,1,0:T(8,128)S(1)} collective-permute-done((f32[2,192,128]{2,1,0:T(8,128)}, f32[2,192,128]{2,1,0:T(8,128)S(1)}, u32[]{:S(2)}, u32[]{:S(2)}) %collective-permute-start.7) | collective-permute-done | bytes 196640 | tf_op jit(solution)/shard_map/ppermute | solution.py:40
  41.6 1.7 %shard_map.88 = (f32[1,192,128]{2,1,0:T(8,128)}, f32[1,192,128]{2,1,0:T(8,128)}) custom-call(s32[1]{0:T(128)} %bitcast.me_ref, f32[2,192,128]{2,1,0:T(8,128)} %get-tuple-element.33.keep_ref, f32[2,192,128]{2,1,0:T(8,128)} %copy-done.7), custom_call_target="tpu_custom_call" | custom-call | tf_op jit(solution)/shard_map/pallas_call | solution.py:55
  43.4 1.6 %collective-permute-start.5 = (bf16[4,128,128]{2,1,0:T(8,128)(2,1)S(1)}, bf16[4,128,128]{2,1,0:T(8,128)(2,1)S(1)}, u32[]{:S(2)}, u32[]{:S(2)}) collective-permute-start(bf16[4,128,128]{2,1,0:T(8,128)(2,1)S(1)} %pad_maximum_fusion.refs_0_), channel_id=1, source_target_pairs={{0,4},{4,0},{8,12},{12,8},{16,20},{20,16},{24,28},{28,24},{1,5},{5... | collective-permute-start | bytes 393224 | tf_op jit(solution)/shard_map/ppermute | solution.py:40
  45.0 4.1 %collective-permute-done.8 = f32[1,192,128]{2,1,0:T(8,128)S(1)} collective-permute-done((f32[1,192,128]{2,1,0:T(8,128)}, f32[1,192,128]{2,1,0:T(8,128)S(1)}, u32[]{:S(2)}, u32[]{:S(2)}) %collective-permute-start.8) | collective-permute-done | bytes 98336 | tf_op jit(solution)/shard_map/ppermute | solution.py:40
  49.1 0.9 add_convert_fusion.1.refs_1_
  50.0 0.8 broadcast_in_dim.8
  50.8 4.6 %all-to-all-start.1 = ((bf16[8,192,128]{2,1,0:T(8,128)(2,1)}), bf16[8,192,128]{2,1,0:T(8,128)(2,1)S(1)}, u32[]{:S(2)}, u32[]{:S(2)}) async-start(bf16[8,192,128]{2,1,0:T(8,128)(2,1)} %broadcast_in_dim.8), calls=%async_computation.1 | async-start | bytes 786432 | tf_op jit(solution)/shard_map/all_to_all | solution.py:123
  55.4 12.7 %shard_map.86 = f32[8,136,128]{2,1,0:T(8,128)S(1)} custom-call(s32[1]{0:T(128)S(6)} %copy.9.len_ref, s32[1]{0:T(128)} %bitcast.me_ref, bf16[4,128,128]{2,1,0:T(8,128)(2,1)S(1)} %pad_maximum_fusion.refs_0_, bf16[4,128,128]{2,1,0:T(8,128)(2,1)S(1)} %collective-permute-done.5.refs_1_, bf16[8192,256]{1,0:T(8,128)(2,1)} %refs_1_.3, bf16[8192,256]{1,0:T(8,128)(2,1)} %refs_2_.5), custom_call_target="tpu_custom_call" | custom-call | flops 8589934592 | bytes 4194304 | tf_op jit(solution)/shard_map/pallas_call | solution.py:342
  68.1 0.7 convert_element_type.33
  68.9 5.1 %all-to-all-start = ((f16[8,136,128]{2,1,0:T(8,128)(2,1)}), f16[8,136,128]{2,1,0:T(8,128)(2,1)S(1)}, u32[]{:S(2)}, u32[]{:S(2)}) async-start(f16[8,136,128]{2,1,0:T(8,128)(2,1)} %convert_element_type.33), calls=%async_computation | async-start | bytes 557056 | tf_op jit(solution)/shard_map/all_to_all | solution.py:566
  73.9 12.7 %shard_map.91 = f32[8,136,128]{2,1,0:T(8,128)S(1)} custom-call(s32[1]{0:T(128)S(6)} %copy.9.len_ref, s32[1]{0:T(128)} %bitcast.me_ref, bf16[8,192,128]{2,1,0:T(8,128)(2,1)S(1)} %all-to-all-done.1.refs_2_.refs_0_, bf16[8192,256]{1,0:T(8,128)(2,1)} %refs_1_.3, bf16[8192,256]{1,0:T(8,128)(2,1)} %refs_2_.5), custom_call_target="tpu_custom_call" | custom-call | flops 8589934592 | bytes 4194304 | tf_op jit(solution)/shard_map/pallas_call | solution.py:342
  86.7 0.8 convert_element_type.36
  87.4 5.1 %all-to-all-start.2 = ((f16[8,136,128]{2,1,0:T(8,128)(2,1)}), f16[8,136,128]{2,1,0:T(8,128)(2,1)S(1)}, u32[]{:S(2)}, u32[]{:S(2)}) async-start(f16[8,136,128]{2,1,0:T(8,128)(2,1)} %convert_element_type.36), calls=%async_computation.2 | async-start | bytes 557056 | tf_op jit(solution)/shard_map/all_to_all | solution.py:566
  92.6 0.8 convert_element_type.34.part_ref
  93.4 2.3 %shard_map.89 = (f32[128,128]{1,0:T(8,128)}, f32[128,128]{1,0:T(8,128)}, f32[128,128]{1,0:T(8,128)}, f32[128,128]{1,0:T(8,128)}) custom-call(s32[1]{0:T(128)} %bitcast.me_ref, bf16[1,128,128]{2,1,0:T(8,128)(2,1)} %copy-done.3, bf16[1,192,128]{2,1,0:T(8,128)(2,1)} %copy-done.4, bf16[8,192,128]{2,1,0:T(8,128)(2,1)} %copy-done), custom_call_target="tpu_custom_call" | custom-call | tf_op jit(solution)/shard_map/pallas_call | solution.py:398
  95.7 2.4 %shard_map.90 = bf16[1,128,128]{2,1,0:T(8,128)(2,1)} custom-call(s32[1]{0:T(128)} %bitcast.me_ref, f32[8,136,128]{2,1,0:T(8,128)} %convert_element_type.34.part_ref, f32[128,128]{1,0:T(8,128)} %get-tuple-element.37.out_ref, f32[128,128]{1,0:T(8,128)} %get-tuple-element.38.stat_ref), custom_call_target="tpu_custom_call" | custom-call | tf_op jit(solution)/shard_map/pallas_call | solution.py:433
  98.1 2.9 %collective-permute-start.9 = (bf16[1,128,128]{2,1,0:T(8,128)(2,1)}, bf16[1,128,128]{2,1,0:T(8,128)(2,1)S(1)}, u32[]{:S(2)}, u32[]{:S(2)}) collective-permute-start(bf16[1,128,128]{2,1,0:T(8,128)(2,1)} %shard_map.90), channel_id=1, source_target_pairs={{0,16},{4,20},{8,24},{12,28},{16,0},{20,4},{24,8},{28,12},{1,17},{... | collective-permute-start | bytes 98312 | tf_op jit(solution)/shard_map/ppermute | solution.py:40
  101.0 2.1 %collective-permute-done.9 = bf16[1,128,128]{2,1,0:T(8,128)(2,1)S(1)} collective-permute-done((bf16[1,128,128]{2,1,0:T(8,128)(2,1)}, bf16[1,128,128]{2,1,0:T(8,128)(2,1)S(1)}, u32[]{:S(2)}, u32[]{:S(2)}) %collective-permute-start.9) | collective-permute-done | bytes 32800 | tf_op jit(solution)/shard_map/ppermute | solution.py:40
  103.1 0.8 pad_maximum_fusion.2.refs_0_.first_ref
  103.9 2.1 %collective-permute-start.10 = (bf16[2,128,128]{2,1,0:T(8,128)(2,1)S(1)}, bf16[2,128,128]{2,1,0:T(8,128)(2,1)S(1)}, u32[]{:S(2)}, u32[]{:S(2)}) collective-permute-start(bf16[2,128,128]{2,1,0:T(8,128)(2,1)S(1)} %pad_maximum_fusion.2.refs_0_.first_ref), channel_id=1, source_target_pairs={{0,8},{4,12},{8,0},{12,4},{16,24},{20,28},{24,16},{28,20},{1,9},{5... | collective-permute-start | bytes 196616 | tf_op jit(solution)/shard_map/ppermute | solution.py:40
  106.0 0.8 convert_element_type.37.part_ref
  106.8 2.4 %shard_map.92.attended_ref = bf16[1,128,128]{2,1,0:T(8,128)(2,1)} custom-call(s32[1]{0:T(128)} %bitcast.me_ref, f32[8,136,128]{2,1,0:T(8,128)} %convert_element_type.37.part_ref, f32[128,128]{1,0:T(8,128)} %get-tuple-element.39.out_ref, f32[128,128]{1,0:T(8,128)} %get-tuple-element.40.stat_ref, bf16[2,128,128]{2,1,0:T(8,128)(2,1)} %copy-done.2), custom_call_target="tpu_custom_call" | custom-call | tf_op jit(solution)/shard_map/pallas_call | solution.py:433
  109.9 1.6 %shard_map.93 = (bf16[4,128,128]{2,1,0:T(8,128)(2,1)}, bf16[8,128,128]{2,1,0:T(8,128)(2,1)}) custom-call(bf16[2,128,128]{2,1,0:T(8,128)(2,1)} %copy-done.2, bf16[2,128,128]{2,1,0:T(8,128)(2,1)} %copy-done.9, bf16[1,128,128]{2,1,0:T(8,128)(2,1)} %shard_map.92.attended_ref), custom_call_target="tpu_custom_call" | custom-call | tf_op jit(solution)/shard_map/pallas_call | solution.py:104
  111.6 5.3 %all-to-all-start.3 = ((bf16[8,128,128]{2,1,0:T(8,128)(2,1)}), bf16[8,128,128]{2,1,0:T(8,128)(2,1)S(1)}, u32[]{:S(2)}, u32[]{:S(2)}) async-start(bf16[8,128,128]{2,1,0:T(8,128)(2,1)} %get-tuple-element.41), calls=%async_computation.3 | async-start | bytes 524288 | tf_op jit(solution)/shard_map/all_to_all | solution.py:123
  116.9 2.0 %collective-permute-start.11 = (bf16[4,128,128]{2,1,0:T(8,128)(2,1)}, bf16[4,128,128]{2,1,0:T(8,128)(2,1)S(1)}, u32[]{:S(2)}, u32[]{:S(2)}) collective-permute-start(bf16[4,128,128]{2,1,0:T(8,128)(2,1)} %get-tuple-element.42.refs_0_), channel_id=1, source_target_pairs={{0,4},{4,0},{8,12},{12,8},{16,20},{20,16},{24,28},{28,24},{1,5},{5... | collective-permute-start | bytes 393224 | tf_op jit(solution)/shard_map/ppermute | solution.py:40
  118.9 4.2 %collective-permute-done.11.refs_1_ = bf16[4,128,128]{2,1,0:T(8,128)(2,1)S(1)} collective-permute-done((bf16[4,128,128]{2,1,0:T(8,128)(2,1)}, bf16[4,128,128]{2,1,0:T(8,128)(2,1)S(1)}, u32[]{:S(2)}, u32[]{:S(2)}) %collective-permute-start.11) | collective-permute-done | bytes 131104 | tf_op jit(solution)/shard_map/ppermute | solution.py:40
  123.1 0.9 copy-done.1
  124.0 1.8 %shard_map.94.refs_1_ = f32[128,1024]{1,0:T(8,128)S(1)} custom-call(s32[1]{0:T(128)} %bitcast.me_ref, s32[1]{0:T(128)} %bitcast.1.place_ref, bf16[2048,1024]{1,0:T(8,128)(2,1)} %w_hbm.3, bf16[4,128,128]{2,1,0:T(8,128)(2,1)S(1)} %copy-done.1, bf16[4,128,128]{2,1,0:T(8,128)(2,1)S(1)} %collective-permute-done.11.refs_1_), custom_call_target="tpu_custom_call" | custom-call | flops 268435456 | bytes 2097152 | tf_op jit(solution)/shard_map/pallas_call | solution.py:498
  125.8 1.9 %shard_map.95 = (f32[2,32,1024]{2,1,0:T(8,128)S(1)}, f32[2,32,1024]{2,1,0:T(8,128)S(1)}) custom-call(s32[1]{0:T(128)} %bitcast.me_ref, s32[1]{0:T(128)} %bitcast.1.place_ref, bf16[2048,1024]{1,0:T(8,128)(2,1)} %w_hbm.3, bf16[8,128,128]{2,1,0:T(8,128)(2,1)S(1)} %all-to-all-done.3.refs_0_, f32[128,1024]{1,0:T(8,128)S(1)} %shard_map.94.refs_1_), custom_call_target="tpu_custom_call" | custom-call | flops 268435456 | bytes 2097152 | tf_op jit(solution)/shard_map/pallas_call | solution.py:498
  127.8 1.5 %collective-permute-done.12 = f32[2,32,1024]{2,1,0:T(8,128)S(1)} collective-permute-done((f32[2,32,1024]{2,1,0:T(8,128)S(1)}, f32[2,32,1024]{2,1,0:T(8,128)S(1)}, u32[]{:S(2)}, u32[]{:S(2)}) %collective-permute-start.12) | collective-permute-done | bytes 262176 | tf_op jit(solution)/shard_map/ppermute | solution.py:40
  129.4 1.6 %collective-permute-start.13 = (f16[1,32,1024]{2,1,0:T(8,128)(2,1)S(1)}, f16[1,32,1024]{2,1,0:T(8,128)(2,1)S(1)}, u32[]{:S(2)}, u32[]{:S(2)}) collective-permute-start(f16[1,32,1024]{2,1,0:T(8,128)(2,1)S(1)} %multiply_convert_fusion), channel_id=1, source_target_pairs={{0,2},{1,3},{2,0},{3,1},{4,6},{5,7},{6,4},{7,5},{8,10},{9,11},{10,... | collective-permute-start | bytes 196616 | tf_op jit(solution)/shard_map/ppermute | solution.py:40
  130.9 2.7 %collective-permute-done.13 = f16[1,32,1024]{2,1,0:T(8,128)(2,1)S(1)} collective-permute-done((f16[1,32,1024]{2,1,0:T(8,128)(2,1)S(1)}, f16[1,32,1024]{2,1,0:T(8,128)(2,1)S(1)}, u32[]{:S(2)}, u32[]{:S(2)}) %collective-permute-start.13) | collective-permute-done | bytes 65568 | tf_op jit(solution)/shard_map/ppermute | solution.py:40
  (35 shorter events, 3.6 us)
Async XLA Ops:
  3.5 9.5 %collective-permute-start = (f32[4,128,128]{2,1,0:T(8,128)}, f32[4,128,128]{2,1,0:T(8,128)S(1)}, u32[]{:S(2)}, u32[]{:S(2)}) collective-permute-start(f32[4,128,128]{2,1,0:T(8,128)} %get-tuple-element.26), channel_id=1, source_target_pairs={{0,4},{4,0},{8,12},{12,8},{16,20},{20,16},{24,28},{28,24},{1,5},{5... | collective-permute-start | bytes 786440 | tf_op jit(solution)/shard_map/ppermute | solution.py:40
  13.1 0.7 copy-start.6
  15.5 5.2 %collective-permute-start.1 = (f32[2,128,128]{2,1,0:T(8,128)}, f32[2,128,128]{2,1,0:T(8,128)S(1)}, u32[]{:S(2)}, u32[]{:S(2)}) collective-permute-start(f32[2,128,128]{2,1,0:T(8,128)} %get-tuple-element.29), channel_id=1, source_target_pairs={{0,8},{4,12},{8,0},{12,4},{16,24},{20,28},{24,16},{28,20},{1,9},{5... | collective-permute-start | bytes 393224 | tf_op jit(solution)/shard_map/ppermute | solution.py:40
  17.4 14.9 %collective-permute-start.6 = (f32[4,192,128]{2,1,0:T(8,128)}, f32[4,192,128]{2,1,0:T(8,128)S(1)}, u32[]{:S(2)}, u32[]{:S(2)}) collective-permute-start(f32[4,192,128]{2,1,0:T(8,128)} %get-tuple-element.27.refs_0_), channel_id=1, source_target_pairs={{0,4},{4,0},{8,12},{12,8},{16,20},{20,16},{24,28},{28,24},{1,5},{5... | collective-permute-start | bytes 1179656 | tf_op jit(solution)/shard_map/ppermute | solution.py:40
  20.7 0.7 copy-start.8
  23.0 5.4 %collective-permute-start.2 = (f32[1,128,128]{2,1,0:T(8,128)}, f32[1,128,128]{2,1,0:T(8,128)S(1)}, u32[]{:S(2)}, u32[]{:S(2)}) collective-permute-start(f32[1,128,128]{2,1,0:T(8,128)} %get-tuple-element.31), channel_id=1, source_target_pairs={{0,16},{4,20},{8,24},{12,28},{16,0},{20,4},{24,8},{28,12},{1,17},{... | collective-permute-start | bytes 196616 | tf_op jit(solution)/shard_map/ppermute | solution.py:40
  29.2 38.9 %copy-start.3 = (bf16[1,128,128]{2,1,0:T(8,128)(2,1)}, bf16[1,128,128]{2,1,0:T(8,128)(2,1)S(1)}, u32[]{:S(2)}) copy-start(bf16[1,128,128]{2,1,0:T(8,128)(2,1)S(1)} %add_convert_fusion.2.refs_0_) | copy-start | bytes 98308
  29.2 7.8 %collective-permute-start.3 = (bf16[1,128,128]{2,1,0:T(8,128)(2,1)S(1)}, bf16[1,128,128]{2,1,0:T(8,128)(2,1)S(1)}, u32[]{:S(2)}, u32[]{:S(2)}) collective-permute-start(bf16[1,128,128]{2,1,0:T(8,128)(2,1)S(1)} %add_convert_fusion.2.refs_0_), channel_id=1, source_target_pairs={{0,16},{4,20},{8,24},{12,28},{16,0},{20,4},{24,8},{28,12},{1,17},{... | collective-permute-start | bytes 98312 | tf_op jit(solution)/shard_map/ppermute | solution.py:40
  32.2 0.8 copy-start.5
  34.9 6.1 %collective-permute-start.7 = (f32[2,192,128]{2,1,0:T(8,128)}, f32[2,192,128]{2,1,0:T(8,128)S(1)}, u32[]{:S(2)}, u32[]{:S(2)}) collective-permute-start(f32[2,192,128]{2,1,0:T(8,128)} %get-tuple-element.34), channel_id=1, source_target_pairs={{0,8},{4,12},{8,0},{12,4},{16,24},{20,28},{24,16},{28,20},{1,9},{5... | collective-permute-start | bytes 589832 | tf_op jit(solution)/shard_map/ppermute | solution.py:40
  37.0 6.4 %collective-permute-start.4 = (bf16[2,128,128]{2,1,0:T(8,128)(2,1)S(1)}, bf16[2,128,128]{2,1,0:T(8,128)(2,1)S(1)}, u32[]{:S(2)}, u32[]{:S(2)}) collective-permute-start(bf16[2,128,128]{2,1,0:T(8,128)(2,1)S(1)} %pad_maximum_fusion.1), channel_id=1, source_target_pairs={{0,8},{4,12},{8,0},{12,4},{16,24},{20,28},{24,16},{28,20},{1,9},{5... | collective-permute-start | bytes 196616 | tf_op jit(solution)/shard_map/ppermute | solution.py:40
  41.0 0.7 copy-start.7
  43.4 5.7 %collective-permute-start.8 = (f32[1,192,128]{2,1,0:T(8,128)}, f32[1,192,128]{2,1,0:T(8,128)S(1)}, u32[]{:S(2)}, u32[]{:S(2)}) collective-permute-start(f32[1,192,128]{2,1,0:T(8,128)} %get-tuple-element.36), channel_id=1, source_target_pairs={{0,16},{4,20},{8,24},{12,28},{16,0},{20,4},{24,8},{28,12},{1,17},{... | collective-permute-start | bytes 294920 | tf_op jit(solution)/shard_map/ppermute | solution.py:40
  43.4 12.0 %collective-permute-start.5 = (bf16[4,128,128]{2,1,0:T(8,128)(2,1)S(1)}, bf16[4,128,128]{2,1,0:T(8,128)(2,1)S(1)}, u32[]{:S(2)}, u32[]{:S(2)}) collective-permute-start(bf16[4,128,128]{2,1,0:T(8,128)(2,1)S(1)} %pad_maximum_fusion.refs_0_), channel_id=1, source_target_pairs={{0,4},{4,0},{8,12},{12,8},{16,20},{20,16},{24,28},{28,24},{1,5},{5... | collective-permute-start | bytes 393224 | tf_op jit(solution)/shard_map/ppermute | solution.py:40
  50.0 18.1 %copy-start.4 = (bf16[1,192,128]{2,1,0:T(8,128)(2,1)}, bf16[1,192,128]{2,1,0:T(8,128)(2,1)S(1)}, u32[]{:S(2)}) copy-start(bf16[1,192,128]{2,1,0:T(8,128)(2,1)S(1)} %add_convert_fusion.1.refs_1_) | copy-start | bytes 147460
  50.8 18.0 %all-to-all-start.1 = ((bf16[8,192,128]{2,1,0:T(8,128)(2,1)}), bf16[8,192,128]{2,1,0:T(8,128)(2,1)S(1)}, u32[]{:S(2)}, u32[]{:S(2)}) async-start(bf16[8,192,128]{2,1,0:T(8,128)(2,1)} %broadcast_in_dim.8), calls=%async_computation.1 | async-start | bytes 786432 | tf_op jit(solution)/shard_map/all_to_all | solution.py:123
  68.9 17.8 %copy-start = (bf16[8,192,128]{2,1,0:T(8,128)(2,1)}, bf16[8,192,128]{2,1,0:T(8,128)(2,1)S(1)}, u32[]{:S(2)}) copy-start(bf16[8,192,128]{2,1,0:T(8,128)(2,1)S(1)} %all-to-all-done.1.refs_2_.refs_0_) | copy-start | bytes 1179652
  68.9 18.6 %all-to-all-start = ((f16[8,136,128]{2,1,0:T(8,128)(2,1)}), f16[8,136,128]{2,1,0:T(8,128)(2,1)S(1)}, u32[]{:S(2)}, u32[]{:S(2)}) async-start(f16[8,136,128]{2,1,0:T(8,128)(2,1)} %convert_element_type.33), calls=%async_computation | async-start | bytes 557056 | tf_op jit(solution)/shard_map/all_to_all | solution.py:566
  87.4 18.6 %all-to-all-start.2 = ((f16[8,136,128]{2,1,0:T(8,128)(2,1)}), f16[8,136,128]{2,1,0:T(8,128)(2,1)S(1)}, u32[]{:S(2)}, u32[]{:S(2)}) async-start(f16[8,136,128]{2,1,0:T(8,128)(2,1)} %convert_element_type.36), calls=%async_computation.2 | async-start | bytes 557056 | tf_op jit(solution)/shard_map/all_to_all | solution.py:566
  98.1 5.0 %collective-permute-start.9 = (bf16[1,128,128]{2,1,0:T(8,128)(2,1)}, bf16[1,128,128]{2,1,0:T(8,128)(2,1)S(1)}, u32[]{:S(2)}, u32[]{:S(2)}) collective-permute-start(bf16[1,128,128]{2,1,0:T(8,128)(2,1)} %shard_map.90), channel_id=1, source_target_pairs={{0,16},{4,20},{8,24},{12,28},{16,0},{20,4},{24,8},{28,12},{1,17},{... | collective-permute-start | bytes 98312 | tf_op jit(solution)/shard_map/ppermute | solution.py:40
  103.9 2.9 %copy-start.2 = (bf16[2,128,128]{2,1,0:T(8,128)(2,1)}, bf16[2,128,128]{2,1,0:T(8,128)(2,1)S(1)}, u32[]{:S(2)}) copy-start(bf16[2,128,128]{2,1,0:T(8,128)(2,1)S(1)} %pad_maximum_fusion.2.refs_0_.first_ref) | copy-start | bytes 196612
  103.9 5.4 %collective-permute-start.10 = (bf16[2,128,128]{2,1,0:T(8,128)(2,1)S(1)}, bf16[2,128,128]{2,1,0:T(8,128)(2,1)S(1)}, u32[]{:S(2)}, u32[]{:S(2)}) collective-permute-start(bf16[2,128,128]{2,1,0:T(8,128)(2,1)S(1)} %pad_maximum_fusion.2.refs_0_.first_ref), channel_id=1, source_target_pairs={{0,8},{4,12},{8,0},{12,4},{16,24},{20,28},{24,16},{28,20},{1,9},{5... | collective-permute-start | bytes 196616 | tf_op jit(solution)/shard_map/ppermute | solution.py:40
  109.3 0.6 copy-start.9
  111.6 14.3 %all-to-all-start.3 = ((bf16[8,128,128]{2,1,0:T(8,128)(2,1)}), bf16[8,128,128]{2,1,0:T(8,128)(2,1)S(1)}, u32[]{:S(2)}, u32[]{:S(2)}) async-start(bf16[8,128,128]{2,1,0:T(8,128)(2,1)} %get-tuple-element.41), calls=%async_computation.3 | async-start | bytes 524288 | tf_op jit(solution)/shard_map/all_to_all | solution.py:123
  116.9 6.2 %collective-permute-start.11 = (bf16[4,128,128]{2,1,0:T(8,128)(2,1)}, bf16[4,128,128]{2,1,0:T(8,128)(2,1)S(1)}, u32[]{:S(2)}, u32[]{:S(2)}) collective-permute-start(bf16[4,128,128]{2,1,0:T(8,128)(2,1)} %get-tuple-element.42.refs_0_), channel_id=1, source_target_pairs={{0,4},{4,0},{8,12},{12,8},{16,20},{20,16},{24,28},{28,24},{1,5},{5... | collective-permute-start | bytes 393224 | tf_op jit(solution)/shard_map/ppermute | solution.py:40
  123.1 0.9 copy-start.1
  127.7 1.6 %collective-permute-start.12 = (f32[2,32,1024]{2,1,0:T(8,128)S(1)}, f32[2,32,1024]{2,1,0:T(8,128)S(1)}, u32[]{:S(2)}, u32[]{:S(2)}) collective-permute-start(f32[2,32,1024]{2,1,0:T(8,128)S(1)} %get-tuple-element.44), channel_id=1, source_target_pairs={{0,1},{1,0},{2,3},{3,2},{4,5},{5,4},{6,7},{7,6},{8,9},{9,8},{10,11... | collective-permute-start | bytes 786440 | tf_op jit(solution)/shard_map/ppermute | solution.py:40
  129.4 4.3 %collective-permute-start.13 = (f16[1,32,1024]{2,1,0:T(8,128)(2,1)S(1)}, f16[1,32,1024]{2,1,0:T(8,128)(2,1)S(1)}, u32[]{:S(2)}, u32[]{:S(2)}) collective-permute-start(f16[1,32,1024]{2,1,0:T(8,128)(2,1)S(1)} %multiply_convert_fusion), channel_id=1, source_target_pairs={{0,2},{1,3},{2,0},{3,1},{4,6},{5,7},{6,4},{7,5},{8,10},{9,11},{10,... | collective-permute-start | bytes 196616 | tf_op jit(solution)/shard_map/ppermute | solution.py:40

commit v7 on v5

--- a/solution.py
+++ b/solution.py
@@ -17,6 +17,7 @@
 STAT_ROWS = 8
 VMEM_GRANT = 51 << 20
 PROJECT_GRANT = 56 << 20
+OUTPUT_GRANT = 16 << 20
 NT = (((1,), (1,)), ((), ()))
 
 OUTPUT_SCALE = 2.0**12
@@ -40,8 +41,8 @@
     return lax.ppermute(array, axis, [(i, i ^ mask) for i in range(size)])
 
 
-def owners_sum(keep, send, me):
-    total = keep + swap(send, "seq", 1)
+def owners_sum(keep, received, me):
+    total = keep + received
     mask = 2
     while mask < lax.axis_size("seq"):
         bit = me // mask % 2
@@ -78,8 +79,9 @@
     return lax.all_to_all(copies, "seq", 0, 0)
 
 
-def project_kernel(me_ref, hidden_ref, *refs, extra, chunk, blocks, pieces):
-    weight_refs, refs = refs[: 1 + extra], refs[1 + extra :]
+def project_kernel(me_ref, hidden_ref, *refs, extra, carried, chunk, blocks, pieces):
+    weight_refs, refs = refs[: 1 + extra], refs[1 + extra + carried :]
+    refs = refs[:2] + refs[2 + carried :]
     keep_ref, send_ref, q_all, *others_all, sems = refs
     tokens, depth = hidden_ref.shape
     odd = lax.rem(me_ref[0], 2) == 1
@@ -129,7 +131,7 @@
         deal(jnp.concatenate(both, axis=1), 1)
 
 
-def project(me, hidden, query_weight, others, chunk, columns, count):
+def project(me, hidden, query_weight, others, carried, chunk, columns, count):
     tokens, depth = hidden.shape
     wide = columns + sum(other.shape[1] for other in others)
     pieces = max(1, depth // 256)
@@ -137,11 +139,17 @@
     shape = jax.ShapeDtypeStruct((count // 2, sum(blocks), LANES), jnp.float32)
     return pl.pallas_call(
         functools.partial(
-            project_kernel, extra=len(others), chunk=chunk, blocks=blocks, pieces=pieces
+            project_kernel,
+            extra=len(others),
+            carried=len(carried),
+            chunk=chunk,
+            blocks=blocks,
+            pieces=pieces,
         ),
-        out_shape=[shape] * 2,
-        in_specs=[smem_spec(), vmem_spec()] + [hbm_spec()] * (1 + len(others)),
-        out_specs=[vmem_spec()] * 2,
+        out_shape=[shape] * 2 + [jax.ShapeDtypeStruct(one.shape, one.dtype) for one in carried],
+        in_specs=[smem_spec(), vmem_spec()] + [hbm_spec()] * (1 + len(others) + len(carried)),
+        out_specs=[vmem_spec()] * 2 + [hbm_spec()] * len(carried),
+        input_output_aliases={3 + len(others) + i: 2 + i for i in range(len(carried))},
         scratch_shapes=[pltpu.VMEM((depth, columns), jnp.bfloat16)]
         + [pltpu.VMEM(other.shape, jnp.bfloat16) for other in others]
         + [pltpu.SemaphoreType.DMA((pieces + len(others),))],
@@ -151,7 +159,7 @@
             bytes_accessed=2 * depth * wide,
             transcendentals=0,
         ),
-    )(me, hidden, query_weight, *others)
+    )(me, hidden, query_weight, *others, *carried)
 
 
 def attention_kernel(len_ref, me_ref, *refs, sources, band, step, block, head):
@@ -322,40 +330,45 @@
     )(length, me, *queries, keys, values)
 
 
-def fresh_kernel(me_ref, q_ref, last_ref, out_ref, stat_ref, kv_all, *, block, tokens, head):
+def fresh_kernel(me_ref, *refs, heads, block, tokens):
+    q_refs, last_ref, outs, kv_all = refs[:heads], refs[heads], refs[heads + 1 : -1], refs[-1]
     kv_block = last_ref.shape[1] - block
     for k in range(last_ref.shape[0]):
         rows = last_ref[k, block:, :].astype(jnp.float32)
         kv_all[k * kv_block : (k + 1) * kv_block, :] = rows
-    half = kv_all.shape[0] // 2
-    keys = kv_all[head * tokens : (head + 1) * tokens, :].astype(jnp.bfloat16)
-    values = kv_all[half + head * tokens : half + (head + 1) * tokens, :].astype(jnp.bfloat16)
-
-    s = lax.dot_general(q_ref[0, :block, :], keys, NT, preferred_element_type=jnp.float32)
-    s = s * (math.log2(math.e) / math.sqrt(HD))
-    token = lax.rem(me_ref[0] * block, tokens) + lax.broadcasted_iota(jnp.int32, s.shape, 0)
-    visible = lax.broadcasted_iota(jnp.int32, s.shape, 1) <= token
-    s = jnp.where(visible, s, NEG_BIG)
-    top = jnp.max(s, axis=1, keepdims=True)
-    weights = jnp.where(visible, jnp.exp2(s - top), 0.0).astype(jnp.bfloat16)
-    total = jnp.sum(weights.astype(jnp.float32), axis=1, keepdims=True)
-    out_ref[...] = jnp.dot(weights, values, preferred_element_type=jnp.float32)
-    lane = lax.broadcasted_iota(jnp.int32, stat_ref.shape, 1)
-    stat_ref[...] = jnp.where(lane < LANES // 2, top, total)
-
-
-def fresh(me, mine, last, block, tokens, head):
+    half = heads * tokens
+    for head in range(heads):
+        q_ref, (out_ref, stat_ref) = q_refs[head], outs[2 * head : 2 * head + 2]
+        first = head * tokens
+        keys = kv_all[first : first + tokens, :].astype(jnp.bfloat16)
+        values = kv_all[half + first : half + first + tokens, :].astype(jnp.bfloat16)
+        s = lax.dot_general(q_ref[0, :block, :], keys, NT, preferred_element_type=jnp.float32)
+        s = s * (math.log2(math.e) / math.sqrt(HD))
+        token = lax.rem(me_ref[0] * block, tokens) + lax.broadcasted_iota(jnp.int32, s.shape, 0)
+        visible = lax.broadcasted_iota(jnp.int32, s.shape, 1) <= token
+        s = jnp.where(visible, s, NEG_BIG)
+        top = jnp.max(s, axis=1, keepdims=True)
+        weights = jnp.where(visible, jnp.exp2(s - top), 0.0).astype(jnp.bfloat16)
+        total = jnp.sum(weights.astype(jnp.float32), axis=1, keepdims=True)
+        out_ref[...] = jnp.dot(weights, values, preferred_element_type=jnp.float32)
+        lane = lax.broadcasted_iota(jnp.int32, stat_ref.shape, 1)
+        stat_ref[...] = jnp.where(lane < LANES // 2, top, total)
+
+
+def fresh(me, mine, last, block, tokens):
+    heads = len(mine)
     kv_rows = last.shape[0] * (last.shape[1] - block)
     return pl.pallas_call(
-        functools.partial(fresh_kernel, block=block, tokens=tokens, head=head),
-        out_shape=[jax.ShapeDtypeStruct((block, HD), jnp.float32)] * 2,
-        in_specs=[smem_spec()] + [vmem_spec()] * 2,
-        out_specs=[vmem_spec()] * 2,
+        functools.partial(fresh_kernel, heads=heads, block=block, tokens=tokens),
+        out_shape=[jax.ShapeDtypeStruct((block, HD), jnp.float32)] * (2 * heads),
+        in_specs=[smem_spec()] + [vmem_spec()] * (heads + 1),
+        out_specs=[vmem_spec()] * (2 * heads),
         scratch_shapes=[pltpu.VMEM((kv_rows, HD), jnp.float32)],
-    )(me, mine, last)
-
-
-def merge_kernel(me_ref, part_ref, out_ref, stat_ref, copies_ref, turned):
+    )(me, *mine, last)
+
+
+def merge_kernel(me_ref, part_ref, out_ref, stat_ref, *refs):
+    copies_ref, turned = refs[-2:]
     count = part_ref.shape[0]
     block = out_ref.shape[0]
     new_top = stat_ref[:, 0:1]
@@ -376,60 +389,41 @@
         whole_out = whole_out + part_ref[k, :block, :] * scaled[:, k : k + 1]
     attended = (whole_out / whole_total).astype(jnp.bfloat16)
     for k in range(copies_ref.shape[0]):
-        copies_ref[k] = attended
-
-
-def merge(me, parts, new_out, new_stat, copies):
+        for i, ref in enumerate(refs[:-2]):
+            copies_ref[k, i * block : (i + 1) * block, :] = ref[0]
+        copies_ref[k, (len(refs) - 2) * block :, :] = attended
+
+
+def merge(me, parts, new_out, new_stat, before, copies):
+    block = new_out.shape[0]
+    shape = (copies, (len(before) + 1) * block, HD)
     return pl.pallas_call(
         merge_kernel,
-        out_shape=jax.ShapeDtypeStruct((copies,) + new_out.shape, jnp.bfloat16),
-        in_specs=[smem_spec()] + [vmem_spec()] * 3,
+        out_shape=jax.ShapeDtypeStruct(shape, jnp.bfloat16),
+        in_specs=[smem_spec()] + [vmem_spec()] * (3 + len(before)),
         out_specs=vmem_spec(),
         scratch_shapes=[pltpu.VMEM((LANES, parts.shape[0]), jnp.float32)],
-    )(me, parts, new_out, new_stat)
-
-
-def output_kernel(
-    me_ref, place_ref, w_hbm, *refs, sources, tokens, groups, chunk, has_before, last
-):
-    a_refs, refs = refs[:sources], refs[sources:]
-    before = refs[0] if has_before else None
-    outs, (w_all, a_all, total, sems) = refs[int(has_before) : -4], refs[-4:]
-    copies = []
-    for g in range(groups):
-        copies.append(
-            pltpu.make_async_copy(
-                w_hbm.at[pl.ds((chunk * groups + g) * HD, HD), :],
-                w_all.at[pl.ds(g * HD, HD), :],
-                sems.at[g],
-            )
-        )
-        copies[-1].start()
-    half, block = a_refs[0].shape[:2]
-    per = sources * half // groups
-    if sources == 1:
-        pieces = [a_refs[0][g * per : (g + 1) * per].reshape(tokens, HD) for g in range(groups)]
-    else:
-        for k, offset in enumerate(doubling_offsets(sources * half)):
-            owner = me_ref[0] ^ offset
-            start = pl.multiple_of(lax.rem(owner, per) * block, block)
-            a_all[owner // per, pl.ds(start, block), :] = a_refs[k // half][k % half]
-        pieces = [a_all[g] for g in range(groups)]
-    product = before[...] if has_before else None
-    for g in range(0, groups, 2):
-        copies[g].wait()
-        copies[g + 1].wait()
+    )(me, parts, new_out, new_stat, *before)
+
+
+def output_kernel(place_ref, w_ref, a_ref, keep_ref, send_ref, total, *, block):
+    count, rows = a_ref.shape[:2]
+    tokens = total.shape[0]
+    per = tokens // block
+    groups = count // per
+    product = None
+    for j in range(rows // block):
+        here = slice(j * block, (j + 1) * block)
+        pieces = [
+            a_ref[g * per : (g + 1) * per, here, :].reshape(tokens, HD) for g in range(groups)
+        ]
         term = jnp.dot(
-            jnp.concatenate(pieces[g : g + 2], axis=1),
-            w_all[g * HD : (g + 2) * HD, :],
+            jnp.concatenate(pieces, axis=1),
+            w_ref[j * groups * HD : (j + 1) * groups * HD, :],
             preferred_element_type=jnp.float32,
         )
         product = term if product is None else product + term
-    if not last:
-        outs[0][...] = product
-        return
     total[...] = product
-    keep_ref, send_ref = outs
     share = keep_ref.shape[1]
     odd = lax.rem(place_ref[0], 2)
     for i in range(keep_ref.shape[0]):
@@ -438,41 +432,22 @@
             ref[i] = total[pl.ds(start, share), :]
 
 
-def output_part(me, place, weight, attended, tokens, before, chunk, heads, last):
-    groups = QH // KVH
-    width = weight.shape[1]
-    has_before = before is not None
-    shapes = [jax.ShapeDtypeStruct((tokens, width), jnp.float32)]
-    if last:
-        shapes = [jax.ShapeDtypeStruct((heads // 2, tokens // heads, width), jnp.float32)] * 2
+def output_halves(place, weight, attended, block, tokens, heads):
+    depth, width = weight.shape
+    shape = jax.ShapeDtypeStruct((heads // 2, tokens // heads, width), jnp.float32)
     return pl.pallas_call(
-        functools.partial(
-            output_kernel,
-            sources=len(attended),
-            tokens=tokens,
-            groups=groups,
-            chunk=chunk,
-            has_before=has_before,
-            last=last,
-        ),
-        out_shape=shapes,
-        in_specs=[smem_spec()] * 2
-        + [hbm_spec()]
-        + [vmem_spec()] * (len(attended) + int(has_before)),
-        out_specs=[vmem_spec()] * len(shapes),
-        scratch_shapes=[
-            pltpu.VMEM((groups * HD, width), jnp.bfloat16),
-            pltpu.VMEM((groups, tokens, HD), jnp.bfloat16),
-            pltpu.VMEM((tokens, width), jnp.float32),
-            pltpu.SemaphoreType.DMA((groups,)),
-        ],
-        compiler_params=pltpu.CompilerParams(vmem_limit_bytes=VMEM_GRANT),
+        functools.partial(output_kernel, block=block),
+        out_shape=[shape] * 2,
+        in_specs=[smem_spec()] + [vmem_spec()] * 2,
+        out_specs=[vmem_spec()] * 2,
+        scratch_shapes=[pltpu.VMEM((tokens, width), jnp.float32)],
+        compiler_params=pltpu.CompilerParams(vmem_limit_bytes=OUTPUT_GRANT),
         cost_estimate=pl.CostEstimate(
-            flops=2 * tokens * groups * HD * width,
-            bytes_accessed=2 * groups * HD * width,
+            flops=2 * tokens * depth * width,
+            bytes_accessed=2 * depth * width,
             transcendentals=0,
         ),
-    )(me, place, weight, *attended, *([before] if has_before else []))
+    )(place, weight, attended)
 
 
 def shards(
@@ -494,30 +469,36 @@
     me = lax.axis_index("seq").reshape(1)
     place = lax.axis_index("head").reshape(1)
 
+    kept, received = [], []
+    for j in range(kv_local):
+        others = [key_weight, value_weight] if j == kv_local - 1 else []
+        keep, send, *kept = project(
+            me, hidden, query_weight, others, kept, j, columns, count
+        )
+        kept.append(keep)
+        received.append(swap(send, "seq", 1))
     mine, queries = [], []
     for j in range(kv_local):
-        last = j == kv_local - 1
-        others = [key_weight, value_weight] if last else []
-        keep, send = project(me, hidden, query_weight, others, j, columns, count)
-        mine.append(owners_sum(keep, send, me[0]))
-        if last:
+        mine.append(owners_sum(kept[j], received[j], me[0]))
+        if j == kv_local - 1:
             copies = jnp.broadcast_to(mine[j], (count,) + mine[j].shape[1:])
             queries.append([gather_at_once(copies)])
         else:
             queries.append(gather_doubling(mine[j]))
 
-    mixed = None
+    fresh_parts = fresh(me, mine, queries[-1][0], block, tokens)
+    before = []
     for j in range(kv_local):
-        last = j == kv_local - 1
         parts = attention(queries[j], block, cache_keys, cache_values, cache_lens, me, j)
         parts = lax.all_to_all(parts.astype(jnp.float16), "seq", 0, 0).astype(jnp.float32)
-        new_out, new_stat = fresh(me, mine[j], queries[-1][0], block, tokens, j)
-        copies = merge(me, parts, new_out, new_stat, count if last else 1)
-        attended = [gather_at_once(copies)] if last else gather_doubling(copies)
-        result = output_part(
-            me, place, output_weight, attended, tokens, mixed, j, heads, last
-        )
-        mixed = result if last else result[0]
+        new_out, new_stat = fresh_parts[2 * j : 2 * j + 2]
+        last = j == kv_local - 1
+        attended = merge(
+            me, parts, new_out, new_stat, before if last else [], count if last else 1
+        )
+        before.append(attended)
+    attended = gather_at_once(before[-1])
+    mixed = output_halves(place, output_weight, attended, block, tokens, heads)
 
     keep, send = mixed
     mixed = keep + swap(send, "head", 1)

time: 129 us -> 121 us (0.938); the launches traced: 129 us -> 119 us
  starting transfers between devices: 46 us -> 37.2 us
  Pallas kernels: 45.9 us -> 41.2 us
  waiting for transfers between devices: 27.8 us -> 30.9 us
  local copies, waits for them, and re-layouts: 0.88 us -> 3.09 us
  other arithmetic: 7.6 us -> 6.03 us
    all_to_all x2, waiting for transfers between devices: 0.01 us -> 10.2 us  [gather_at_once(): return lax.all_to_all(copies, 'seq', 0, 0)]
    ppermute x14 -> x11, waiting for transfers between devices: 27.8 us -> 18 us  [swap(): return lax.ppermute(array, axis, [(i, i ^ mask) for i in range(size)])]
    ppermute x14 -> x11, starting transfers between devices: 27 us -> 20.2 us  [swap(): return lax.ppermute(array, axis, [(i, i ^ mask) for i in range(size)])]
    pallas_call x8 -> x6, Pallas kernels: 20.5 us -> 15.8 us  [the longest x2 7.75 us: project(): pl.pallas_call(functools.partial(project_kernel, extra=len(others), carri...]
    all_to_all x2, waiting for transfers between devices: 0.01 us -> 2.75 us  [shards(): lax.all_to_all(parts.astype(jnp.float16), 'seq', 0, 0).astype(jnp.float32)]
    unnamed x6 -> x8, local copies, waits for them, and re-layouts: 0.01 us -> 2.2 us
    all_to_all x2, starting transfers between devices: 11.9 us -> 10.1 us  [shards(): lax.all_to_all(parts.astype(jnp.float16), 'seq', 0, 0).astype(jnp.float32)]
    concatenate x4 -> x2, other arithmetic: 1.56 us -> 0.02 us  [gather_doubling(): block = jnp.concatenate([block, swap(block, 'seq', mask)])]
  transfers between devices with their start and end apart: 18 -> 15, of which waited for: 9 -> 10; matrix products, arithmetic and copies ran while one was open for 5% -> 4% of each run, Pallas kernels for 31% -> 29%
where the time goes in v7:
time: 121 us; the launch traced here: 119 us
  Pallas kernels  41.2 us (34%)
  starting transfers between devices  37.2 us (31%)
  waiting for transfers between devices  30.9 us (26%)
  other arithmetic  6.03 us (5%)
  local copies, waits for them, and re-layouts  3.09 us (3%)
    pallas_call x2, Pallas kernels, attention(): pl.pallas_call(functools.partial(attention_kernel, sources=sources, band=...  25.4 us
    ppermute x11, starting transfers between devices, swap(): return lax.ppermute(array, axis, [(i, i ^ mask) for i in range(size)])  20.2 us
    ppermute x11, waiting for transfers between devices, swap(): return lax.ppermute(array, axis, [(i, i ^ mask) for i in range(size)])  18 us
    all_to_all x2, waiting for transfers between devices, gather_at_once(): return lax.all_to_all(copies, 'seq', 0, 0)  10.2 us
    all_to_all x2, starting transfers between devices, shards(): lax.all_to_all(parts.astype(jnp.float16), 'seq', 0, 0).astype(jnp.float32)  10.1 us
    pallas_call x2, Pallas kernels, project(): pl.pallas_call(functools.partial(project_kernel, extra=len(others), carri...  7.75 us
    all_to_all x2, starting transfers between devices, gather_at_once(): return lax.all_to_all(copies, 'seq', 0, 0)  6.94 us
    pallas_call x2, Pallas kernels, merge(): pl.pallas_call(merge_kernel, out_shape=jax.ShapeDtypeStruct(shape, jnp.bf...  5.06 us
  transfers between devices with their start and end apart: 15, of which 10 were waited for; matrix products, arithmetic and copies ran while one was open for 4% of the time, Pallas kernels for 29%

profile of v7, /device:TPU:0, one launch (start us, length us, event | category | flops | bytes accessed | tf_op | source)
XLA Modules:
  0.0 119.4 jit_solution(450081474303131455)
XLA Ops:
  0.0 3.5 %shard_map.82 = (f32[4,128,128]{2,1,0:T(8,128)}, f32[4,128,128]{2,1,0:T(8,128)}) custom-call(s32[1]{0:T(128)} %bitcast.1.me_ref, bf16[128,1024]{1,0:T(8,128)(2,1)} %hidden_ref.3, bf16[1024,2048]{1,0:T(8,128)(2,1)} %refs_0_.3), custom_call_target="tpu_custom_call" | custom-call | flops 268435456 | bytes 2097152 | tf_op jit(solution)/shard_map/pallas_call | solution.py:140
  3.5 3.0 %collective-permute-start.3 = (f32[4,128,128]{2,1,0:T(8,128)}, f32[4,128,128]{2,1,0:T(8,128)S(1)}, u32[]{:S(2)}, u32[]{:S(2)}) collective-permute-start(f32[4,128,128]{2,1,0:T(8,128)} %get-tuple-element.20), channel_id=1, source_target_pairs={{0,4},{4,0},{8,12},{12,8},{16,20},{20,16},{24,28},{28,24},{1,5},{5... | collective-permute-start | bytes 786440 | tf_op jit(solution)/shard_map/ppermute | solution.py:41
  6.5 4.2 %shard_map.83 = (f32[4,192,128]{2,1,0:T(8,128)}, f32[4,192,128]{2,1,0:T(8,128)}, f32[4,128,128]{2,1,0:T(8,128)}) custom-call(s32[1]{0:T(128)} %bitcast.1.me_ref, bf16[128,1024]{1,0:T(8,128)(2,1)} %hidden_ref.3, bf16[1024,2048]{1,0:T(8,128)(2,1)} %refs_0_.3, bf16[1024,256]{1,0:T(8,128)(2,1)} %refs_1_.2, ...), custom_call_target="tpu_custom_call", output_to_operand_aliasing={{2}: (5, {})} | custom-call | flops 402653184 | bytes 3145728 | tf_op jit(solution)/shard_map/pallas_call | solution.py:140
  10.8 2.3 %collective-permute-done.3 = f32[4,128,128]{2,1,0:T(8,128)S(1)} collective-permute-done((f32[4,128,128]{2,1,0:T(8,128)}, f32[4,128,128]{2,1,0:T(8,128)S(1)}, u32[]{:S(2)}, u32[]{:S(2)}) %collective-permute-start.3) | collective-permute-done | bytes 262176 | tf_op jit(solution)/shard_map/ppermute | solution.py:41
  13.0 1.0 add.78
  14.1 1.9 %collective-permute-start.4 = (f32[2,128,128]{2,1,0:T(8,128)S(1)}, f32[2,128,128]{2,1,0:T(8,128)S(1)}, u32[]{:S(2)}, u32[]{:S(2)}) collective-permute-start(f32[2,128,128]{2,1,0:T(8,128)S(1)} %dynamic-slice_bitcast_fusion.1), channel_id=1, source_target_pairs={{0,8},{4,12},{8,0},{12,4},{16,24},{20,28},{24,16},{28,20},{1,9},{5... | collective-permute-start | bytes 393224 | tf_op jit(solution)/shard_map/ppermute | solution.py:41
  15.9 1.5 %collective-permute-start = (f32[4,192,128]{2,1,0:T(8,128)}, f32[4,192,128]{2,1,0:T(8,128)S(1)}, u32[]{:S(2)}, u32[]{:S(2)}) collective-permute-start(f32[4,192,128]{2,1,0:T(8,128)} %get-tuple-element.18), channel_id=1, source_target_pairs={{0,4},{4,0},{8,12},{12,8},{16,20},{20,16},{24,28},{28,24},{1,5},{5... | collective-permute-start | bytes 1179656 | tf_op jit(solution)/shard_map/ppermute | solution.py:41
  17.4 1.6 %collective-permute-done.4 = f32[2,128,128]{2,1,0:T(8,128)S(1)} collective-permute-done((f32[2,128,128]{2,1,0:T(8,128)S(1)}, f32[2,128,128]{2,1,0:T(8,128)S(1)}, u32[]{:S(2)}, u32[]{:S(2)}) %collective-permute-start.4) | collective-permute-done | bytes 131104 | tf_op jit(solution)/shard_map/ppermute | solution.py:41
  19.1 2.9 %collective-permute-start.5 = (f32[1,128,128]{2,1,0:T(8,128)S(1)}, f32[1,128,128]{2,1,0:T(8,128)S(1)}, u32[]{:S(2)}, u32[]{:S(2)}) collective-permute-start(f32[1,128,128]{2,1,0:T(8,128)S(1)} %constant_dynamic-slice_fusion), channel_id=1, source_target_pairs={{0,16},{4,20},{8,24},{12,28},{16,0},{20,4},{24,8},{28,12},{1,17},{... | collective-permute-start | bytes 196616 | tf_op jit(solution)/shard_map/ppermute | solution.py:41
  22.0 3.8 %collective-permute-done = f32[4,192,128]{2,1,0:T(8,128)S(1)} collective-permute-done((f32[4,192,128]{2,1,0:T(8,128)}, f32[4,192,128]{2,1,0:T(8,128)S(1)}, u32[]{:S(2)}, u32[]{:S(2)}) %collective-permute-start) | collective-permute-done | bytes 393248 | tf_op jit(solution)/shard_map/ppermute | solution.py:41
  25.9 1.0 add.69
  26.9 0.6 collective-permute-start.1
  27.5 0.0 collective-permute-done.5
  27.5 2.6 %collective-permute-start.6 = (bf16[1,128,128]{2,1,0:T(8,128)(2,1)S(1)}, bf16[1,128,128]{2,1,0:T(8,128)(2,1)S(1)}, u32[]{:S(2)}, u32[]{:S(2)}) collective-permute-start(bf16[1,128,128]{2,1,0:T(8,128)(2,1)S(1)} %add_convert_fusion.2.refs_0_), channel_id=1, source_target_pairs={{0,16},{4,20},{8,24},{12,28},{16,0},{20,4},{24,8},{28,12},{1,17},{... | collective-permute-start | bytes 98312 | tf_op jit(solution)/shard_map/ppermute | solution.py:41
  30.8 1.8 %collective-permute-done.6 = bf16[1,128,128]{2,1,0:T(8,128)(2,1)S(1)} collective-permute-done((bf16[1,128,128]{2,1,0:T(8,128)(2,1)S(1)}, bf16[1,128,128]{2,1,0:T(8,128)(2,1)S(1)}, u32[]{:S(2)}, u32[]{:S(2)}) %collective-permute-start.6) | collective-permute-done | bytes 32800 | tf_op jit(solution)/shard_map/ppermute | solution.py:41
  32.5 4.2 %collective-permute-start.7 = (bf16[2,128,128]{2,1,0:T(8,128)(2,1)S(1)}, bf16[2,128,128]{2,1,0:T(8,128)(2,1)S(1)}, u32[]{:S(2)}, u32[]{:S(2)}) collective-permute-start(bf16[2,128,128]{2,1,0:T(8,128)(2,1)S(1)} %pad_maximum_fusion.1), channel_id=1, source_target_pairs={{0,8},{4,12},{8,0},{12,4},{16,24},{20,28},{24,16},{28,20},{1,9},{5... | collective-permute-start | bytes 196616 | tf_op jit(solution)/shard_map/ppermute | solution.py:41
  36.7 0.0 collective-permute-done.1
  36.8 0.3 collective-permute-start.2
  37.1 1.9 %collective-permute-done.7 = bf16[2,128,128]{2,1,0:T(8,128)(2,1)S(1)} collective-permute-done((bf16[2,128,128]{2,1,0:T(8,128)(2,1)S(1)}, bf16[2,128,128]{2,1,0:T(8,128)(2,1)S(1)}, u32[]{:S(2)}, u32[]{:S(2)}) %collective-permute-start.7) | collective-permute-done | bytes 65568 | tf_op jit(solution)/shard_map/ppermute | solution.py:41
  39.0 1.6 %collective-permute-start.8 = (bf16[4,128,128]{2,1,0:T(8,128)(2,1)S(1)}, bf16[4,128,128]{2,1,0:T(8,128)(2,1)S(1)}, u32[]{:S(2)}, u32[]{:S(2)}) collective-permute-start(bf16[4,128,128]{2,1,0:T(8,128)(2,1)S(1)} %pad_maximum_fusion.refs_0_), channel_id=1, source_target_pairs={{0,4},{4,0},{8,12},{12,8},{16,20},{20,16},{24,28},{28,24},{1,5},{5... | collective-permute-start | bytes 393224 | tf_op jit(solution)/shard_map/ppermute | solution.py:41
  40.6 2.3 %collective-permute-done.2 = f32[1,192,128]{2,1,0:T(8,128)S(1)} collective-permute-done((f32[1,192,128]{2,1,0:T(8,128)S(1)}, f32[1,192,128]{2,1,0:T(8,128)S(1)}, u32[]{:S(2)}, u32[]{:S(2)}) %collective-permute-start.2) | collective-permute-done | bytes 98336 | tf_op jit(solution)/shard_map/ppermute | solution.py:41
  42.9 0.8 broadcast_in_dim.8
  43.7 3.5 %all-to-all-start = ((bf16[8,192,128]{2,1,0:T(8,128)(2,1)}), bf16[8,192,128]{2,1,0:T(8,128)(2,1)S(1)}, u32[]{:S(2)}, u32[]{:S(2)}) async-start(bf16[8,192,128]{2,1,0:T(8,128)(2,1)} %broadcast_in_dim.8), calls=%async_computation | async-start | bytes 786432 | tf_op jit(solution)/shard_map/all_to_all | solution.py:79
  47.2 0.0 collective-permute-done.8.refs_1_
  47.2 12.6 %shard_map.86 = f32[8,136,128]{2,1,0:T(8,128)S(1)} custom-call(s32[1]{0:T(128)S(6)} %copy.19.len_ref, s32[1]{0:T(128)} %bitcast.1.me_ref, bf16[4,128,128]{2,1,0:T(8,128)(2,1)S(1)} %pad_maximum_fusion.refs_0_, bf16[4,128,128]{2,1,0:T(8,128)(2,1)S(1)} %collective-permute-done.8.refs_1_, bf16[8192,256]{1,0:T(8,128)(2,1)} %refs_2_.5, bf16[8192,256]{1,0:T(8,128)(2,1)} %refs_3_.1), custom_call_target="tpu_custom_call" | custom-call | flops 8589934592 | bytes 4194304 | tf_op jit(solution)/shard_map/pallas_call | solution.py:305
  59.9 0.0 copy-done.2
  59.9 0.8 convert_element_type.36
  60.6 0.0 all-to-all-done.refs_0_.refs_2_
  60.6 5.0 %all-to-all-start.2 = ((f16[8,136,128]{2,1,0:T(8,128)(2,1)}), f16[8,136,128]{2,1,0:T(8,128)(2,1)S(1)}, u32[]{:S(2)}, u32[]{:S(2)}) async-start(f16[8,136,128]{2,1,0:T(8,128)(2,1)} %convert_element_type.36), calls=%async_computation.2 | async-start | bytes 557056 | tf_op jit(solution)/shard_map/all_to_all | solution.py:493
  65.6 12.7 %shard_map.84 = f32[8,136,128]{2,1,0:T(8,128)S(1)} custom-call(s32[1]{0:T(128)S(6)} %copy.19.len_ref, s32[1]{0:T(128)} %bitcast.1.me_ref, bf16[8,192,128]{2,1,0:T(8,128)(2,1)S(1)} %all-to-all-done.refs_0_.refs_2_, bf16[8192,256]{1,0:T(8,128)(2,1)} %refs_2_.5, bf16[8192,256]{1,0:T(8,128)(2,1)} %refs_3_.1), custom_call_target="tpu_custom_call" | custom-call | flops 8589934592 | bytes 4194304 | tf_op jit(solution)/shard_map/pallas_call | solution.py:305
  78.4 0.7 convert_element_type.33
  79.1 0.0 all-to-all-done.2
  79.1 5.1 %all-to-all-start.1 = ((f16[8,136,128]{2,1,0:T(8,128)(2,1)}), f16[8,136,128]{2,1,0:T(8,128)(2,1)S(1)}, u32[]{:S(2)}, u32[]{:S(2)}) async-start(f16[8,136,128]{2,1,0:T(8,128)(2,1)} %convert_element_type.33), calls=%async_computation.1 | async-start | bytes 557056 | tf_op jit(solution)/shard_map/all_to_all | solution.py:493
  84.3 0.9 convert_element_type.37.part_ref
  85.1 2.3 %shard_map.85 = (f32[128,128]{1,0:T(8,128)}, f32[128,128]{1,0:T(8,128)}, f32[128,128]{1,0:T(8,128)}, f32[128,128]{1,0:T(8,128)}) custom-call(s32[1]{0:T(128)} %bitcast.1.me_ref, bf16[1,128,128]{2,1,0:T(8,128)(2,1)} %copy-done.2, bf16[1,192,128]{2,1,0:T(8,128)(2,1)} %copy-done.3, bf16[8,192,128]{2,1,0:T(8,128)(2,1)} %copy-done.1), custom_call_target="tpu_custom_call" | custom-call | tf_op jit(solution)/shard_map/pallas_call | solution.py:361
  87.4 2.4 %shard_map.87.refs_0_ = bf16[1,128,128]{2,1,0:T(8,128)(2,1)} custom-call(s32[1]{0:T(128)} %bitcast.1.me_ref, f32[8,136,128]{2,1,0:T(8,128)} %convert_element_type.37.part_ref, f32[128,128]{1,0:T(8,128)} %get-tuple-element.23.out_ref, f32[128,128]{1,0:T(8,128)} %get-tuple-element.24.stat_ref), custom_call_target="tpu_custom_call" | custom-call | tf_op jit(solution)/shard_map/pallas_call | solution.py:400
  89.8 2.8 %all-to-all-done.1 = f16[8,136,128]{2,1,0:T(8,128)(2,1)S(1)} async-done(((f16[8,136,128]{2,1,0:T(8,128)(2,1)}), f16[8,136,128]{2,1,0:T(8,128)(2,1)S(1)}, u32[]{:S(2)}, u32[]{:S(2)}) %all-to-all-start.1) | async-done | bytes 278560 | tf_op jit(solution)/shard_map/all_to_all | solution.py:493
  92.6 0.9 convert_element_type.34.part_ref
  93.4 2.6 %shard_map.88 = bf16[8,256,128]{2,1,0:T(8,128)(2,1)} custom-call(s32[1]{0:T(128)} %bitcast.1.me_ref, f32[8,136,128]{2,1,0:T(8,128)} %convert_element_type.34.part_ref, f32[128,128]{1,0:T(8,128)} %get-tuple-element.21.out_ref, f32[128,128]{1,0:T(8,128)} %get-tuple-element.22.stat_ref, bf16[1,128,128]{2,1,0:T(8,128)(2,1)} %shard_map.87.refs_0_), custom_call_target="tpu_custom_call" | custom-call | tf_op jit(solution)/shard_map/pallas_call | solution.py:400
  96.1 3.5 %all-to-all-start.3 = ((bf16[8,256,128]{2,1,0:T(8,128)(2,1)}), bf16[8,256,128]{2,1,0:T(8,128)(2,1)S(1)}, u32[]{:S(2)}, u32[]{:S(2)}) async-start(bf16[8,256,128]{2,1,0:T(8,128)(2,1)} %shard_map.88), calls=%async_computation.3 | async-start | bytes 1048576 | tf_op jit(solution)/shard_map/all_to_all | solution.py:79
  99.6 10.2 %all-to-all-done.3.a_ref = bf16[8,256,128]{2,1,0:T(8,128)(2,1)S(1)} async-done(((bf16[8,256,128]{2,1,0:T(8,128)(2,1)}), bf16[8,256,128]{2,1,0:T(8,128)(2,1)S(1)}, u32[]{:S(2)}, u32[]{:S(2)}) %all-to-all-start.3) | async-done | bytes 524320 | tf_op jit(solution)/shard_map/all_to_all | solution.py:79
  109.8 2.2 %copy-done = bf16[2048,1024]{1,0:T(8,128)(2,1)S(1)} copy-done((bf16[2048,1024]{1,0:T(8,128)(2,1)S(1)}, bf16[2048,1024]{1,0:T(8,128)(2,1)}, u32[]{:S(2)}) %copy-start) | copy-done | bytes 4194328
  112.0 0.8 shard_map.89
  112.7 0.1 collective-permute-start.9
  112.8 1.5 %collective-permute-done.9 = f32[2,32,1024]{2,1,0:T(8,128)S(1)} collective-permute-done((f32[2,32,1024]{2,1,0:T(8,128)S(1)}, f32[2,32,1024]{2,1,0:T(8,128)S(1)}, u32[]{:S(2)}, u32[]{:S(2)}) %collective-permute-start.9) | collective-permute-done | bytes 262176 | tf_op jit(solution)/shard_map/ppermute | solution.py:41
  114.4 1.6 %collective-permute-start.10 = (f16[1,32,1024]{2,1,0:T(8,128)(2,1)S(1)}, f16[1,32,1024]{2,1,0:T(8,128)(2,1)S(1)}, u32[]{:S(2)}, u32[]{:S(2)}) collective-permute-start(f16[1,32,1024]{2,1,0:T(8,128)(2,1)S(1)} %multiply_convert_fusion), channel_id=1, source_target_pairs={{0,2},{1,3},{2,0},{3,1},{4,6},{5,7},{6,4},{7,5},{8,10},{9,11},{10,... | collective-permute-start | bytes 196616 | tf_op jit(solution)/shard_map/ppermute | solution.py:41
  116.0 2.7 %collective-permute-done.10 = f16[1,32,1024]{2,1,0:T(8,128)(2,1)S(1)} collective-permute-done((f16[1,32,1024]{2,1,0:T(8,128)(2,1)S(1)}, f16[1,32,1024]{2,1,0:T(8,128)(2,1)S(1)}, u32[]{:S(2)}, u32[]{:S(2)}) %collective-permute-start.10) | collective-permute-done | bytes 65568 | tf_op jit(solution)/shard_map/ppermute | solution.py:41
  118.7 0.6 fusion
  (18 shorter events, 0.2 us)
Async XLA Ops:
  3.5 9.5 %collective-permute-start.3 = (f32[4,128,128]{2,1,0:T(8,128)}, f32[4,128,128]{2,1,0:T(8,128)S(1)}, u32[]{:S(2)}, u32[]{:S(2)}) collective-permute-start(f32[4,128,128]{2,1,0:T(8,128)} %get-tuple-element.20), channel_id=1, source_target_pairs={{0,4},{4,0},{8,12},{12,8},{16,20},{20,16},{24,28},{28,24},{1,5},{5... | collective-permute-start | bytes 786440 | tf_op jit(solution)/shard_map/ppermute | solution.py:41
  14.1 5.0 %collective-permute-start.4 = (f32[2,128,128]{2,1,0:T(8,128)S(1)}, f32[2,128,128]{2,1,0:T(8,128)S(1)}, u32[]{:S(2)}, u32[]{:S(2)}) collective-permute-start(f32[2,128,128]{2,1,0:T(8,128)S(1)} %dynamic-slice_bitcast_fusion.1), channel_id=1, source_target_pairs={{0,8},{4,12},{8,0},{12,4},{16,24},{20,28},{24,16},{28,20},{1,9},{5... | collective-permute-start | bytes 393224 | tf_op jit(solution)/shard_map/ppermute | solution.py:41
  15.9 9.9 %collective-permute-start = (f32[4,192,128]{2,1,0:T(8,128)}, f32[4,192,128]{2,1,0:T(8,128)S(1)}, u32[]{:S(2)}, u32[]{:S(2)}) collective-permute-start(f32[4,192,128]{2,1,0:T(8,128)} %get-tuple-element.18), channel_id=1, source_target_pairs={{0,4},{4,0},{8,12},{12,8},{16,20},{20,16},{24,28},{28,24},{1,5},{5... | collective-permute-start | bytes 1179656 | tf_op jit(solution)/shard_map/ppermute | solution.py:41
  19.1 8.4 %collective-permute-start.5 = (f32[1,128,128]{2,1,0:T(8,128)S(1)}, f32[1,128,128]{2,1,0:T(8,128)S(1)}, u32[]{:S(2)}, u32[]{:S(2)}) collective-permute-start(f32[1,128,128]{2,1,0:T(8,128)S(1)} %constant_dynamic-slice_fusion), channel_id=1, source_target_pairs={{0,16},{4,20},{8,24},{12,28},{16,0},{20,4},{24,8},{28,12},{1,17},{... | collective-permute-start | bytes 196616 | tf_op jit(solution)/shard_map/ppermute | solution.py:41
  26.9 9.8 %collective-permute-start.1 = (f32[2,192,128]{2,1,0:T(8,128)S(1)}, f32[2,192,128]{2,1,0:T(8,128)S(1)}, u32[]{:S(2)}, u32[]{:S(2)}) collective-permute-start(f32[2,192,128]{2,1,0:T(8,128)S(1)} %dynamic-slice_bitcast_fusion), channel_id=1, source_target_pairs={{0,8},{4,12},{8,0},{12,4},{16,24},{20,28},{24,16},{28,20},{1,9},{5... | collective-permute-start | bytes 589832 | tf_op jit(solution)/shard_map/ppermute | solution.py:41
  27.5 32.3 %copy-start.2 = (bf16[1,128,128]{2,1,0:T(8,128)(2,1)}, bf16[1,128,128]{2,1,0:T(8,128)(2,1)S(1)}, u32[]{:S(2)}) copy-start(bf16[1,128,128]{2,1,0:T(8,128)(2,1)S(1)} %add_convert_fusion.2.refs_0_) | copy-start | bytes 98308
  27.5 5.0 %collective-permute-start.6 = (bf16[1,128,128]{2,1,0:T(8,128)(2,1)S(1)}, bf16[1,128,128]{2,1,0:T(8,128)(2,1)S(1)}, u32[]{:S(2)}, u32[]{:S(2)}) collective-permute-start(bf16[1,128,128]{2,1,0:T(8,128)(2,1)S(1)} %add_convert_fusion.2.refs_0_), channel_id=1, source_target_pairs={{0,16},{4,20},{8,24},{12,28},{16,0},{20,4},{24,8},{28,12},{1,17},{... | collective-permute-start | bytes 98312 | tf_op jit(solution)/shard_map/ppermute | solution.py:41
  32.5 6.4 %collective-permute-start.7 = (bf16[2,128,128]{2,1,0:T(8,128)(2,1)S(1)}, bf16[2,128,128]{2,1,0:T(8,128)(2,1)S(1)}, u32[]{:S(2)}, u32[]{:S(2)}) collective-permute-start(bf16[2,128,128]{2,1,0:T(8,128)(2,1)S(1)} %pad_maximum_fusion.1), channel_id=1, source_target_pairs={{0,8},{4,12},{8,0},{12,4},{16,24},{20,28},{24,16},{28,20},{1,9},{5... | collective-permute-start | bytes 196616 | tf_op jit(solution)/shard_map/ppermute | solution.py:41
  36.8 6.1 %collective-permute-start.2 = (f32[1,192,128]{2,1,0:T(8,128)S(1)}, f32[1,192,128]{2,1,0:T(8,128)S(1)}, u32[]{:S(2)}, u32[]{:S(2)}) collective-permute-start(f32[1,192,128]{2,1,0:T(8,128)S(1)} %constant_dynamic-slice_fusion.1), channel_id=1, source_target_pairs={{0,16},{4,20},{8,24},{12,28},{16,0},{20,4},{24,8},{28,12},{1,17},{... | collective-permute-start | bytes 294920 | tf_op jit(solution)/shard_map/ppermute | solution.py:41
  39.0 8.2 %collective-permute-start.8 = (bf16[4,128,128]{2,1,0:T(8,128)(2,1)S(1)}, bf16[4,128,128]{2,1,0:T(8,128)(2,1)S(1)}, u32[]{:S(2)}, u32[]{:S(2)}) collective-permute-start(bf16[4,128,128]{2,1,0:T(8,128)(2,1)S(1)} %pad_maximum_fusion.refs_0_), channel_id=1, source_target_pairs={{0,4},{4,0},{8,12},{12,8},{16,20},{20,16},{24,28},{28,24},{1,5},{5... | collective-permute-start | bytes 393224 | tf_op jit(solution)/shard_map/ppermute | solution.py:41
  42.9 17.0 %copy-start.3 = (bf16[1,192,128]{2,1,0:T(8,128)(2,1)}, bf16[1,192,128]{2,1,0:T(8,128)(2,1)S(1)}, u32[]{:S(2)}) copy-start(bf16[1,192,128]{2,1,0:T(8,128)(2,1)S(1)} %add_convert_fusion.1.refs_1_) | copy-start | bytes 147460
  43.7 16.9 %all-to-all-start = ((bf16[8,192,128]{2,1,0:T(8,128)(2,1)}), bf16[8,192,128]{2,1,0:T(8,128)(2,1)S(1)}, u32[]{:S(2)}, u32[]{:S(2)}) async-start(bf16[8,192,128]{2,1,0:T(8,128)(2,1)} %broadcast_in_dim.8), calls=%async_computation | async-start | bytes 786432 | tf_op jit(solution)/shard_map/all_to_all | solution.py:79
  60.6 17.7 %copy-start.1 = (bf16[8,192,128]{2,1,0:T(8,128)(2,1)}, bf16[8,192,128]{2,1,0:T(8,128)(2,1)S(1)}, u32[]{:S(2)}) copy-start(bf16[8,192,128]{2,1,0:T(8,128)(2,1)S(1)} %all-to-all-done.refs_0_.refs_2_) | copy-start | bytes 1179652
  60.6 18.5 %all-to-all-start.2 = ((f16[8,136,128]{2,1,0:T(8,128)(2,1)}), f16[8,136,128]{2,1,0:T(8,128)(2,1)S(1)}, u32[]{:S(2)}, u32[]{:S(2)}) async-start(f16[8,136,128]{2,1,0:T(8,128)(2,1)} %convert_element_type.36), calls=%async_computation.2 | async-start | bytes 557056 | tf_op jit(solution)/shard_map/all_to_all | solution.py:493
  79.1 13.5 %all-to-all-start.1 = ((f16[8,136,128]{2,1,0:T(8,128)(2,1)}), f16[8,136,128]{2,1,0:T(8,128)(2,1)S(1)}, u32[]{:S(2)}, u32[]{:S(2)}) async-start(f16[8,136,128]{2,1,0:T(8,128)(2,1)} %convert_element_type.33), calls=%async_computation.1 | async-start | bytes 557056 | tf_op jit(solution)/shard_map/all_to_all | solution.py:493
  96.1 13.7 %all-to-all-start.3 = ((bf16[8,256,128]{2,1,0:T(8,128)(2,1)}), bf16[8,256,128]{2,1,0:T(8,128)(2,1)S(1)}, u32[]{:S(2)}, u32[]{:S(2)}) async-start(bf16[8,256,128]{2,1,0:T(8,128)(2,1)} %shard_map.88), calls=%async_computation.3 | async-start | bytes 1048576 | tf_op jit(solution)/shard_map/all_to_all | solution.py:79
  109.8 2.2 %copy-start = (bf16[2048,1024]{1,0:T(8,128)(2,1)S(1)}, bf16[2048,1024]{1,0:T(8,128)(2,1)}, u32[]{:S(2)}) copy-start(bf16[2048,1024]{1,0:T(8,128)(2,1)} %w_ref.1) | copy-start | bytes 12582916
  112.7 1.6 %collective-permute-start.9 = (f32[2,32,1024]{2,1,0:T(8,128)S(1)}, f32[2,32,1024]{2,1,0:T(8,128)S(1)}, u32[]{:S(2)}, u32[]{:S(2)}) collective-permute-start(f32[2,32,1024]{2,1,0:T(8,128)S(1)} %get-tuple-element.26), channel_id=1, source_target_pairs={{0,1},{1,0},{2,3},{3,2},{4,5},{5,4},{6,7},{7,6},{8,9},{9,8},{10,11... | collective-permute-start | bytes 786440 | tf_op jit(solution)/shard_map/ppermute | solution.py:41
  114.4 4.3 %collective-permute-start.10 = (f16[1,32,1024]{2,1,0:T(8,128)(2,1)S(1)}, f16[1,32,1024]{2,1,0:T(8,128)(2,1)S(1)}, u32[]{:S(2)}, u32[]{:S(2)}) collective-permute-start(f16[1,32,1024]{2,1,0:T(8,128)(2,1)S(1)} %multiply_convert_fusion), channel_id=1, source_target_pairs={{0,2},{1,3},{2,0},{3,1},{4,6},{5,7},{6,4},{7,5},{8,10},{9,11},{10,... | collective-permute-start | bytes 196616 | tf_op jit(solution)/shard_map/ppermute | solution.py:41

commit v8 on v7

--- a/solution.py
+++ b/solution.py
@@ -17,7 +17,7 @@
 STAT_ROWS = 8
 VMEM_GRANT = 51 << 20
 PROJECT_GRANT = 56 << 20
-OUTPUT_GRANT = 16 << 20
+SMALL_GRANT = 16 << 20
 NT = (((1,), (1,)), ((), ()))
 
 OUTPUT_SCALE = 2.0**12
@@ -41,48 +41,45 @@
     return lax.ppermute(array, axis, [(i, i ^ mask) for i in range(size)])
 
 
-def owners_sum(keep, received, me):
-    total = keep + received
+def last_two(keep, received, me):
     mask = 2
     while mask < lax.axis_size("seq"):
         bit = me // mask % 2
+        total = keep + received
         pairs = total.reshape((-1, 2) + total.shape[1:])
         keep = lax.dynamic_index_in_dim(pairs, bit, 1, False)
         send = lax.dynamic_index_in_dim(pairs, 1 - bit, 1, False)
-        total = keep + swap(send, "seq", mask)
+        received = swap(send, "seq", mask)
         mask *= 2
-    return total.astype(jnp.bfloat16)
-
-
-def doubling_masks(size):
-    masks = []
-    while size > 2:
-        size //= 2
-        masks.append(size)
-    return masks
-
-
-def gather_doubling(block):
-    for mask in doubling_masks(lax.axis_size("seq")):
-        block = jnp.concatenate([block, swap(block, "seq", mask)])
-    return [block, swap(block, "seq", 1)]
-
-
-def doubling_offsets(size):
-    offsets = [0]
-    for mask in doubling_masks(size):
-        offsets = offsets + [offset ^ mask for offset in offsets]
-    return offsets + [offset ^ 1 for offset in offsets]
-
-
-def gather_at_once(copies):
-    return lax.all_to_all(copies, "seq", 0, 0)
-
-
-def project_kernel(me_ref, hidden_ref, *refs, extra, carried, chunk, blocks, pieces):
-    weight_refs, refs = refs[: 1 + extra], refs[1 + extra + carried :]
-    refs = refs[:2] + refs[2 + carried :]
-    keep_ref, send_ref, q_all, *others_all, sems = refs
+    return [keep, received]
+
+
+def collect_kernel(*refs):
+    part_refs, (mine_ref, copies_ref) = refs[:-2], refs[-2:]
+    total = None
+    for ref in part_refs:
+        for k in range(ref.shape[0]):
+            total = ref[k] if total is None else total + ref[k]
+    total = total.astype(jnp.bfloat16)
+    mine_ref[0] = total
+    for k in range(copies_ref.shape[0]):
+        copies_ref[k] = total
+
+
+def collect(parts, copies):
+    shape = parts[0].shape[1:]
+    return pl.pallas_call(
+        collect_kernel,
+        out_shape=[jax.ShapeDtypeStruct((n,) + shape, jnp.bfloat16) for n in (1, copies)],
+        in_specs=[vmem_spec()] * len(parts),
+        out_specs=[vmem_spec()] * 2,
+        compiler_params=pltpu.CompilerParams(vmem_limit_bytes=SMALL_GRANT),
+    )(*parts)
+
+
+def project_kernel(me_ref, hidden_ref, *refs, extra, halved, chunk, blocks, pieces):
+    weight_refs, refs = refs[: 1 + extra], refs[1 + extra :]
+    outs, (q_all, *others_all, sems) = refs[: 1 + halved], refs[1 + halved :]
     tokens, depth = hidden_ref.shape
     odd = lax.rem(me_ref[0], 2) == 1
     rows = depth // pieces
@@ -110,9 +107,13 @@
             for c in range(product.shape[1] // LANES)
             for e in range(tokens // block)
         ]
+        if not halved:
+            for i, part in enumerate(parts):
+                outs[0][i, first : first + block, :] = part
+            return
         for i, (even_part, odd_part) in enumerate(zip(parts[0::2], parts[1::2])):
-            keep_ref[i, first : first + block, :] = jnp.where(odd, odd_part, even_part)
-            send_ref[i, first : first + block, :] = jnp.where(odd, even_part, odd_part)
+            outs[0][i, first : first + block, :] = jnp.where(odd, odd_part, even_part)
+            outs[1][i, first : first + block, :] = jnp.where(odd, even_part, odd_part)
 
     total = None
     for i in range(pieces):
@@ -131,25 +132,25 @@
         deal(jnp.concatenate(both, axis=1), 1)
 
 
-def project(me, hidden, query_weight, others, carried, chunk, columns, count):
+def project(me, hidden, query_weight, others, halved, chunk, columns, count):
     tokens, depth = hidden.shape
     wide = columns + sum(other.shape[1] for other in others)
     pieces = max(1, depth // 256)
     blocks = [width // LANES * tokens // count for width in (columns, wide - columns)]
-    shape = jax.ShapeDtypeStruct((count // 2, sum(blocks), LANES), jnp.float32)
+    owners = count // 2 if halved else count
+    shape = jax.ShapeDtypeStruct((owners, sum(blocks), LANES), jnp.float32)
     return pl.pallas_call(
         functools.partial(
             project_kernel,
             extra=len(others),
-            carried=len(carried),
+            halved=halved,
             chunk=chunk,
             blocks=blocks,
             pieces=pieces,
         ),
-        out_shape=[shape] * 2 + [jax.ShapeDtypeStruct(one.shape, one.dtype) for one in carried],
-        in_specs=[smem_spec(), vmem_spec()] + [hbm_spec()] * (1 + len(others) + len(carried)),
-        out_specs=[vmem_spec()] * 2 + [hbm_spec()] * len(carried),
-        input_output_aliases={3 + len(others) + i: 2 + i for i in range(len(carried))},
+        out_shape=[shape] * (1 + halved),
+        in_specs=[smem_spec(), vmem_spec()] + [hbm_spec()] * (1 + len(others)),
+        out_specs=[vmem_spec()] * (1 + halved),
         scratch_shapes=[pltpu.VMEM((depth, columns), jnp.bfloat16)]
         + [pltpu.VMEM(other.shape, jnp.bfloat16) for other in others]
         + [pltpu.SemaphoreType.DMA((pieces + len(others),))],
@@ -159,33 +160,29 @@
             bytes_accessed=2 * depth * wide,
             transcendentals=0,
         ),
-    )(me, hidden, query_weight, *others, *carried)
-
-
-def attention_kernel(len_ref, me_ref, *refs, sources, band, step, block, head):
-    q_refs, refs = refs[:sources], refs[sources:]
-    k_hbm, v_hbm, o_ref, k_ref, v_ref, sems = refs[:6]
-    s_bufs, m_bufs = refs[6:8], refs[8:10]
-    shift, acc, lse_all = refs[10:]
-    half = q_refs[0].shape[0]
-    rows = sources * half * block
+    )(me, hidden, query_weight, *others)
+
+
+def attention_kernel(len_ref, q_ref, k_hbm, v_hbm, o_ref, *refs, band, step, block, head, dma):
+    k_ref, v_ref, sems = refs[:3]
+    s_bufs, m_bufs = refs[3:5], refs[5:7]
+    shift, acc, lse_all = refs[7:]
+    count = q_ref.shape[0]
+    rows = count * block
     bands = rows // band
     share = band // block
     scale = math.log2(math.e) / math.sqrt(HD)
     piece = math.gcd(step, 1024)
     tiles = piece // LANES
+    fold = math.gcd(band, 128)
     lanes = slice(head * HD, (head + 1) * HD)
-    offsets = doubling_offsets(sources * half)
-
-    def owner_of(k):
-        return k if sources == 1 else me_ref[0] ^ offsets[k]
 
     length = len_ref[0]
     full = length // step
     rest = length - full * step
 
     def copy_in(source, target, which, i):
-        where = pl.ds(pl.multiple_of(i * step, step), step)
+        where = pl.ds(pl.multiple_of(i * dma, dma), dma)
         return pltpu.make_async_copy(
             source.at[where, :], target.at[where, :], sems.at[which, i]
         )
@@ -196,7 +193,7 @@
     def values_in(i):
         return copy_in(v_hbm, v_ref, 1, i)
 
-    needed = (length + step - 1) // step
+    needed = (length + step - 1) // step * (step // dma)
 
     def start_keys(i, carry):
         keys_in(i).start()
@@ -210,9 +207,7 @@
     lax.fori_loop(0, needed, start_values, 0)
 
     def score(r, i, first, masked):
-        source = q_refs[r * share // half]
-        at = r * share % half
-        q = source[at : at + share, :block, :].reshape(band, HD)
+        q = q_ref[r * share : (r + 1) * share, :block, :].reshape(band, HD)
         keys = k_ref[pl.ds(pl.multiple_of(i * step + first, piece), piece), lanes]
         s = lax.dot_general(q, keys, NT, preferred_element_type=jnp.float32)
         if masked:
@@ -225,15 +220,17 @@
         m_bufs[r % 2][...] = jnp.maximum(m_bufs[r % 2][...], tops[0])
 
     def weigh(r, i, first):
-        s = s_bufs[r % 2][i, :, first : first + piece]
-        low = shift[...]
-        weights = jnp.concatenate(
-            [
-                jnp.exp2(s[:, c * LANES : (c + 1) * LANES] * scale - low).astype(jnp.bfloat16)
+        blocks = []
+        for top in range(0, band, fold):
+            here = slice(top, top + fold)
+            low = shift[here, :]
+            tiled = [
+                s_bufs[r % 2][i, here, first + c * LANES : first + (c + 1) * LANES]
                 for c in range(tiles)
-            ],
-            axis=1,
-        )
+            ]
+            tiled = [jnp.exp2(s * scale - low).astype(jnp.bfloat16) for s in tiled]
+            blocks.append(jnp.concatenate(tiled, axis=1))
+        weights = jnp.concatenate(blocks, axis=0)
         values = v_ref[pl.ds(pl.multiple_of(i * step + first, piece), piece), lanes]
         wide = jnp.concatenate([values, jnp.ones((piece, LANES), jnp.bfloat16)], axis=1)
         acc[...] += jnp.dot(weights, wide, preferred_element_type=jnp.float32)
@@ -248,11 +245,12 @@
             acc[...] = jnp.zeros(acc.shape, jnp.float32)
 
         def both(i, masked):
-            if r == 0:
-                keys_in(i).wait()
-            if r == 1:
-                values_in(i).wait()
             for first in range(0, step, piece):
+                arrived = i * (step // dma) + first // dma
+                if r == 0 and first % dma == 0:
+                    keys_in(arrived).wait()
+                if r == 1 and first % dma == 0:
+                    values_in(arrived).wait()
                 if weighs:
                     weigh(r - 1, i, first)
                 if scores:
@@ -272,49 +270,49 @@
             totals = acc[:, LANES:]
             mean = acc[:, :LANES] / totals * OUTPUT_SCALE
             levels = shift[...] + jnp.log2(totals)
-            for e in range(share):
-                k = (r - 1) * share + e
-                owner = owner_of(k)
-                here = slice(e * block, (e + 1) * block)
-                o_ref[owner, :block, :] = mean[here, :]
-                lse_all[pl.ds(pl.multiple_of(owner * block, block), block), :] = levels[here, :]
+            o_ref[(r - 1) * share : r * share, :block, :] = mean.reshape(share, block, HD)
+            lse_all[(r - 1) * band : r * band, :] = levels
 
     per = LANES // block
-    row = lax.broadcasted_iota(jnp.int32, (STAT_ROWS, LANES), 0)
     for g in range(rows // LANES):
-        level = lse_all[g * LANES : (g + 1) * LANES, :].T[:STAT_ROWS, :]
-        exponent = jnp.floor(jnp.log2(jnp.maximum(jnp.abs(level), 1e-30)))
-        exponent = jnp.minimum(exponent, 120.0)
-        rest_of = level * jnp.exp2(-exponent)
-        first = jnp.floor(rest_of * 2.0**9 + 0.5)
-        rest_of = rest_of - first * 2.0**-9
-        second = jnp.floor(rest_of * 2.0**20 + 0.5)
-        third = (rest_of - second * 2.0**-20) * 2.0**31
-        stats = jnp.where(row == 0, exponent, jnp.where(row == 1, first, second))
-        stats = jnp.where(row >= 3, third, stats)
+        stats = encode_levels(lse_all[g * LANES : (g + 1) * LANES, :].T[:STAT_ROWS, :])
         for e in range(per):
             o_ref[g * per + e, block:, :] = stats
 
 
-def attention(queries, block, keys, values, length, me, head):
-    sources = len(queries)
-    count = sources * queries[0].shape[0]
+def encode_levels(level):
+    row = lax.broadcasted_iota(jnp.int32, level.shape, 0)
+    exponent = jnp.floor(jnp.log2(jnp.maximum(jnp.abs(level), 1e-30)))
+    exponent = jnp.minimum(exponent, 120.0)
+    rest = level * jnp.exp2(-exponent)
+    first = jnp.floor(rest * 2.0**9 + 0.5)
+    rest = rest - first * 2.0**-9
+    second = jnp.floor(rest * 2.0**20 + 0.5)
+    third = (rest - second * 2.0**-20) * 2.0**31
+    stats = jnp.where(row == 0, exponent, jnp.where(row == 1, first, second))
+    return jnp.where(row >= 3, third, stats)
+
+
+def attention(queries, block, keys, values, length, head):
+    count = queries.shape[0]
     rows, slots = count * block, keys.shape[0]
     band = math.gcd(rows // 2, 512)
-    step = math.gcd(slots, 2048)
+    step = math.gcd(slots, 4096)
+    dma = math.gcd(step, 2048)
+    steps = slots // step
     return pl.pallas_call(
         functools.partial(
-            attention_kernel, sources=sources, band=band, step=step, block=block, head=head
+            attention_kernel, band=band, step=step, block=block, head=head, dma=dma
         ),
         out_shape=jax.ShapeDtypeStruct((count, block + STAT_ROWS, HD), jnp.float32),
-        in_specs=[smem_spec()] * 2 + [vmem_spec()] * sources + [hbm_spec()] * 2,
+        in_specs=[smem_spec(), vmem_spec()] + [hbm_spec()] * 2,
         out_specs=vmem_spec(),
         scratch_shapes=[
             pltpu.VMEM(keys.shape, keys.dtype),
             pltpu.VMEM(values.shape, values.dtype),
-            pltpu.SemaphoreType.DMA((2, slots // step)),
-            pltpu.VMEM((slots // step, band, step), jnp.float32),
-            pltpu.VMEM((slots // step, band, step), jnp.float32),
+            pltpu.SemaphoreType.DMA((2, slots // dma)),
+            pltpu.VMEM((steps, band, step), jnp.float32),
+            pltpu.VMEM((steps, band, step), jnp.float32),
             pltpu.VMEM((band, LANES), jnp.float32),
             pltpu.VMEM((band, LANES), jnp.float32),
             pltpu.VMEM((band, LANES), jnp.float32),
@@ -327,7 +325,7 @@
             bytes_accessed=4 * slots * HD,
             transcendentals=rows * slots,
         ),
-    )(length, me, *queries, keys, values)
+    )(length, queries, keys, values)
 
 
 def fresh_kernel(me_ref, *refs, heads, block, tokens):
@@ -364,6 +362,7 @@
         in_specs=[smem_spec()] + [vmem_spec()] * (heads + 1),
         out_specs=[vmem_spec()] * (2 * heads),
         scratch_shapes=[pltpu.VMEM((kv_rows, HD), jnp.float32)],
+        compiler_params=pltpu.CompilerParams(vmem_limit_bytes=SMALL_GRANT),
     )(me, *mine, last)
 
 
@@ -403,6 +402,7 @@
         in_specs=[smem_spec()] + [vmem_spec()] * (3 + len(before)),
         out_specs=vmem_spec(),
         scratch_shapes=[pltpu.VMEM((LANES, parts.shape[0]), jnp.float32)],
+        compiler_params=pltpu.CompilerParams(vmem_limit_bytes=SMALL_GRANT),
     )(me, parts, new_out, new_stat, *before)
 
 
@@ -432,6 +432,23 @@
             ref[i] = total[pl.ds(start, share), :]
 
 
+def bring_kernel(w_hbm, after_ref, w_ref, sem):
+    copy = pltpu.make_async_copy(w_hbm, w_ref, sem)
+    copy.start()
+    copy.wait()
+
+
+def bring(weight, after):
+    return pl.pallas_call(
+        bring_kernel,
+        out_shape=jax.ShapeDtypeStruct(weight.shape, weight.dtype),
+        in_specs=[hbm_spec()] * 2,
+        out_specs=vmem_spec(),
+        scratch_shapes=[pltpu.SemaphoreType.DMA],
+        compiler_params=pltpu.CompilerParams(vmem_limit_bytes=SMALL_GRANT),
+    )(weight, after)
+
+
 def output_halves(place, weight, attended, block, tokens, heads):
     depth, width = weight.shape
     shape = jax.ShapeDtypeStruct((heads // 2, tokens // heads, width), jnp.float32)
@@ -441,7 +458,7 @@
         in_specs=[smem_spec()] + [vmem_spec()] * 2,
         out_specs=[vmem_spec()] * 2,
         scratch_shapes=[pltpu.VMEM((tokens, width), jnp.float32)],
-        compiler_params=pltpu.CompilerParams(vmem_limit_bytes=OUTPUT_GRANT),
+        compiler_params=pltpu.CompilerParams(vmem_limit_bytes=SMALL_GRANT),
         cost_estimate=pl.CostEstimate(
             flops=2 * tokens * depth * width,
             bytes_accessed=2 * depth * width,
@@ -469,27 +486,28 @@
     me = lax.axis_index("seq").reshape(1)
     place = lax.axis_index("head").reshape(1)
 
-    kept, received = [], []
+    partials = []
     for j in range(kv_local):
-        others = [key_weight, value_weight] if j == kv_local - 1 else []
-        keep, send, *kept = project(
-            me, hidden, query_weight, others, kept, j, columns, count
+        last = j == kv_local - 1
+        others = [key_weight, value_weight] if last else []
+        partials.append(
+            project(me, hidden, query_weight, others, int(last), j, columns, count)
         )
-        kept.append(keep)
-        received.append(swap(send, "seq", 1))
     mine, queries = [], []
     for j in range(kv_local):
-        mine.append(owners_sum(kept[j], received[j], me[0]))
         if j == kv_local - 1:
-            copies = jnp.broadcast_to(mine[j], (count,) + mine[j].shape[1:])
-            queries.append([gather_at_once(copies)])
+            keep, send = partials[j]
+            parts = last_two(keep, swap(send, "seq", 1), me[0])
         else:
-            queries.append(gather_doubling(mine[j]))
-
-    fresh_parts = fresh(me, mine, queries[-1][0], block, tokens)
+            parts = [lax.all_to_all(partials[j][0], "seq", 0, 0)]
+        rows, copies = collect(parts, count)
+        mine.append(rows)
+        queries.append(lax.all_to_all(copies, "seq", 0, 0))
+
+    fresh_parts = fresh(me, mine, queries[-1], block, tokens)
     before = []
     for j in range(kv_local):
-        parts = attention(queries[j], block, cache_keys, cache_values, cache_lens, me, j)
+        parts = attention(queries[j], block, cache_keys, cache_values, cache_lens, j)
         parts = lax.all_to_all(parts.astype(jnp.float16), "seq", 0, 0).astype(jnp.float32)
         new_out, new_stat = fresh_parts[2 * j : 2 * j + 2]
         last = j == kv_local - 1
@@ -497,8 +515,9 @@
             me, parts, new_out, new_stat, before if last else [], count if last else 1
         )
         before.append(attended)
-    attended = gather_at_once(before[-1])
-    mixed = output_halves(place, output_weight, attended, block, tokens, heads)
+    attended = lax.all_to_all(before[-1], "seq", 0, 0)
+    weight = bring(output_weight, before[-1])
+    mixed = output_halves(place, weight, attended, block, tokens, heads)
 
     keep, send = mixed
     mixed = keep + swap(send, "head", 1)

time: 121 us -> 127 us (1.050)
  Pallas kernels: 41.2 us -> 27.5 us
  waiting for transfers between devices: 30.9 us -> 43.2 us
  starting transfers between devices: 37.2 us -> 44.5 us
  local copies, waits for them, and re-layouts: 3.09 us -> 6.35 us
  other arithmetic: 6.03 us -> 3.32 us
    ppermute x11 -> x5, starting transfers between devices: 20.2 us -> 8.3 us  [swap(): return lax.ppermute(array, axis, [(i, i ^ mask) for i in range(size)])]
    all_to_all x2 -> x4, starting transfers between devices: 6.94 us -> 17.8 us  [the longest x1 7.27 us: shards(): parts = [lax.all_to_all(partials[j][0], 'seq', 0, 0)]]
    pallas_call x4 -> x7, Pallas kernels: 33.1 us -> 23.9 us  [the longest x2 14.3 us: attention(): pl.pallas_call(functools.partial(attention_kernel, band=band, step=step,...]
    all_to_all x2, starting transfers between devices: 10.1 us -> 18.5 us  [shards(): lax.all_to_all(parts.astype(jnp.float16), 'seq', 0, 0).astype(jnp.float32)]
    ppermute x11 -> x5, waiting for transfers between devices: 18 us -> 25 us  [swap(): return lax.ppermute(array, axis, [(i, i ^ mask) for i in range(size)])]
    all_to_all x2, waiting for transfers between devices: 2.75 us -> 7.44 us  [shards(): lax.all_to_all(parts.astype(jnp.float16), 'seq', 0, 0).astype(jnp.float32)]
    unnamed x8 -> x6, local copies, waits for them, and re-layouts: 2.2 us -> 6.31 us
    pallas_call x2, Pallas kernels: 5.06 us -> 2.27 us  [merge(): pl.pallas_call(merge_kernel, out_shape=jax.ShapeDtypeStruct(shape, jnp.bf...]
  transfers between devices with their start and end apart: 15 -> 11, of which waited for: 10 -> 9; matrix products, arithmetic and copies ran while one was open for 4% -> 2% of each run, Pallas kernels for 29% -> 17%
where the time goes in v8:
time: 127 us; the launch traced here: 126 us
  starting transfers between devices  44.5 us (35%)
  waiting for transfers between devices  43.2 us (34%)
  Pallas kernels  27.5 us (22%)
  local copies, waits for them, and re-layouts  6.35 us (5%)
  other arithmetic  3.32 us (3%)
    ppermute x5, waiting for transfers between devices, swap(): return lax.ppermute(array, axis, [(i, i ^ mask) for i in range(size)])  25 us
    all_to_all x2, starting transfers between devices, shards(): lax.all_to_all(parts.astype(jnp.float16), 'seq', 0, 0).astype(jnp.float32)  18.5 us
    pallas_call x2, Pallas kernels, attention(): pl.pallas_call(functools.partial(attention_kernel, band=band, step=step,...  14.3 us
    ppermute x5, starting transfers between devices, swap(): return lax.ppermute(array, axis, [(i, i ^ mask) for i in range(size)])  8.3 us
    pallas_call x2, Pallas kernels, project(): pl.pallas_call(functools.partial(project_kernel, extra=len(others), halve...  7.78 us
    all_to_all x2, waiting for transfers between devices, shards(): lax.all_to_all(parts.astype(jnp.float16), 'seq', 0, 0).astype(jnp.float32)  7.44 us
    all_to_all x1, waiting for transfers between devices, shards(): attended = lax.all_to_all(before[-1], 'seq', 0, 0)  7.36 us
    all_to_all x1, starting transfers between devices, shards(): parts = [lax.all_to_all(partials[j][0], 'seq', 0, 0)]  7.27 us
  transfers between devices with their start and end apart: 11, of which 9 were waited for; matrix products, arithmetic and copies ran while one was open for 2% of the time, Pallas kernels for 17%

profile of v8, /device:TPU:0, one launch (start us, length us, event | category | flops | bytes accessed | tf_op | source)
XLA Modules:
  0.0 125.9 jit_solution(16917983737801593154)
XLA Ops:
  0.0 3.5 %shard_map.85 = f32[8,128,128]{2,1,0:T(8,128)} custom-call(s32[1]{0:T(128)} %bitcast.1.me_ref, bf16[128,1024]{1,0:T(8,128)(2,1)} %hidden_ref.3, bf16[1024,2048]{1,0:T(8,128)(2,1)} %refs_0_.3), custom_call_target="tpu_custom_call" | custom-call | flops 268435456 | bytes 2097152 | tf_op jit(solution)/shard_map/pallas_call | solution.py:142
  3.5 7.3 %all-to-all-start.2 = ((f32[8,128,128]{2,1,0:T(8,128)}), f32[8,128,128]{2,1,0:T(8,128)S(1)}, u32[]{:S(2)}, u32[]{:S(2)}) async-start(f32[8,128,128]{2,1,0:T(8,128)} %shard_map.85), calls=%async_computation.2 | async-start | bytes 1048576 | tf_op jit(solution)/shard_map/all_to_all | solution.py:502
  10.8 4.2 %shard_map.82 = (f32[4,192,128]{2,1,0:T(8,128)}, f32[4,192,128]{2,1,0:T(8,128)}) custom-call(s32[1]{0:T(128)} %bitcast.1.me_ref, bf16[128,1024]{1,0:T(8,128)(2,1)} %hidden_ref.3, bf16[1024,2048]{1,0:T(8,128)(2,1)} %refs_0_.3, bf16[1024,256]{1,0:T(8,128)(2,1)} %refs_1_.1, bf16[1024,256]{1,0:T(8,128)(2,1)} %refs_2_.1), custom_call_target="tpu_custom_call" | custom-call | flops 402653184 | bytes 3145728 | tf_op jit(solution)/shard_map/pallas_call | solution.py:142
  15.1 2.1 %collective-permute-start = (f32[4,192,128]{2,1,0:T(8,128)}, f32[4,192,128]{2,1,0:T(8,128)S(1)}, u32[]{:S(2)}, u32[]{:S(2)}) collective-permute-start(f32[4,192,128]{2,1,0:T(8,128)} %get-tuple-element.18), channel_id=1, source_target_pairs={{0,4},{4,0},{8,12},{12,8},{16,20},{20,16},{24,28},{28,24},{1,5},{5... | collective-permute-start | bytes 1179656 | tf_op jit(solution)/shard_map/ppermute | solution.py:41
  17.2 11.1 %collective-permute-done = f32[4,192,128]{2,1,0:T(8,128)S(1)} collective-permute-done((f32[4,192,128]{2,1,0:T(8,128)}, f32[4,192,128]{2,1,0:T(8,128)S(1)}, u32[]{:S(2)}, u32[]{:S(2)}) %collective-permute-start) | collective-permute-done | bytes 393248 | tf_op jit(solution)/shard_map/ppermute | solution.py:41
  28.2 1.0 add.49
  29.3 2.2 %collective-permute-start.1 = (f32[2,192,128]{2,1,0:T(8,128)S(1)}, f32[2,192,128]{2,1,0:T(8,128)S(1)}, u32[]{:S(2)}, u32[]{:S(2)}) collective-permute-start(f32[2,192,128]{2,1,0:T(8,128)S(1)} %dynamic-slice_bitcast_fusion), channel_id=1, source_target_pairs={{0,8},{4,12},{8,0},{12,4},{16,24},{20,28},{24,16},{28,20},{1,9},{5... | collective-permute-start | bytes 589832 | tf_op jit(solution)/shard_map/ppermute | solution.py:41
  31.5 0.0 all-to-all-done.2.refs_0_
  31.5 0.7 shard_map.86
  32.2 3.4 %all-to-all-start.3 = ((bf16[8,128,128]{2,1,0:T(8,128)(2,1)}), bf16[8,128,128]{2,1,0:T(8,128)(2,1)S(1)}, u32[]{:S(2)}, u32[]{:S(2)}) async-start(bf16[8,128,128]{2,1,0:T(8,128)(2,1)} %get-tuple-element.24), calls=%async_computation.3 | async-start | bytes 524288 | tf_op jit(solution)/shard_map/all_to_all | solution.py:505
  35.7 0.5 collective-permute-done.1
  36.2 2.4 %collective-permute-start.2 = (f32[1,192,128]{2,1,0:T(8,128)S(1)}, f32[1,192,128]{2,1,0:T(8,128)S(1)}, u32[]{:S(2)}, u32[]{:S(2)}) collective-permute-start(f32[1,192,128]{2,1,0:T(8,128)S(1)} %get-tuple-element.29), channel_id=1, source_target_pairs={{0,16},{4,20},{8,24},{12,28},{16,0},{20,4},{24,8},{28,12},{1,17},{... | collective-permute-start | bytes 294920 | tf_op jit(solution)/shard_map/ppermute | solution.py:41
  39.2 9.2 %collective-permute-done.2.refs_1_ = f32[1,192,128]{2,1,0:T(8,128)S(1)} collective-permute-done((f32[1,192,128]{2,1,0:T(8,128)S(1)}, f32[1,192,128]{2,1,0:T(8,128)S(1)}, u32[]{:S(2)}, u32[]{:S(2)}) %collective-permute-start.2) | collective-permute-done | bytes 98336 | tf_op jit(solution)/shard_map/ppermute | solution.py:41
  48.4 0.8 shard_map.83
  49.2 0.0 all-to-all-done.3.q_ref
  49.2 3.6 %all-to-all-start = ((bf16[8,192,128]{2,1,0:T(8,128)(2,1)}), bf16[8,192,128]{2,1,0:T(8,128)(2,1)S(1)}, u32[]{:S(2)}, u32[]{:S(2)}) async-start(bf16[8,192,128]{2,1,0:T(8,128)(2,1)} %get-tuple-element.19), calls=%async_computation | async-start | bytes 786432 | tf_op jit(solution)/shard_map/all_to_all | solution.py:505
  52.8 7.1 %shard_map.88 = f32[8,136,128]{2,1,0:T(8,128)S(1)} custom-call(s32[1]{0:T(128)S(6)} %copy.13.len_ref, bf16[8,128,128]{2,1,0:T(8,128)(2,1)S(1)} %all-to-all-done.3.q_ref, bf16[8192,256]{1,0:T(8,128)(2,1)} %k_hbm.3, bf16[8192,256]{1,0:T(8,128)(2,1)} %v_hbm.3), custom_call_target="tpu_custom_call" | custom-call | flops 8589934592 | bytes 4194304 | tf_op jit(solution)/shard_map/pallas_call | solution.py:303
  60.0 0.7 convert_element_type.28
  60.7 3.5 %all-to-all-done.q_ref.refs_2_ = bf16[8,192,128]{2,1,0:T(8,128)(2,1)S(1)} async-done(((bf16[8,192,128]{2,1,0:T(8,128)(2,1)}), bf16[8,192,128]{2,1,0:T(8,128)(2,1)S(1)}, u32[]{:S(2)}, u32[]{:S(2)}) %all-to-all-start) | async-done | bytes 393248 | tf_op jit(solution)/shard_map/all_to_all | solution.py:505
  64.2 7.8 %all-to-all-start.4 = ((f16[8,136,128]{2,1,0:T(8,128)(2,1)}), f16[8,136,128]{2,1,0:T(8,128)(2,1)S(1)}, u32[]{:S(2)}, u32[]{:S(2)}) async-start(f16[8,136,128]{2,1,0:T(8,128)(2,1)} %convert_element_type.28), calls=%async_computation.4 | async-start | bytes 557056 | tf_op jit(solution)/shard_map/all_to_all | solution.py:511
  71.9 7.2 %shard_map.84 = f32[8,136,128]{2,1,0:T(8,128)S(1)} custom-call(s32[1]{0:T(128)S(6)} %copy.13.len_ref, bf16[8,192,128]{2,1,0:T(8,128)(2,1)S(1)} %all-to-all-done.q_ref.refs_2_, bf16[8192,256]{1,0:T(8,128)(2,1)} %k_hbm.3, bf16[8192,256]{1,0:T(8,128)(2,1)} %v_hbm.3), custom_call_target="tpu_custom_call" | custom-call | flops 8589934592 | bytes 4194304 | tf_op jit(solution)/shard_map/pallas_call | solution.py:303
  79.1 0.7 convert_element_type.26
  79.9 0.5 all-to-all-done.4
  80.4 10.7 %all-to-all-start.1 = ((f16[8,136,128]{2,1,0:T(8,128)(2,1)}), f16[8,136,128]{2,1,0:T(8,128)(2,1)S(1)}, u32[]{:S(2)}, u32[]{:S(2)}) async-start(f16[8,136,128]{2,1,0:T(8,128)(2,1)} %convert_element_type.26), calls=%async_computation.1 | async-start | bytes 557056 | tf_op jit(solution)/shard_map/all_to_all | solution.py:511
  91.1 0.6 shard_map.87
  91.7 0.7 shard_map.89.refs_0_
  92.5 6.9 %all-to-all-done.1 = f16[8,136,128]{2,1,0:T(8,128)(2,1)S(1)} async-done(((f16[8,136,128]{2,1,0:T(8,128)(2,1)}), f16[8,136,128]{2,1,0:T(8,128)(2,1)S(1)}, u32[]{:S(2)}, u32[]{:S(2)}) %all-to-all-start.1) | async-done | bytes 278560 | tf_op jit(solution)/shard_map/all_to_all | solution.py:511
  99.5 1.5 %shard_map.90.after_ref = bf16[8,256,128]{2,1,0:T(8,128)(2,1)} custom-call(s32[1]{0:T(128)} %bitcast.1.me_ref, f32[8,136,128]{2,1,0:T(8,128)S(1)} %convert_element_type.27.part_ref, f32[128,128]{1,0:T(8,128)S(1)} %get-tuple-element.22.out_ref, f32[128,128]{1,0:T(8,128)S(1)} %get-tuple-element.23.stat_ref, bf16[1,128,128]{2,1,0:T(8,128)(2,1)S(1)} %shard_map.89.refs_0_), custom_call_target="tpu_custom_call" | custom-call | tf_op jit(solution)/shard_map/pallas_call | solution.py:399
  101.0 3.5 %all-to-all-start.5 = ((bf16[8,256,128]{2,1,0:T(8,128)(2,1)}), bf16[8,256,128]{2,1,0:T(8,128)(2,1)S(1)}, u32[]{:S(2)}, u32[]{:S(2)}) async-start(bf16[8,256,128]{2,1,0:T(8,128)(2,1)} %shard_map.90.after_ref), calls=%async_computation.5 | async-start | bytes 1048576 | tf_op jit(solution)/shard_map/all_to_all | solution.py:518
  104.5 0.0 copy-start.2
  104.5 2.2 %copy-done.2 = bf16[2048,1024]{1,0:T(8,128)(2,1)S(1)} copy-done((bf16[2048,1024]{1,0:T(8,128)(2,1)S(1)}, bf16[2048,1024]{1,0:T(8,128)(2,1)}, u32[]{:S(2)}) %copy-start.2) | copy-done | bytes 4194328
  106.7 0.3 shard_map.91.w_ref
  107.0 0.0 copy-start
  107.0 1.9 %copy-done = bf16[2048,1024]{1,0:T(8,128)(2,1)} copy-done((bf16[2048,1024]{1,0:T(8,128)(2,1)}, bf16[2048,1024]{1,0:T(8,128)(2,1)S(1)}, u32[]{:S(2)}) %copy-start) | copy-done | bytes 4194328
  108.9 7.4 %all-to-all-done.5.a_ref = bf16[8,256,128]{2,1,0:T(8,128)(2,1)S(1)} async-done(((bf16[8,256,128]{2,1,0:T(8,128)(2,1)}), bf16[8,256,128]{2,1,0:T(8,128)(2,1)S(1)}, u32[]{:S(2)}, u32[]{:S(2)}) %all-to-all-start.5) | async-done | bytes 524320 | tf_op jit(solution)/shard_map/all_to_all | solution.py:518
  116.3 0.0 copy-start.1
  116.3 2.2 %copy-done.1 = bf16[2048,1024]{1,0:T(8,128)(2,1)S(1)} copy-done((bf16[2048,1024]{1,0:T(8,128)(2,1)S(1)}, bf16[2048,1024]{1,0:T(8,128)(2,1)}, u32[]{:S(2)}) %copy-start.1) | copy-done | bytes 4194328
  118.5 0.8 shard_map.92
  119.2 0.1 collective-permute-start.3
  119.4 1.5 %collective-permute-done.3 = f32[2,32,1024]{2,1,0:T(8,128)S(1)} collective-permute-done((f32[2,32,1024]{2,1,0:T(8,128)S(1)}, f32[2,32,1024]{2,1,0:T(8,128)S(1)}, u32[]{:S(2)}, u32[]{:S(2)}) %collective-permute-start.3) | collective-permute-done | bytes 262176 | tf_op jit(solution)/shard_map/ppermute | solution.py:41
  120.9 1.6 %collective-permute-start.4 = (f16[1,32,1024]{2,1,0:T(8,128)(2,1)S(1)}, f16[1,32,1024]{2,1,0:T(8,128)(2,1)S(1)}, u32[]{:S(2)}, u32[]{:S(2)}) collective-permute-start(f16[1,32,1024]{2,1,0:T(8,128)(2,1)S(1)} %multiply_convert_fusion), channel_id=1, source_target_pairs={{0,2},{1,3},{2,0},{3,1},{4,6},{5,7},{6,4},{7,5},{8,10},{9,11},{10,... | collective-permute-start | bytes 196616 | tf_op jit(solution)/shard_map/ppermute | solution.py:41
  122.5 2.7 %collective-permute-done.4 = f16[1,32,1024]{2,1,0:T(8,128)(2,1)S(1)} collective-permute-done((f16[1,32,1024]{2,1,0:T(8,128)(2,1)S(1)}, f16[1,32,1024]{2,1,0:T(8,128)(2,1)S(1)}, u32[]{:S(2)}, u32[]{:S(2)}) %collective-permute-start.4) | collective-permute-done | bytes 65568 | tf_op jit(solution)/shard_map/ppermute | solution.py:41
  125.2 0.6 fusion
  (7 shorter events, 0.2 us)
Async XLA Ops:
  3.5 27.9 %all-to-all-start.2 = ((f32[8,128,128]{2,1,0:T(8,128)}), f32[8,128,128]{2,1,0:T(8,128)S(1)}, u32[]{:S(2)}, u32[]{:S(2)}) async-start(f32[8,128,128]{2,1,0:T(8,128)} %shard_map.85), calls=%async_computation.2 | async-start | bytes 1048576 | tf_op jit(solution)/shard_map/all_to_all | solution.py:502
  15.1 13.2 %collective-permute-start = (f32[4,192,128]{2,1,0:T(8,128)}, f32[4,192,128]{2,1,0:T(8,128)S(1)}, u32[]{:S(2)}, u32[]{:S(2)}) collective-permute-start(f32[4,192,128]{2,1,0:T(8,128)} %get-tuple-element.18), channel_id=1, source_target_pairs={{0,4},{4,0},{8,12},{12,8},{16,20},{20,16},{24,28},{28,24},{1,5},{5... | collective-permute-start | bytes 1179656 | tf_op jit(solution)/shard_map/ppermute | solution.py:41
  29.3 6.9 %collective-permute-start.1 = (f32[2,192,128]{2,1,0:T(8,128)S(1)}, f32[2,192,128]{2,1,0:T(8,128)S(1)}, u32[]{:S(2)}, u32[]{:S(2)}) collective-permute-start(f32[2,192,128]{2,1,0:T(8,128)S(1)} %dynamic-slice_bitcast_fusion), channel_id=1, source_target_pairs={{0,8},{4,12},{8,0},{12,4},{16,24},{20,28},{24,16},{28,20},{1,9},{5... | collective-permute-start | bytes 589832 | tf_op jit(solution)/shard_map/ppermute | solution.py:41
  32.2 17.0 %all-to-all-start.3 = ((bf16[8,128,128]{2,1,0:T(8,128)(2,1)}), bf16[8,128,128]{2,1,0:T(8,128)(2,1)S(1)}, u32[]{:S(2)}, u32[]{:S(2)}) async-start(bf16[8,128,128]{2,1,0:T(8,128)(2,1)} %get-tuple-element.24), calls=%async_computation.3 | async-start | bytes 524288 | tf_op jit(solution)/shard_map/all_to_all | solution.py:505
  36.2 12.2 %collective-permute-start.2 = (f32[1,192,128]{2,1,0:T(8,128)S(1)}, f32[1,192,128]{2,1,0:T(8,128)S(1)}, u32[]{:S(2)}, u32[]{:S(2)}) collective-permute-start(f32[1,192,128]{2,1,0:T(8,128)S(1)} %get-tuple-element.29), channel_id=1, source_target_pairs={{0,16},{4,20},{8,24},{12,28},{16,0},{20,4},{24,8},{28,12},{1,17},{... | collective-permute-start | bytes 294920 | tf_op jit(solution)/shard_map/ppermute | solution.py:41
  49.2 15.0 %all-to-all-start = ((bf16[8,192,128]{2,1,0:T(8,128)(2,1)}), bf16[8,192,128]{2,1,0:T(8,128)(2,1)S(1)}, u32[]{:S(2)}, u32[]{:S(2)}) async-start(bf16[8,192,128]{2,1,0:T(8,128)(2,1)} %get-tuple-element.19), calls=%async_computation | async-start | bytes 786432 | tf_op jit(solution)/shard_map/all_to_all | solution.py:505
  64.2 16.2 %all-to-all-start.4 = ((f16[8,136,128]{2,1,0:T(8,128)(2,1)}), f16[8,136,128]{2,1,0:T(8,128)(2,1)S(1)}, u32[]{:S(2)}, u32[]{:S(2)}) async-start(f16[8,136,128]{2,1,0:T(8,128)(2,1)} %convert_element_type.28), calls=%async_computation.4 | async-start | bytes 557056 | tf_op jit(solution)/shard_map/all_to_all | solution.py:511
  80.4 19.0 %all-to-all-start.1 = ((f16[8,136,128]{2,1,0:T(8,128)(2,1)}), f16[8,136,128]{2,1,0:T(8,128)(2,1)S(1)}, u32[]{:S(2)}, u32[]{:S(2)}) async-start(f16[8,136,128]{2,1,0:T(8,128)(2,1)} %convert_element_type.26), calls=%async_computation.1 | async-start | bytes 557056 | tf_op jit(solution)/shard_map/all_to_all | solution.py:511
  101.0 15.3 %all-to-all-start.5 = ((bf16[8,256,128]{2,1,0:T(8,128)(2,1)}), bf16[8,256,128]{2,1,0:T(8,128)(2,1)S(1)}, u32[]{:S(2)}, u32[]{:S(2)}) async-start(bf16[8,256,128]{2,1,0:T(8,128)(2,1)} %shard_map.90.after_ref), calls=%async_computation.5 | async-start | bytes 1048576 | tf_op jit(solution)/shard_map/all_to_all | solution.py:518
  104.5 2.2 %copy-start.2 = (bf16[2048,1024]{1,0:T(8,128)(2,1)S(1)}, bf16[2048,1024]{1,0:T(8,128)(2,1)}, u32[]{:S(2)}) copy-start(bf16[2048,1024]{1,0:T(8,128)(2,1)} %w_hbm.1) | copy-start | bytes 12582916
  107.0 1.9 %copy-start = (bf16[2048,1024]{1,0:T(8,128)(2,1)}, bf16[2048,1024]{1,0:T(8,128)(2,1)S(1)}, u32[]{:S(2)}) copy-start(bf16[2048,1024]{1,0:T(8,128)(2,1)S(1)} %shard_map.91.w_ref) | copy-start | bytes 12582916
  116.3 2.2 %copy-start.1 = (bf16[2048,1024]{1,0:T(8,128)(2,1)S(1)}, bf16[2048,1024]{1,0:T(8,128)(2,1)}, u32[]{:S(2)}) copy-start(bf16[2048,1024]{1,0:T(8,128)(2,1)} %copy-done) | copy-start | bytes 12582916
  119.2 1.6 %collective-permute-start.3 = (f32[2,32,1024]{2,1,0:T(8,128)S(1)}, f32[2,32,1024]{2,1,0:T(8,128)S(1)}, u32[]{:S(2)}, u32[]{:S(2)}) collective-permute-start(f32[2,32,1024]{2,1,0:T(8,128)S(1)} %get-tuple-element.28), channel_id=1, source_target_pairs={{0,1},{1,0},{2,3},{3,2},{4,5},{5,4},{6,7},{7,6},{8,9},{9,8},{10,11... | collective-permute-start | bytes 786440 | tf_op jit(solution)/shard_map/ppermute | solution.py:41
  120.9 4.3 %collective-permute-start.4 = (f16[1,32,1024]{2,1,0:T(8,128)(2,1)S(1)}, f16[1,32,1024]{2,1,0:T(8,128)(2,1)S(1)}, u32[]{:S(2)}, u32[]{:S(2)}) collective-permute-start(f16[1,32,1024]{2,1,0:T(8,128)(2,1)S(1)} %multiply_convert_fusion), channel_id=1, source_target_pairs={{0,2},{1,3},{2,0},{3,1},{4,6},{5,7},{6,4},{7,5},{8,10},{9,11},{10,... | collective-permute-start | bytes 196616 | tf_op jit(solution)/shard_map/ppermute | solution.py:41
